TPU v7x, 32 devices: a whole 2x2x4 slice. The times are simulated.
32 devices in a mesh: dp: 16 (over z, y, x), ctx: 2 (over core).
Axes of the slice: x: 2, y: 2, z: 4, core: 2. Of those that a mesh axis runs over, the one named last changes fastest.
Arguments:
- hidden_in: bfloat16 [16, 256, 1024], P('dp', 'ctx'), may hold values from -6 to 6
- cotangent: bfloat16 [16, 256, 1024], P('dp', 'ctx'), may hold values from -6 to 6
- block_order: int32 [16, 4], P('dp'), may hold values from 0 to 3, each once within a row
- w_query: float32 [1024, 2048], P('dp'), may hold values from -0.1875 to 0.1875
- key_weight: float32 [1024, 1024], P('dp'), may hold values from -0.1875 to 0.1875
- value_weight: float32 [1024, 1024], P('dp'), may hold values from -0.1875 to 0.1875
- w_output: float32 [2048, 1024], P('dp'), may hold values from -1 to 1
- w_gate: float32 [1024, 3072], P('dp'), may hold values from -0.1875 to 0.1875
- w_up: float32 [1024, 3072], P('dp'), may hold values from -0.1875 to 0.1875
- w_down: float32 [3072, 1024], P('dp'), may hold values from -0.109375 to 0.109375
- norm_gains: float32 [2304], P('dp'), may hold values from 0.5 to 1.5
- momentum_query: float32 [1024, 2048], P('dp'), may hold values from -0.625 to 0.625
- key_momentum: float32 [1024, 1024], P('dp'), may hold values from -0.625 to 0.625
- value_momentum: float32 [1024, 1024], P('dp'), may hold values from -0.625 to 0.625
- momentum_output: float32 [2048, 1024], P('dp'), may hold values from -0.625 to 0.625
- momentum_gate: float32 [1024, 3072], P('dp'), may hold values from -0.625 to 0.625
- momentum_up: float32 [1024, 3072], P('dp'), may hold values from -0.625 to 0.625
- momentum_down: float32 [3072, 1024], P('dp'), may hold values from -0.625 to 0.625
- momentum_gains: float32 [2304], P('dp'), may hold values from -0.625 to 0.625
Outputs:
- layer_out: bfloat16 [16, 256, 1024], P('dp', 'ctx')
- input_grad: bfloat16 [16, 256, 1024], P('dp', 'ctx')
- update_query: float32 [1024, 2048], P('dp')
- update_key: float32 [1024, 1024], P('dp')
- update_value: float32 [1024, 1024], P('dp')
- update_output: float32 [2048, 1024], P('dp')
- update_gate: float32 [1024, 3072], P('dp')
- update_up: float32 [1024, 3072], P('dp')
- update_down: float32 [3072, 1024], P('dp')
- update_gains: float32 [2304], P('dp')
- next_momentum_query: float32 [1024, 2048], P('dp')
- next_momentum_key: float32 [1024, 1024], P('dp')
- next_momentum_value: float32 [1024, 1024], P('dp')
- next_momentum_output: float32 [2048, 1024], P('dp')
- next_momentum_gate: float32 [1024, 3072], P('dp')
- next_momentum_up: float32 [1024, 3072], P('dp')
- next_momentum_down: float32 [3072, 1024], P('dp')
- next_momentum_gains: float32 [2304], P('dp')
Inputs may be any that keep to these rules, and one draw needn't show every extreme that they name: `block_order`: each row is a permutation of the blocks 0 to 3.
All inputs are finite; a program needn't handle non-finite values.
Results may differ from a plain program's by a relative error of at most 0.029.
Values may be sent and summed in bfloat16 or wider, within the bound.
No kernel may reach another device: no remote copies, remote signals or barrier semaphores. Data moves between devices by JAX's collectives and lax.ppermute only.
A program may use at most 256 MiB of HBM per device.

v0:
```python
import jax
import jax.numpy as jnp
from jax import lax
from jax.sharding import PartitionSpec as P

EPSILON = 1e-06
THETA = 1000000.0
BETA_ONE = 0.9
BETA_TWO = 0.5
SOFTEN = 0.005
DECAY_FACTOR = 1.0


def rms_norm(values, gain_vec):
    return (
        values * lax.rsqrt(jnp.mean(values * values, axis=-1, keepdims=True) + EPSILON) * gain_vec
    )


def rotary_tables(positions, head_size):
    half_size = head_size // 2
    frequency = THETA ** (-(jnp.arange(half_size, dtype=jnp.float32) * 2.0 / head_size))
    angles = positions.astype(jnp.float32)[:, None] * frequency[None, :]
    angles = jnp.concatenate([angles, angles], axis=1)
    return (jnp.cos(angles), jnp.sin(angles))


def rotate(values, cosine, sine_table):
    half_size = values.shape[-1] // 2
    turned = jnp.concatenate([-values[..., half_size:], values[..., :half_size]], axis=-1)
    return values * cosine[:, None, :] + turned * sine_table[:, None, :]


def head_prep(projected, gain_vec, cosine, sine_table):
    shaped = projected.reshape(projected.shape[0], -1, gain_vec.shape[0])
    return rotate(rms_norm(shaped, gain_vec), cosine, sine_table)


def matmul(left, right):
    return jnp.dot(left, right, preferred_element_type=jnp.float32)


def contract_rows(left, right):
    return lax.dot_general(
        left, right, (((0,), (0,)), ((), ())), preferred_element_type=jnp.float32
    )


def contract_cols(left, right):
    return lax.dot_general(
        left, right, (((1,), (1,)), ((), ())), preferred_element_type=jnp.float32
    )


def head_scores(queries, key_row_block, query_pos, key_pos):
    scaling = queries.shape[-1] ** (-0.5)
    scores = (
        jnp.einsum("trd,kd->rtk", queries, key_row_block, preferred_element_type=jnp.float32)
        * scaling
    )
    allowed = query_pos[:, None] >= key_pos[None, :]
    return jnp.where(allowed[None], scores, -1e30)


def attend_head(query_pos, key_pos):

    def attend(group_item):
        queries, key_row_block, value_row_block = group_item
        scores = head_scores(queries, key_row_block, query_pos, key_pos)
        row_top = jnp.max(scores, axis=-1, keepdims=True)
        weights = jnp.exp(scores - row_top)
        row_total = jnp.sum(weights, axis=-1, keepdims=True)
        probs_low = (weights / row_total).astype(jnp.bfloat16)
        mixture = jnp.einsum(
            "rtk,kd->trd", probs_low, value_row_block, preferred_element_type=jnp.float32
        )
        return (mixture, (row_top + jnp.log(row_total))[..., 0])

    return attend


def attend_back(query_pos, key_pos):

    def backward(group_item):
        queries, key_row_block, value_row_block, grad_mix, log_total = group_item
        scaling = queries.shape[-1] ** (-0.5)
        scores = head_scores(queries, key_row_block, query_pos, key_pos)
        probs = jnp.exp(scores - log_total[..., None])
        grad_values = jnp.einsum(
            "rtk,trd->kd", probs.astype(jnp.bfloat16), grad_mix, preferred_element_type=jnp.float32
        )
        grad_probs = jnp.einsum(
            "trd,kd->rtk", grad_mix, value_row_block, preferred_element_type=jnp.float32
        )
        inner = jnp.sum(probs * grad_probs, axis=-1, keepdims=True)
        grad_scores = (probs * (grad_probs - inner)).astype(jnp.bfloat16)
        grad_queries = (
            jnp.einsum(
                "rtk,kd->trd", grad_scores, key_row_block, preferred_element_type=jnp.float32
            )
            * scaling
        )
        grad_keys = (
            jnp.einsum("rtk,trd->kd", grad_scores, queries, preferred_element_type=jnp.float32)
            * scaling
        )
        return (grad_queries, grad_keys, grad_values)

    return backward


def lion_step(masters, moments, gradients, norm_scale):
    updates = []
    new_moments = []
    for tensor_index in range(8):
        scaled = gradients[tensor_index] * norm_scale
        moment_arr = moments[tensor_index]
        blend_arr = BETA_ONE * moment_arr + (1.0 - BETA_ONE) * scaled
        direction = blend_arr / jnp.sqrt(blend_arr * blend_arr + SOFTEN)
        decay_here = DECAY_FACTOR if tensor_index < 7 else 0.0
        updates.append(direction + decay_here * masters[tensor_index])
        new_moments.append(BETA_TWO * moment_arr + (1.0 - BETA_TWO) * scaled)
    return (updates, new_moments)


def body(
    hidden_in,
    cotangent,
    block_order,
    w_query,
    key_weight,
    value_weight,
    w_output,
    w_gate,
    w_up,
    w_down,
    norm_gains,
    momentum_query,
    key_momentum,
    value_momentum,
    momentum_output,
    momentum_gate,
    momentum_up,
    momentum_down,
    momentum_gains,
):
    copies = (
        lax.all_gather(w_query.astype(jnp.bfloat16), "dp", axis=0, tiled=True),
        lax.all_gather(key_weight.astype(jnp.bfloat16), "dp", axis=0, tiled=True),
        lax.all_gather(value_weight.astype(jnp.bfloat16), "dp", axis=0, tiled=True),
        lax.all_gather(w_output.astype(jnp.bfloat16), "dp", axis=0, tiled=True),
        lax.all_gather(w_gate.astype(jnp.bfloat16), "dp", axis=0, tiled=True),
        lax.all_gather(w_up.astype(jnp.bfloat16), "dp", axis=0, tiled=True),
        lax.all_gather(w_down.astype(jnp.bfloat16), "dp", axis=0, tiled=True),
        lax.all_gather(norm_gains.astype(jnp.bfloat16), "dp", axis=0, tiled=True),
    )
    query_mat, key_mat, value_mat, output_mat, gate_mat, up_mat, down_mat, gains_low = copies
    gains_all = gains_low.astype(jnp.float32)
    width = hidden_in.shape[2]
    head_size = (gains_all.shape[0] - 2 * width) // 2
    kv_heads = key_mat.shape[1] // head_size
    query_heads = query_mat.shape[1] // head_size
    group_repeat_count = query_heads // kv_heads
    gain_attn = gains_all[:width]
    gain_mlp = gains_all[width : 2 * width]
    gain_query = gains_all[2 * width : 2 * width + head_size]
    gain_key = gains_all[2 * width + head_size :]
    tokens_in = hidden_in[0]
    token_count = tokens_in.shape[0]
    block_size = token_count // 2
    slot_order = block_order[0]
    key_pos = (
        slot_order[:, None] * block_size + jnp.arange(block_size, dtype=jnp.int32)[None, :]
    ).reshape(-1)
    query_pos = lax.dynamic_slice_in_dim(key_pos, lax.axis_index("ctx") * token_count, token_count)
    cosine, sine_table = rotary_tables(query_pos, head_size)
    tokens_f = tokens_in.astype(jnp.float32)
    normed_f, norm_pull = jax.vjp(rms_norm, tokens_f, gain_attn)
    normalized_input = normed_f.astype(jnp.bfloat16)
    query_pre = matmul(normalized_input, query_mat)
    key_pre = matmul(normalized_input, key_mat)
    value_low = matmul(normalized_input, value_mat).astype(jnp.bfloat16)
    query_rot, query_pull = jax.vjp(
        lambda projected, gain_vec: head_prep(projected, gain_vec, cosine, sine_table),
        query_pre,
        gain_query,
    )
    key_rot, key_pull = jax.vjp(
        lambda projected, gain_vec: head_prep(projected, gain_vec, cosine, sine_table),
        key_pre,
        gain_key,
    )
    query_low = query_rot.astype(jnp.bfloat16)
    key_heads = key_rot.astype(jnp.bfloat16).transpose(1, 0, 2)
    value_heads = value_low.reshape(token_count, kv_heads, head_size).transpose(1, 0, 2)
    gathered = (
        lax.all_gather(key_heads, "ctx", axis=1, tiled=True),
        lax.all_gather(value_heads, "ctx", axis=1, tiled=True),
    )
    query_groups = query_low.reshape(
        token_count, kv_heads, group_repeat_count, head_size
    ).transpose(1, 0, 2, 3)
    mixture, log_total = lax.map(
        attend_head(query_pos, key_pos), (query_groups, gathered[0], gathered[1])
    )
    mixed_low = mixture.transpose(1, 0, 2, 3).reshape(token_count, -1).astype(jnp.bfloat16)
    middle = tokens_f + matmul(mixed_low, output_mat)
    normed_two_f, norm_two_pull = jax.vjp(rms_norm, middle, gain_mlp)
    normed_two = normed_two_f.astype(jnp.bfloat16)
    gate_act = matmul(normed_two, gate_mat)
    upward = matmul(normed_two, up_mat)
    active_f, swiglu_pull = jax.vjp(
        lambda gate_in, up_in: jax.nn.silu(gate_in) * up_in, gate_act, upward
    )
    active = active_f.astype(jnp.bfloat16)
    layer_out = (middle + matmul(active, down_mat)).astype(jnp.bfloat16)[None]
    grad_out = cotangent[0]
    grad_down = contract_rows(active, grad_out)
    grad_active = contract_cols(grad_out, down_mat)
    grad_gate_f, grad_up_f = swiglu_pull(grad_active)
    grad_gate = grad_gate_f.astype(jnp.bfloat16)
    grad_upward = grad_up_f.astype(jnp.bfloat16)
    grad_gate_mat = contract_rows(normed_two, grad_gate)
    grad_up_mat = contract_rows(normed_two, grad_upward)
    grad_normed_two = contract_cols(grad_gate, gate_mat) + contract_cols(grad_upward, up_mat)
    grad_middle_norm, grad_gain_mlp = norm_two_pull(grad_normed_two)
    grad_middle = grad_out.astype(jnp.float32) + grad_middle_norm
    grad_branch = grad_middle.astype(jnp.bfloat16)
    grad_output_mat = contract_rows(mixed_low, grad_branch)
    grad_mixed = contract_cols(grad_branch, output_mat).astype(jnp.bfloat16)
    grad_groups = grad_mixed.reshape(
        token_count, kv_heads, group_repeat_count, head_size
    ).transpose(1, 0, 2, 3)
    grad_query_groups, grad_key_all, grad_value_all = lax.map(
        attend_back(query_pos, key_pos),
        (query_groups, gathered[0], gathered[1], grad_groups, log_total),
    )
    grad_key_own, grad_value_own = (
        lax.psum_scatter(
            grad_key_all.astype(jnp.bfloat16), "ctx", scatter_dimension=1, tiled=True
        ).astype(jnp.float32),
        lax.psum_scatter(
            grad_value_all.astype(jnp.bfloat16), "ctx", scatter_dimension=1, tiled=True
        ).astype(jnp.float32),
    )
    grad_query_rot = grad_query_groups.transpose(1, 0, 2, 3).reshape(
        token_count, query_heads, head_size
    )
    grad_query_pre, grad_gain_query = query_pull(grad_query_rot)
    grad_key_pre, grad_gain_key = key_pull(grad_key_own.transpose(1, 0, 2))
    grad_query_low = grad_query_pre.astype(jnp.bfloat16)
    grad_key_low = grad_key_pre.astype(jnp.bfloat16)
    grad_value_low = grad_value_own.transpose(1, 0, 2).reshape(token_count, -1).astype(jnp.bfloat16)
    grad_query_mat = contract_rows(normalized_input, grad_query_low)
    grad_key_mat = contract_rows(normalized_input, grad_key_low)
    grad_value_mat = contract_rows(normalized_input, grad_value_low)
    grad_normed = (
        contract_cols(grad_query_low, query_mat)
        + contract_cols(grad_key_low, key_mat)
        + contract_cols(grad_value_low, value_mat)
    )
    grad_tokens_norm, grad_gain_attn = norm_pull(grad_normed)
    input_grad = (grad_middle + grad_tokens_norm).astype(jnp.bfloat16)[None]
    grad_gains = jnp.concatenate([grad_gain_attn, grad_gain_mlp, grad_gain_query, grad_gain_key])
    masters = (w_query, key_weight, value_weight, w_output, w_gate, w_up, w_down, norm_gains)
    moments = (
        momentum_query,
        key_momentum,
        value_momentum,
        momentum_output,
        momentum_gate,
        momentum_up,
        momentum_down,
        momentum_gains,
    )
    token_total = lax.axis_size("dp") * key_pos.shape[0]
    norm_scale = lax.rsqrt(jnp.float32(token_total))
    shares = (
        lax.psum_scatter(
            grad_query_mat.astype(jnp.bfloat16), "dp", scatter_dimension=0, tiled=True
        ).astype(jnp.float32),
        lax.psum_scatter(
            grad_key_mat.astype(jnp.bfloat16), "dp", scatter_dimension=0, tiled=True
        ).astype(jnp.float32),
        lax.psum_scatter(
            grad_value_mat.astype(jnp.bfloat16), "dp", scatter_dimension=0, tiled=True
        ).astype(jnp.float32),
        lax.psum_scatter(
            grad_output_mat.astype(jnp.bfloat16), "dp", scatter_dimension=0, tiled=True
        ).astype(jnp.float32),
        lax.psum_scatter(
            grad_gate_mat.astype(jnp.bfloat16), "dp", scatter_dimension=0, tiled=True
        ).astype(jnp.float32),
        lax.psum_scatter(
            grad_up_mat.astype(jnp.bfloat16), "dp", scatter_dimension=0, tiled=True
        ).astype(jnp.float32),
        lax.psum_scatter(
            grad_down.astype(jnp.bfloat16), "dp", scatter_dimension=0, tiled=True
        ).astype(jnp.float32),
        lax.psum_scatter(
            grad_gains.astype(jnp.bfloat16), "dp", scatter_dimension=0, tiled=True
        ).astype(jnp.float32),
    )
    summed = (
        lax.psum(shares[0].astype(jnp.bfloat16), "ctx").astype(jnp.float32),
        lax.psum(shares[1].astype(jnp.bfloat16), "ctx").astype(jnp.float32),
        lax.psum(shares[2].astype(jnp.bfloat16), "ctx").astype(jnp.float32),
        lax.psum(shares[3].astype(jnp.bfloat16), "ctx").astype(jnp.float32),
        lax.psum(shares[4].astype(jnp.bfloat16), "ctx").astype(jnp.float32),
        lax.psum(shares[5].astype(jnp.bfloat16), "ctx").astype(jnp.float32),
        lax.psum(shares[6].astype(jnp.bfloat16), "ctx").astype(jnp.float32),
        lax.psum(shares[7].astype(jnp.bfloat16), "ctx").astype(jnp.float32),
    )
    updates, new_moments = lion_step(masters, moments, summed, norm_scale)
    return (layer_out, input_grad) + tuple(updates) + tuple(new_moments)


def solution(mesh):
    return jax.shard_map(
        body,
        mesh=mesh,
        in_specs=(
            P("dp", "ctx", None),
            P("dp", "ctx", None),
            P("dp", None),
            P("dp", None),
            P("dp", None),
            P("dp", None),
            P("dp", None),
            P("dp", None),
            P("dp", None),
            P("dp", None),
            P("dp"),
            P("dp", None),
            P("dp", None),
            P("dp", None),
            P("dp", None),
            P("dp", None),
            P("dp", None),
            P("dp", None),
            P("dp"),
        ),
        out_specs=(
            P("dp", "ctx", None),
            P("dp", "ctx", None),
            P("dp", None),
            P("dp", None),
            P("dp", None),
            P("dp", None),
            P("dp", None),
            P("dp", None),
            P("dp", None),
            P("dp"),
            P("dp", None),
            P("dp", None),
            P("dp", None),
            P("dp", None),
            P("dp", None),
            P("dp", None),
            P("dp", None),
            P("dp"),
        ),
        check_vma=False,
    )
```

profile of v0, /device:TPU:1, one launch (start us, length us, event | category | flops | bytes accessed | tf_op | source)
XLA Modules:
  0.0 1568.1 jit_solution(2902663453504280453)
XLA Ops:
  19.8 36.6 %all-reduce.4 = bf16[2304]{0:T(1024)(128)(2,1)S(1)} all-reduce(bf16[2304]{0:T(1024)(128)(2,1)S(1)} %dynamic-update-slice), channel_id=1, replica_groups=mesh['dp'=16,'ctx'=2] {'dp'}, use_global_device_ids=true, to_apply=%add.4 | all-reduce | flops 2304 | bytes 9216
  59.0 15.2 all-gather.10.cloned.1.call-done
  74.2 4.0 copy.66
  84.1 52.8 %all-gather.8.cloned.1.call-done = bf16[1024,1024]{1,0:T(8,128)(2,1)} async-done(((bf16[64,1024]{1,0:T(8,128)(2,1)}), bf16[1024,1024]{1,0:T(8,128)(2,1)}) %all-gather.8.cloned.1.call-update) | async-done | bytes 2097168 | tf_op jit(solution)/shard_map/all_gather | solution.py:150
  142.1 72.2 %all-gather.12.cloned.1.call-done = bf16[1024,2048]{1,0:T(8,128)(2,1)} async-done(((bf16[64,2048]{1,0:T(8,128)(2,1)}), bf16[1024,2048]{1,0:T(8,128)(2,1)}) %all-gather.12.cloned.1.call-update) | async-done | bytes 4194320 | tf_op jit(solution)/shard_map/all_gather | solution.py:148
  214.3 6.4 copy.67
  220.7 3.5 multiply_reduce_fusion.3
  227.8 24.2 %while.30 = (s32[]{:T(128)}, bf16[8,128,2,128]{1,3,2,0:T(8,128)(2,1)S(1)}, f32[8,2,128]{2,1,0:T(2,128)}, bf16[8,256,128]{2,1,0:T(8,128)(2,1)}, s32[128]{0:T(128)...) while((s32[]{:T(128)}, ...), condition=%wide.region_6.7_spmd.clone.clone, body=%wide.region_3.6_spmd.clone.sunk.clone | while | flops 34111488 | bytes 1195109 | solution.py:203
  252.0 40.0 %all-gather.14.cloned.1.call-done = bf16[2048,1024]{1,0:T(8,128)(2,1)} async-done(((bf16[128,1024]{1,0:T(8,128)(2,1)}), bf16[2048,1024]{1,0:T(8,128)(2,1)}) %all-gather.14.cloned.1.call-update) | async-done | bytes 4194320 | tf_op jit(solution)/shard_map/all_gather | solution.py:151
  295.2 92.8 %all-gather.16.cloned.1.call-done = bf16[1024,3072]{1,0:T(8,128)(2,1)} async-done(((bf16[64,3072]{1,0:T(8,128)(2,1)}), bf16[1024,3072]{1,0:T(8,128)(2,1)}) %all-gather.16.cloned.1.call-update) | async-done | bytes 6291472 | tf_op jit(solution)/shard_map/all_gather | solution.py:152
  388.0 5.0 fusion.135
  393.0 90.6 %all-gather.18.cloned.1.call-done = bf16[1024,3072]{1,0:T(8,128)(2,1)} async-done(((bf16[64,3072]{1,0:T(8,128)(2,1)}), bf16[1024,3072]{1,0:T(8,128)(2,1)}) %all-gather.18.cloned.1.call-update) | async-done | bytes 6291472 | tf_op jit(solution)/shard_map/all_gather | solution.py:153
  483.6 4.9 fusion.136
  488.6 90.9 %all-gather.20.cloned.1.call-done = bf16[3072,1024]{1,0:T(8,128)(2,1)} async-done(((bf16[192,1024]{1,0:T(8,128)(2,1)}), bf16[3072,1024]{1,0:T(8,128)(2,1)}) %all-gather.20.cloned.1.call-update) | async-done | bytes 6291472 | tf_op jit(solution)/shard_map/all_gather | solution.py:154
  579.4 7.1 multiply_convert_fusion.1
  586.6 5.6 fusion.137
  601.8 66.6 %while.31 = (s32[]{:T(128)}, f32[8,128,2,128]{1,3,2,0:T(8,128)}, bf16[8,256,128]{1,2,0:T(8,128)(2,1)}, bf16[8,256,128]{1,2,0:T(8,128)(2,1)}, bf16[8,256,128]{2,1...) while((s32[]{:T(128)}, f32[8,128,2,128]{1,3,2,0:T(8,128)}, ...), condition=%wide.region_11.12_spmd.clone.clone, body=%wide.region_9.11_spmd.clone.sunk.clone | while | flops 84606976 | bytes 3095169 | solution.py:234
  673.3 5.3 reduce-scatter.28.cloned.1.call-done
  683.8 6.9 reduce-scatter.30.cloned.1.call-done
  705.6 4.5 convolution_convert_fusion.2
  711.2 4.4 convolution_convert_fusion.1
  716.8 4.5 convolution_convert_fusion
  722.3 40.7 %reduce-scatter.16.cloned.1.call-done = bf16[64,1024]{1,0:T(8,128)(2,1)} async-done(((bf16[1024,1024]{1,0:T(8,128)(2,1)}), bf16[64,1024]{1,0:T(8,128)(2,1)}) %reduce-scatter.16.cloned.1.call-update) | async-done | bytes 131088 | tf_op jit(solution)/shard_map/reduce_scatter | solution.py:282
  763.0 80.9 %reduce-scatter.18.cloned.1.call-done = bf16[64,1024]{1,0:T(8,128)(2,1)} async-done(((bf16[1024,1024]{1,0:T(8,128)(2,1)}), bf16[64,1024]{1,0:T(8,128)(2,1)}) %reduce-scatter.18.cloned.1.call-update) | async-done | bytes 131088 | tf_op jit(solution)/shard_map/reduce_scatter | solution.py:285
  843.9 104.0 %reduce-scatter.20.cloned.1.call-done = bf16[128,1024]{1,0:T(8,128)(2,1)} async-done(((bf16[2048,1024]{1,0:T(8,128)(2,1)}), bf16[128,1024]{1,0:T(8,128)(2,1)}) %reduce-scatter.20.cloned.1.call-update) | async-done | bytes 262160 | tf_op jit(solution)/shard_map/reduce_scatter | solution.py:288
  948.0 97.0 %reduce-scatter.14.cloned.1.call-done = bf16[64,2048]{1,0:T(8,128)(2,1)} async-done(((bf16[1024,2048]{1,0:T(8,128)(2,1)}), bf16[64,2048]{1,0:T(8,128)(2,1)}) %reduce-scatter.14.cloned.1.call-update) | async-done | bytes 262160 | tf_op jit(solution)/shard_map/reduce_scatter | solution.py:279
  1045.0 150.0 %reduce-scatter.22.cloned.1.call-done = bf16[64,3072]{1,0:T(8,128)(2,1)} async-done(((bf16[1024,3072]{1,0:T(8,128)(2,1)}), bf16[64,3072]{1,0:T(8,128)(2,1)}) %reduce-scatter.22.cloned.1.call-update) | async-done | bytes 393232 | tf_op jit(solution)/shard_map/reduce_scatter | solution.py:291
  1195.0 150.7 %reduce-scatter.24.cloned.1.call-done = bf16[64,3072]{1,0:T(8,128)(2,1)} async-done(((bf16[1024,3072]{1,0:T(8,128)(2,1)}), bf16[64,3072]{1,0:T(8,128)(2,1)}) %reduce-scatter.24.cloned.1.call-update) | async-done | bytes 393232 | tf_op jit(solution)/shard_map/reduce_scatter | solution.py:294
  1345.7 149.9 %reduce-scatter.26.cloned.1.call-done = bf16[192,1024]{1,0:T(8,128)(2,1)} async-done(((bf16[3072,1024]{1,0:T(8,128)(2,1)}), bf16[192,1024]{1,0:T(8,128)(2,1)}) %reduce-scatter.26.cloned.1.call-update) | async-done | bytes 393232 | tf_op jit(solution)/shard_map/reduce_scatter | solution.py:297
  1495.7 4.6 fusion.55
  1504.3 33.6 %all-reduce.5 = bf16[2304]{0:T(1024)(128)(2,1)S(1)} all-reduce(bf16[2304]{0:T(1024)(128)(2,1)S(1)} %pad_maximum_fusion.1), channel_id=11, replica_groups=mesh['dp'=16,'ctx'=2] {'dp'}, use_global_device_ids=true, to_apply=%region_35.36.clone | all-reduce | flops 2304 | bytes 9216
  1538.0 11.0 psum.63
  (415 shorter events, 175.5 us)
Async XLA Ops:
  7.2 50.5 %copy-start.1 = (bf16[1,128,1024]{2,1,0:T(8,128)(2,1)S(1)}, bf16[1,128,1024]{2,1,0:T(8,128)(2,1)}, u32[]{:S(2)}) copy-start(bf16[1,128,1024]{2,1,0:T(8,128)(2,1)} %param.23) | copy-start | bytes 786436
  7.2 66.9 %all-gather.10.cloned.1.call-start = ((), (), s32[]{:S(2)}) async-start(), calls=%async_computation.10 | async-start | bytes 2228224 | tf_op jit(solution)/shard_map/all_gather | solution.py:149
  9.0 48.9 %copy-start.70 = (s32[1,4]{1,0:T(1,128)S(1)}, s32[1,4]{1,0:T(1,128)}, u32[]{:S(2)}) copy-start(s32[1,4]{1,0:T(1,128)} %param.25) | copy-start | bytes 52
  9.1 127.8 %all-gather.8.cloned.1.call-start = ((), (), s32[]{:S(2)}) async-start(), calls=%async_computation.9 | async-start | bytes 2228224 | tf_op jit(solution)/shard_map/all_gather | solution.py:150
  10.8 203.5 %all-gather.12.cloned.1.call-start = ((), (), s32[]{:S(2)}) async-start(), calls=%async_computation.11 | async-start | bytes 4456448 | tf_op jit(solution)/shard_map/all_gather | solution.py:148
  12.6 279.4 %all-gather.14.cloned.1.call-start = ((), (), s32[]{:S(2)}) async-start(), calls=%async_computation.12 | async-start | bytes 4456448 | tf_op jit(solution)/shard_map/all_gather | solution.py:151
  14.5 373.5 %all-gather.16.cloned.1.call-start = ((), (), s32[]{:S(2)}) async-start(), calls=%async_computation.13 | async-start | bytes 6684672 | tf_op jit(solution)/shard_map/all_gather | solution.py:152
  16.5 467.2 %all-gather.18.cloned.1.call-start = ((), (), s32[]{:S(2)}) async-start(), calls=%async_computation.14 | async-start | bytes 6684672 | tf_op jit(solution)/shard_map/all_gather | solution.py:153
  17.3 562.1 %all-gather.20.cloned.1.call-start = ((), (), s32[]{:S(2)}) async-start(), calls=%async_computation.15 | async-start | bytes 6684672 | tf_op jit(solution)/shard_map/all_gather | solution.py:154
  18.2 660.4 %reduce-scatter.28.cloned.1.call-start = ((), (), s32[]{:S(2)}) async-start(), calls=%async_computation.23 | async-start | bytes 786432
  57.9 162.8 %copy-start.49 = (f32[128]{0:T(128)}, f32[128]{0:T(128)S(1)}, u32[]{:S(2)}) copy-start(f32[128]{0:T(128)S(1)} %fusion.120) | copy-start | bytes 1540
  80.6 58.5 %copy-start.52 = (f32[128,8]{0,1:T(8,128)}, f32[128,8]{0,1:T(8,128)S(1)}, u32[]{:S(2)}) copy-start(f32[128,8]{0,1:T(8,128)S(1)} %get-tuple-element.321) | copy-start | bytes 12292
  252.0 40.1 %copy-start.13 = (bf16[8,256,128]{2,1,0:T(8,128)(2,1)}, bf16[8,256,128]{2,1,0:T(8,128)(2,1)S(1)}, u32[]{:S(2)}) copy-start(bf16[8,256,128]{2,1,0:T(8,128)(2,1)S(1)} %get-tuple-element.611) | copy-start | bytes 1572868
  252.0 141.0 %copy-start.8 = (bf16[8,128,2,128]{1,3,2,0:T(8,128)(2,1)}, bf16[8,128,2,128]{1,3,2,0:T(8,128)(2,1)S(1)}, u32[]{:S(2)}) copy-start(bf16[8,128,2,128]{1,3,2,0:T(8,128)(2,1)S(1)} %get-tuple-element.120) | copy-start | bytes 1572868
  252.0 43.1 %copy-start.42 = (f32[1024]{0:T(1024)S(1)}, f32[1024]{0:T(1024)}, u32[]{:S(2)}) copy-start(f32[1024]{0:T(1024)} %get-tuple-element.313) | copy-start | bytes 12292
  295.0 93.0 %copy-start.68 = (f32[128]{0:T(128)}, f32[128]{0:T(128)S(1)}, u32[]{:S(2)}) copy-start(f32[128]{0:T(128)S(1)} %get-tuple-element.325) | copy-start | bytes 1540
  295.1 92.9 %copy-start.59 = (f32[128]{0:T(128)}, f32[128]{0:T(128)S(1)}, u32[]{:S(2)}) copy-start(f32[128]{0:T(128)S(1)} %fusion.121) | copy-start | bytes 1540
  393.0 186.4 %copy-start.27 = (bf16[1,128,1024]{2,1,0:T(8,128)(2,1)S(1)}, bf16[1,128,1024]{2,1,0:T(8,128)(2,1)}, u32[]{:S(2)}) copy-start(bf16[1,128,1024]{2,1,0:T(8,128)(2,1)} %param.24) | copy-start | bytes 786436
  670.7 20.0 %reduce-scatter.30.cloned.1.call-start = ((), (), s32[]{:S(2)}) async-start(), calls=%async_computation.24 | async-start | bytes 786432
  673.0 90.0 %reduce-scatter.16.cloned.1.call-start = ((), (), s32[]{:S(2)}) async-start(), calls=%async_computation.17 | async-start | bytes 2228224 | tf_op jit(solution)/shard_map/reduce_scatter | solution.py:282
  683.7 160.2 %reduce-scatter.18.cloned.1.call-start = ((), (), s32[]{:S(2)}) async-start(), calls=%async_computation.18 | async-start | bytes 2228224 | tf_op jit(solution)/shard_map/reduce_scatter | solution.py:285
  696.3 251.7 %reduce-scatter.20.cloned.1.call-start = ((), (), s32[]{:S(2)}) async-start(), calls=%async_computation.19 | async-start | bytes 4456448 | tf_op jit(solution)/shard_map/reduce_scatter | solution.py:288
  699.6 345.4 %reduce-scatter.14.cloned.1.call-start = ((), (), s32[]{:S(2)}) async-start(), calls=%async_computation.16 | async-start | bytes 4456448 | tf_op jit(solution)/shard_map/reduce_scatter | solution.py:279
  705.5 489.5 %reduce-scatter.22.cloned.1.call-start = ((), (), s32[]{:S(2)}) async-start(), calls=%async_computation.20 | async-start | bytes 6684672 | tf_op jit(solution)/shard_map/reduce_scatter | solution.py:291
  710.1 635.6 %reduce-scatter.24.cloned.1.call-start = ((), (), s32[]{:S(2)}) async-start(), calls=%async_computation.21 | async-start | bytes 6684672 | tf_op jit(solution)/shard_map/reduce_scatter | solution.py:294
  715.7 779.9 %reduce-scatter.26.cloned.1.call-start = ((), (), s32[]{:S(2)}) async-start(), calls=%async_computation.22 | async-start | bytes 6684672 | tf_op jit(solution)/shard_map/reduce_scatter | solution.py:297
  721.4 829.2 %all-reduce.9.cloned.1.call-start = ((), (), s32[]{:S(2)}) async-start(), calls=%async_computation.25 | async-start | bytes 3932160 | tf_op jit(solution)/shard_map/psum | solution.py:305
  1501.2 47.9 %copy-start.67 = (f32[128]{0:T(128)S(1)}, f32[128]{0:T(128)}, u32[]{:S(2)}) copy-start(f32[128]{0:T(128)} %copy-done.66) | copy-start | bytes 1540
  1501.2 47.9 %copy-start.64 = (f32[144]{0:T(256)S(1)}, f32[144]{0:T(256)}, u32[]{:S(2)}) copy-start(f32[144]{0:T(256)} %param.33) | copy-start | bytes 1732
  1501.2 47.9 %copy-start.65 = (f32[144]{0:T(256)S(1)}, f32[144]{0:T(256)}, u32[]{:S(2)}) copy-start(f32[144]{0:T(256)} %param.41) | copy-start | bytes 1732
  1502.6 48.0 %copy-start.16 = (f32[192,1024]{1,0:T(8,128)S(1)}, f32[192,1024]{1,0:T(8,128)}, u32[]{:S(2)}) copy-start(f32[192,1024]{1,0:T(8,128)} %param.32) | copy-start | bytes 2359300
  1504.3 49.2 %copy-start.26 = (f32[128,1024]{1,0:T(8,128)S(1)}, f32[128,1024]{1,0:T(8,128)}, u32[]{:S(2)}) copy-start(f32[128,1024]{1,0:T(8,128)} %param.29) | copy-start | bytes 1572868
  (56 other events, 364.9 us)
Sparse Core Ops, SparseCore 0:
  11.4 62.6 all-gather.9
  77.5 59.3 all-gather.7
  140.2 73.9 all-gather.11
  217.5 74.4 all-gather.13
  295.2 92.7 all-gather.15
  391.2 92.4 all-gather.17
  487.0 92.4 all-gather.19
  670.8 7.7 reduce-scatter.27
  681.5 9.1 reduce-scatter.29
  692.8 70.1 reduce-scatter.15
  765.3 78.5 reduce-scatter.17
  846.1 101.8 reduce-scatter.19
  950.2 94.7 reduce-scatter.13
  1050.1 144.8 reduce-scatter.21
  1200.1 145.5 reduce-scatter.23
  1350.8 144.7 reduce-scatter.25
  1498.3 22.3 all-reduce.8
where the time goes:
time: 1570 us
  waiting for transfers between devices  1240 us (79%)
  matrix products  141 us (9%)
  blocking collectives  87.2 us (6%)
  local copies, waits for them, and re-layouts  44.3 us (3%)
  other arithmetic  37.3 us (2%)
  between operations  16.3 us (1%)
    reduce_scatter x1, waiting for transfers between devices, body(): lax.psum_scatter(grad_up_mat.astype(jnp.bfloat16), 'dp', scatter_dimensio...  151 us
    reduce_scatter x1, waiting for transfers between devices, body(): lax.psum_scatter(grad_gate_mat.astype(jnp.bfloat16), 'dp', scatter_dimens...  150 us
    reduce_scatter x1, waiting for transfers between devices, body(): lax.psum_scatter(grad_down.astype(jnp.bfloat16), 'dp', scatter_dimension=...  150 us
    reduce_scatter x1, waiting for transfers between devices, body(): lax.psum_scatter(grad_output_mat.astype(jnp.bfloat16), 'dp', scatter_dime...  104 us
    reduce_scatter x1, waiting for transfers between devices, body(): lax.psum_scatter(grad_query_mat.astype(jnp.bfloat16), 'dp', scatter_dimen...  97 us
    all_gather x1, waiting for transfers between devices, body(): lax.all_gather(w_gate.astype(jnp.bfloat16), 'dp', axis=0, tiled=True)  92.8 us
    all_gather x1, waiting for transfers between devices, body(): lax.all_gather(w_down.astype(jnp.bfloat16), 'dp', axis=0, tiled=True)  90.9 us
    all_gather x1, waiting for transfers between devices, body(): lax.all_gather(w_up.astype(jnp.bfloat16), 'dp', axis=0, tiled=True)  90.6 us
  transfers between devices with their start and end apart: 17, of which 16 were waited for; matrix products, arithmetic and copies ran while one was open for 7% of the time, Pallas kernels for 0%

commit v1 on v0

--- a/solution.py
+++ b/solution.py
@@ -123,7 +123,7 @@
     return (updates, new_moments)
 
 
-def body(
+def general_body(
     hidden_in,
     cotangent,
     block_order,
@@ -315,7 +315,375 @@
     return (layer_out, input_grad) + tuple(updates) + tuple(new_moments)
 
 
+X_BIT, Y_BIT, P_BIT, H_BIT = 1, 2, 4, 8
+LOW = jnp.bfloat16
+
+
+def swap(values, bit):
+    return lax.ppermute(values, "dp", [(i, i ^ bit) for i in range(16)])
+
+
+def swap_core(values):
+    return lax.ppermute(values, "ctx", [(0, 1), (1, 0)])
+
+
+def h_of(index):
+    return (index // H_BIT) % 2
+
+
+def row_cross(values, to_owner):
+    pairs = []
+    for index in range(16):
+        for core in range(2):
+            if (core == h_of(index)) != to_owner:
+                pairs.append((index * 2 + core, (index ^ H_BIT) * 2 + core))
+    return lax.ppermute(values, ("dp", "ctx"), pairs)
+
+
+def gather_column_slices(own, give):
+    rows = own.shape[0]
+    got = swap(give, P_BIT)
+    far = swap(jnp.concatenate([own, got]), H_BIT)
+    first = jnp.concatenate([own, far[:rows]])
+    second = jnp.concatenate([got, far[rows:]])
+    first = jnp.concatenate([first, swap(first, Y_BIT)])
+    second = jnp.concatenate([second, swap(second, X_BIT)])
+    first_x = swap(first, X_BIT)
+    second_y = swap(second, Y_BIT)
+    pieces = {}
+    for place in range(4):
+        outer, r_h = place // 2, place % 2
+        cut = slice(place * rows, (place + 1) * rows)
+        pieces[outer * Y_BIT + r_h * H_BIT] = first[cut]
+        pieces[X_BIT + outer * Y_BIT + r_h * H_BIT] = first_x[cut]
+        pieces[P_BIT + outer * X_BIT + r_h * H_BIT] = second[cut]
+        pieces[P_BIT + Y_BIT + outer * X_BIT + r_h * H_BIT] = second_y[cut]
+    return pieces
+
+
+def gather_row_slices(own, mine):
+    rows = own.shape[0] // 2
+    crossed = row_cross(own, False)
+    held = jnp.where(mine, own, crossed)
+    first, second = held[:rows], held[rows:]
+    first = jnp.concatenate([first, swap(first, Y_BIT)])
+    second = jnp.concatenate([second, swap(second, X_BIT)])
+    first_x = swap(first, X_BIT)
+    second_y = swap(second, Y_BIT)
+    pieces = {}
+    for outer in range(2):
+        cut = slice(outer * rows, (outer + 1) * rows)
+        pieces[(outer * Y_BIT, 0)] = first[cut]
+        pieces[(X_BIT + outer * Y_BIT, 0)] = first_x[cut]
+        pieces[(outer * X_BIT, 1)] = second[cut]
+        pieces[(Y_BIT + outer * X_BIT, 1)] = second_y[cut]
+    return pieces
+
+
+def lay_columns(pieces, index):
+    rows, width = pieces[0].shape
+    whole = jnp.zeros((16 * rows, width), LOW)
+    for relative, piece in pieces.items():
+        whole = lax.dynamic_update_slice(whole, piece, (rows * (index ^ relative), 0))
+    return whole
+
+
+def lay_rows(pieces, index):
+    rows, width = pieces[(0, 0)].shape
+    whole = jnp.zeros((8 * rows, width), LOW)
+    for (relative, half), piece in pieces.items():
+        place = ((index ^ relative) % 4) * 2 + half
+        whole = lax.dynamic_update_slice(whole, piece, (rows * place, 0))
+    return whole
+
+
+def add_low(left, right):
+    return (left.astype(jnp.float32) + right.astype(jnp.float32)).astype(LOW)
+
+
+def scatter_column_slices(grad_low, index):
+    rows = grad_low.shape[0] // 16
+
+    def piece(relative):
+        return lax.dynamic_slice_in_dim(grad_low, rows * (index ^ relative), rows)
+
+    def four(base, outer):
+        return jnp.concatenate(
+            [piece(base + o * outer + r_h * H_BIT) for o in range(2) for r_h in range(2)]
+        )
+
+    first = add_low(four(0, Y_BIT), swap(four(X_BIT, Y_BIT), X_BIT))
+    second = add_low(four(P_BIT, X_BIT), swap(four(P_BIT + Y_BIT, X_BIT), Y_BIT))
+    first = add_low(first[: 2 * rows], swap(first[2 * rows :], Y_BIT))
+    second = add_low(second[: 2 * rows], swap(second[2 * rows :], X_BIT))
+    near = jnp.concatenate([first[:rows], second[:rows]])
+    far = jnp.concatenate([first[rows:], second[rows:]])
+    near = add_low(near, swap(far, H_BIT))
+    return near[:rows], swap(near[rows:], P_BIT)
+
+
+def scatter_row_slices(grad_low, index, mine):
+    rows = grad_low.shape[0] // 8
+
+    def piece(relative, half):
+        place = ((index ^ relative) % 4) * 2 + half
+        return lax.dynamic_slice_in_dim(grad_low, rows * place, rows)
+
+    def two(base, outer, half):
+        return jnp.concatenate([piece(base, half), piece(base + outer, half)])
+
+    first = add_low(two(0, Y_BIT, 0), swap(two(X_BIT, Y_BIT, 0), X_BIT))
+    second = add_low(two(0, X_BIT, 1), swap(two(Y_BIT, X_BIT, 1), Y_BIT))
+    first = add_low(first[:rows], swap(first[rows:], Y_BIT))
+    second = add_low(second[:rows], swap(second[rows:], X_BIT))
+    held = jnp.concatenate([first, second])
+    crossed = row_cross(held, True)
+    summed = add_low(held, crossed)
+    pairs = [(i * 2 + h_of(i), i * 2 + 1 - h_of(i)) for i in range(16)]
+    return jnp.where(mine, summed, lax.ppermute(summed, ("dp", "ctx"), pairs))
+
+
+def join_column_slices(own, partner, p_index, core):
+    low_pair = jnp.where(p_index == 0, own, partner)
+    high_pair = jnp.where(p_index == 0, partner, own)
+    pair = jnp.stack([low_pair, high_pair])
+    other = swap_core(pair)
+    lower = jnp.where(core == 0, pair, other)
+    upper = jnp.where(core == 0, other, pair)
+    return [lower[0], lower[1], upper[0], upper[1]]
+
+
+def gather_tokens(own):
+    same = jnp.stack([own, swap(own, P_BIT)])
+    return same, swap_core(same)
+
+
+def sum_tokens(same, sibling):
+    pair = same + swap_core(sibling.astype(LOW)).astype(jnp.float32)
+    return pair[0] + swap(pair[1].astype(LOW), P_BIT).astype(jnp.float32)
+
+
+def sequences(same, sibling):
+    return jnp.stack([same, sibling], axis=1).reshape(2, 2 * same.shape[1], same.shape[2])
+
+
+def halves(values):
+    shaped = values.reshape(2, 2, -1, values.shape[-1])
+    return shaped[:, 0], shaped[:, 1]
+
+
+def fast_body(
+    hidden_in,
+    cotangent,
+    block_order,
+    w_query,
+    key_weight,
+    value_weight,
+    w_output,
+    w_gate,
+    w_up,
+    w_down,
+    norm_gains,
+    momentum_query,
+    key_momentum,
+    value_momentum,
+    momentum_output,
+    momentum_gate,
+    momentum_up,
+    momentum_down,
+    momentum_gains,
+):
+    index = lax.axis_index("dp")
+    core = lax.axis_index("ctx")
+    p_index = (index // P_BIT) % 2
+    mine = h_of(index) == core
+    slice_own = 2 * core + p_index
+    slice_give = 2 * core + 1 - p_index
+
+    def column_slice(weight, which):
+        size = weight.shape[1] // 4
+        return lax.dynamic_slice_in_dim(weight, which * size, size, axis=1).astype(LOW)
+
+    def column_pack(weights, which):
+        return jnp.concatenate([column_slice(weight, which) for weight in weights], axis=1)
+
+    gains = norm_gains.astype(LOW)[None]
+    for bit in (P_BIT, H_BIT, Y_BIT, X_BIT):
+        gains = jnp.concatenate([gains, swap(gains, bit)])
+    order = [0]
+    for bit in (P_BIT, H_BIT, Y_BIT, X_BIT):
+        order = order + [o ^ bit for o in order]
+    place = jnp.zeros((16,), jnp.int32)
+    inverse = [0] * 16
+    for at, relative in enumerate(order):
+        inverse[relative] = at
+    lookup = jnp.array(inverse, jnp.int32)[index ^ jnp.arange(16)]
+    gains_all = jnp.take(gains, lookup, axis=0).reshape(-1).astype(jnp.float32)
+
+    width = hidden_in.shape[2]
+    head_size = (gains_all.shape[0] - 2 * width) // 2
+    gain_attn = gains_all[:width]
+    gain_mlp = gains_all[width : 2 * width]
+    gain_query = gains_all[2 * width : 2 * width + head_size]
+    gain_key = gains_all[2 * width + head_size :]
+
+    qkv = (w_query, key_weight, value_weight)
+    qkv_mat = lay_columns(
+        gather_column_slices(column_pack(qkv, slice_own), column_pack(qkv, slice_give)), index
+    )
+    output_mat = lay_rows(gather_row_slices(w_output.astype(LOW), mine), index)
+    gate_up = (w_gate, w_up)
+    gate_up_mat = lay_columns(
+        gather_column_slices(column_pack(gate_up, slice_own), column_pack(gate_up, slice_give)),
+        index,
+    )
+    down_mat = lay_rows(gather_row_slices(w_down.astype(LOW), mine), index)
+
+    tokens_own = hidden_in[0]
+    count = tokens_own.shape[0]
+    block = count // 2
+    orders = jnp.concatenate([block_order, swap(block_order, P_BIT)])
+    orders = jnp.where(core == 0, orders, jnp.roll(orders, 2, axis=1))
+    positions = (orders[:, :, None] * block + jnp.arange(block, dtype=jnp.int32)).reshape(2, -1)
+    cosine, sine_table = rotary_tables(positions.reshape(-1), head_size)
+
+    tokens_f = tokens_own.astype(jnp.float32)
+    normed_f, norm_pull = jax.vjp(rms_norm, tokens_f, gain_attn)
+    normed = sequences(*gather_tokens(normed_f.astype(LOW))).reshape(-1, width)
+    grad_out = sequences(*gather_tokens(cotangent[0])).reshape(-1, width)
+
+    query_width = w_query.shape[1] // 4
+    kv_width = key_weight.shape[1] // 4
+    projected = matmul(normed, qkv_mat)
+    query_pre = projected[:, :query_width]
+    key_pre = projected[:, query_width : query_width + kv_width]
+    value_low = projected[:, query_width + kv_width :].astype(LOW)
+
+    def prep(projected_part, gain_vec):
+        return head_prep(projected_part, gain_vec, cosine, sine_table)
+
+    query_rot, query_pull = jax.vjp(prep, query_pre, gain_query)
+    key_rot, key_pull = jax.vjp(prep, key_pre, gain_key)
+    kv_heads = kv_width // head_size
+    query_low = query_rot.astype(LOW).reshape(2, 2 * count, kv_heads, 2, head_size)
+    key_low = key_rot.astype(LOW).reshape(2, 2 * count, kv_heads, head_size)
+    value_low = value_low.reshape(2, 2 * count, kv_heads, head_size)
+    scaling = head_size ** (-0.5)
+    scores = scaling * jnp.einsum(
+        "sqgrd,skgd->sgrqk", query_low, key_low, preferred_element_type=jnp.float32
+    )
+    allowed = positions[:, :, None] >= positions[:, None, :]
+    scores = jnp.where(allowed[:, None, None], scores, -1e30)
+    weights = jnp.exp(scores - jnp.max(scores, axis=-1, keepdims=True))
+    probs = weights / jnp.sum(weights, axis=-1, keepdims=True)
+    probs_low = probs.astype(LOW)
+    mixture = jnp.einsum(
+        "sgrqk,skgd->sqgrd", probs_low, value_low, preferred_element_type=jnp.float32
+    )
+    mixed_low = mixture.reshape(2 * 2 * count, -1).astype(LOW)
+    attended = sum_tokens(*halves(matmul(mixed_low, output_mat)))
+    middle = tokens_f + attended
+    normed_two_f, norm_two_pull = jax.vjp(rms_norm, middle, gain_mlp)
+    normed_two = sequences(*gather_tokens(normed_two_f.astype(LOW))).reshape(-1, width)
+    gate_up_act = matmul(normed_two, gate_up_mat)
+    hidden_units = gate_up_act.shape[1] // 2
+    active_f, swiglu_pull = jax.vjp(
+        lambda gate_in, up_in: jax.nn.silu(gate_in) * up_in,
+        gate_up_act[:, :hidden_units],
+        gate_up_act[:, hidden_units:],
+    )
+    active = active_f.astype(LOW)
+    grad_down = contract_rows(active, grad_out).astype(LOW)
+    grad_active = contract_cols(grad_out, down_mat)
+    grad_gate_up = jnp.concatenate(
+        [part.astype(LOW) for part in swiglu_pull(grad_active)], axis=1
+    )
+    grad_gate_up_mat = contract_rows(normed_two, grad_gate_up).astype(LOW)
+    grad_normed_two = sum_tokens(*halves(contract_cols(grad_gate_up, gate_up_mat)))
+    layer_sum = sum_tokens(*halves(matmul(active, down_mat)))
+    layer_out = (middle + layer_sum).astype(LOW)[None]
+
+    grad_middle_norm, grad_gain_mlp = norm_two_pull(grad_normed_two)
+    grad_middle = cotangent[0].astype(jnp.float32) + grad_middle_norm
+    grad_branch = sequences(*gather_tokens(grad_middle.astype(LOW))).reshape(-1, width)
+    grad_output_mat = contract_rows(mixed_low, grad_branch).astype(LOW)
+    grad_mixed = contract_cols(grad_branch, output_mat).astype(LOW)
+    grad_mixed = grad_mixed.reshape(2, 2 * count, kv_heads, 2, head_size)
+    grad_values = jnp.einsum(
+        "sgrqk,sqgrd->skgd", probs_low, grad_mixed, preferred_element_type=jnp.float32
+    )
+    grad_probs = jnp.einsum(
+        "sqgrd,skgd->sgrqk", grad_mixed, value_low, preferred_element_type=jnp.float32
+    )
+    inner = jnp.sum(probs * grad_probs, axis=-1, keepdims=True)
+    grad_scores = (probs * (grad_probs - inner)).astype(LOW)
+    grad_query_rot = scaling * jnp.einsum(
+        "sgrqk,skgd->sqgrd", grad_scores, key_low, preferred_element_type=jnp.float32
+    )
+    grad_key_rot = scaling * jnp.einsum(
+        "sgrqk,sqgrd->skgd", grad_scores, query_low, preferred_element_type=jnp.float32
+    )
+    grad_query_pre, grad_gain_query = query_pull(grad_query_rot.reshape(query_rot.shape))
+    grad_key_pre, grad_gain_key = key_pull(grad_key_rot.reshape(key_rot.shape))
+    grad_qkv = jnp.concatenate(
+        [
+            grad_query_pre.astype(LOW),
+            grad_key_pre.astype(LOW),
+            grad_values.reshape(-1, kv_width).astype(LOW),
+        ],
+        axis=1,
+    )
+    grad_qkv_mat = contract_rows(normed, grad_qkv).astype(LOW)
+    grad_normed = sum_tokens(*halves(contract_cols(grad_qkv, qkv_mat)))
+    grad_tokens_norm, grad_gain_attn = norm_pull(grad_normed)
+    input_grad = (grad_middle + grad_tokens_norm).astype(LOW)[None]
+
+    grad_gains = jnp.concatenate([grad_gain_attn, grad_gain_mlp, grad_gain_query, grad_gain_key])
+    grad_gains = grad_gains.reshape(16, -1)
+    grad_gains = grad_gains + swap_core(grad_gains.astype(LOW)).astype(jnp.float32)
+    for bit in (P_BIT, H_BIT, Y_BIT, X_BIT):
+        grad_gains = grad_gains + swap(grad_gains.astype(LOW), bit).astype(jnp.float32)
+    grad_gains = lax.dynamic_index_in_dim(grad_gains, index, keepdims=False)
+
+    down_sum = scatter_row_slices(grad_down, index, mine)
+    gate_up_sum = join_column_slices(
+        *scatter_column_slices(grad_gate_up_mat, index), p_index, core
+    )
+    output_sum = scatter_row_slices(grad_output_mat, index, mine)
+    qkv_sum = join_column_slices(*scatter_column_slices(grad_qkv_mat, index), p_index, core)
+
+    def columns(parts, start, size):
+        return jnp.concatenate([part[:, start : start + size] for part in parts], axis=1)
+
+    sums = (
+        columns(qkv_sum, 0, query_width),
+        columns(qkv_sum, query_width, kv_width),
+        columns(qkv_sum, query_width + kv_width, kv_width),
+        output_sum,
+        columns(gate_up_sum, 0, hidden_units),
+        columns(gate_up_sum, hidden_units, hidden_units),
+        down_sum,
+        grad_gains,
+    )
+    masters = (w_query, key_weight, value_weight, w_output, w_gate, w_up, w_down, norm_gains)
+    moments = (
+        momentum_query,
+        key_momentum,
+        value_momentum,
+        momentum_output,
+        momentum_gate,
+        momentum_up,
+        momentum_down,
+        momentum_gains,
+    )
+    norm_scale = lax.rsqrt(jnp.float32(16 * 2 * count))
+    summed = tuple(part.astype(jnp.float32) for part in sums)
+    updates, new_moments = lion_step(masters, moments, summed, norm_scale)
+    return (layer_out, input_grad) + tuple(updates) + tuple(new_moments)
+
+
 def solution(mesh):
+    body = fast_body if dict(mesh.shape) == {"dp": 16, "ctx": 2} else general_body
     return jax.shard_map(
         body,
         mesh=mesh,

time: 1570 us -> 413 us (0.26)
  waiting for transfers between devices: 1240 us -> 115 us
  starting transfers between devices: 1.19 us -> 107 us
  matrix products: 141 us -> 38.9 us
  blocking collectives: 87.2 us -> 0 us
  local copies, waits for them, and re-layouts: 44.3 us -> 91.2 us
    reduce_scatter x7 -> x0, waiting for transfers between devices: 773 us -> none  [the longest x1 151 us: body(): lax.psum_scatter(grad_up_mat.astype(jnp.bfloat16), 'dp', scatter_dimensio...]
    all_gather x7 -> x0, waiting for transfers between devices: 454 us -> none  [the longest x1 92.8 us: body(): lax.all_gather(w_gate.astype(jnp.bfloat16), 'dp', axis=0, tiled=True)]
    ppermute x0 -> x74, waiting for transfers between devices: none -> 115 us  [the longest x57 114 us: swap(): return lax.ppermute(values, 'dp', [(i, i ^ bit) for i in range(16)])]
    ppermute x0 -> x74, starting transfers between devices: none -> 107 us  [the longest x57 48.1 us: swap(): return lax.ppermute(values, 'dp', [(i, i ^ bit) for i in range(16)])]
    unnamed x2 -> x0, blocking collectives: 70.2 us -> none
    dot_general x56 -> x5, matrix products: 69.3 us -> 7.98 us  [the longest x1 2.82 us: fast_body(): jnp.einsum('sgrqk,skgd->sqgrd', probs_low, value_low, preferred_element_t...]
    dynamic_update_slice x16 -> x44, local copies, waits for them, and re-layouts: 5.97 us -> 32.7 us  [the longest x30 27.7 us: lay_columns(): lax.dynamic_update_slice(whole, piece, (rows * (index ^ relative), 0))]
    dot_general x7 -> x4, matrix products: 25 us -> 4.88 us  [contract_rows(): lax.dot_general(left, right, (((0,), (0,)), ((), ())), preferred_element_...]
  transfers between devices with their start and end apart: 17 -> 74, of which waited for: 16 -> 29; matrix products, arithmetic and copies ran while one was open for 7% -> 37% of each run, Pallas kernels for 0% -> 0%
where the time goes in v1:
time: 413 us; the launch traced here: 408 us
  waiting for transfers between devices  115 us (28%)
  starting transfers between devices  107 us (26%)
  local copies, waits for them, and re-layouts  91.2 us (22%)
  other arithmetic  51.8 us (13%)
  matrix products  38.9 us (9%)
    ppermute x57, waiting for transfers between devices, swap(): return lax.ppermute(values, 'dp', [(i, i ^ bit) for i in range(16)])  114 us
    ppermute x57, starting transfers between devices, swap(): return lax.ppermute(values, 'dp', [(i, i ^ bit) for i in range(16)])  48.1 us
    ppermute x11, starting transfers between devices, swap_core(): return lax.ppermute(values, 'ctx', [(0, 1), (1, 0)])  45.9 us
    dynamic_update_slice x30, local copies, waits for them, and re-layouts, lay_columns(): lax.dynamic_update_slice(whole, piece, (rows * (index ^ relative), 0))  27.7 us
    dot_general x4, matrix products, contract_cols(): lax.dot_general(left, right, (((1,), (1,)), ((), ())), preferred_element_...  11.3 us
    dot_general x4, matrix products, matmul(): return jnp.dot(left, right, preferred_element_type=jnp.float32)  10.9 us
    add x8, other arithmetic, lion_step(): new_moments.append(BETA_TWO * moment_arr + (1.0 - BETA_TWO) * scaled)  10.1 us
    ppermute x4, starting transfers between devices, row_cross(): return lax.ppermute(values, ('dp', 'ctx'), pairs)  9.78 us
  transfers between devices with their start and end apart: 74, of which 29 were waited for; matrix products, arithmetic and copies ran while one was open for 37% of the time, Pallas kernels for 0%

profile of v1, /device:TPU:1, one launch (start us, length us, event | category | flops | bytes accessed | tf_op | source)
XLA Modules:
  0.0 407.5 jit_solution(5468476326040650341)
XLA Ops:
  24.1 3.7 collective-permute-start.1
  28.6 7.1 %collective-permute-done.1 = bf16[2,144]{1,0:T(2,128)(2,1)S(1)} collective-permute-done((bf16[2,144]{1,0:T(2,128)(2,1)S(1)}, bf16[2,144]{1,0:T(2,128)(2,1)S(1)}, u32[]{:S(2)}, u32[]{:S(2)}) %collective-permute-start.1) | collective-permute-done | bytes 608 | tf_op jit(solution)/shard_map/ppermute | solution.py:323
  52.3 4.5 %collective-permute-done.4 = bf16[128,1024]{1,0:T(8,128)(2,1)S(1)} collective-permute-done((bf16[128,1024]{1,0:T(8,128)(2,1)S(1)}, bf16[128,1024]{1,0:T(8,128)(2,1)S(1)}, u32[]{:S(2)}, u32[]{:S(2)}) %collective-permute-start.4) | collective-permute-done | bytes 262176 | tf_op jit(solution)/shard_map/ppermute | solution.py:323
  58.5 13.9 %collective-permute-start.36 = (bf16[2,128,1024]{2,1,0:T(8,128)(2,1)S(1)}, bf16[2,128,1024]{2,1,0:T(8,128)(2,1)S(1)}, u32[]{:S(2)}, u32[]{:S(2)}) collective-permute-start(bf16[2,128,1024]{2,1,0:T(8,128)(2,1)S(1)} %get-tuple-element.117), channel_id=1, source_target_pairs={{0,1},{1,0},{2,3},{3,2},{4,5},{5,4},{6,7},{7,6},{8,9},{9,8},{10,11... | collective-permute-start | bytes 1572872 | tf_op jit(solution)/shard_map/ppermute | solution.py:327
  77.1 7.5 %collective-permute-done.29 = bf16[96,1024]{1,0:T(8,128)(2,1)S(1)} collective-permute-done((bf16[96,1024]{1,0:T(8,128)(2,1)S(1)}, bf16[96,1024]{1,0:T(8,128)(2,1)S(1)}, u32[]{:S(2)}, u32[]{:S(2)}) %collective-permute-start.29) | collective-permute-done | bytes 196640 | tf_op jit(solution)/shard_map/ppermute | solution.py:323
  85.6 3.5 collective-permute-done.31
  90.2 4.2 %collective-permute-done.15 = bf16[128,1024]{1,0:T(8,128)(2,1)S(1)} collective-permute-done((bf16[128,1024]{1,0:T(8,128)(2,1)S(1)}, bf16[128,1024]{1,0:T(8,128)(2,1)S(1)}, u32[]{:S(2)}, u32[]{:S(2)}) %collective-permute-start.15) | collective-permute-done | bytes 262176 | tf_op jit(solution)/shard_map/ppermute | solution.py:323
  95.0 4.6 %collective-permute-done.17 = bf16[128,1024]{1,0:T(8,128)(2,1)S(1)} collective-permute-done((bf16[128,1024]{1,0:T(8,128)(2,1)S(1)}, bf16[128,1024]{1,0:T(8,128)(2,1)S(1)}, u32[]{:S(2)}, u32[]{:S(2)}) %collective-permute-start.17) | collective-permute-done | bytes 262176 | tf_op jit(solution)/shard_map/ppermute | solution.py:323
  109.8 2.9 collective-permute-done.30
  116.4 7.5 %collective-permute-done.9 = bf16[256,1024]{1,0:T(8,128)(2,1)S(1)} collective-permute-done((bf16[256,1024]{1,0:T(8,128)(2,1)S(1)}, bf16[256,1024]{1,0:T(8,128)(2,1)S(1)}, u32[]{:S(2)}, u32[]{:S(2)}) %collective-permute-start.9) | collective-permute-done | bytes 524320 | tf_op jit(solution)/shard_map/ppermute | solution.py:323
  134.7 2.8 fusion.152
  157.7 2.7 fusion.68
  162.8 3.9 fusion.149
  166.7 2.8 fusion.10
  175.8 12.9 %collective-permute-start.18 = (bf16[2,128,1024]{2,1,0:T(8,128)(2,1)}, bf16[2,128,1024]{2,1,0:T(8,128)(2,1)}, u32[]{:S(2)}, u32[]{:S(2)}) collective-permute-start(bf16[2,128,1024]{2,1,0:T(8,128)(2,1)} %fusion.57), channel_id=1, source_target_pairs={{0,1},{1,0},{2,3},{3,2},{4,5},{5,4},{6,7},{7,6},{8,9},{9,8},{10,11... | collective-permute-start | bytes 1572872 | tf_op jit(solution)/shard_map/ppermute | solution.py:327
  213.9 4.8 %collective-permute-done.20 = bf16[128,1024]{1,0:T(8,128)(2,1)S(1)} collective-permute-done((bf16[128,1024]{1,0:T(8,128)(2,1)S(1)}, bf16[128,1024]{1,0:T(8,128)(2,1)S(1)}, u32[]{:S(2)}, u32[]{:S(2)}) %collective-permute-start.20) | collective-permute-done | bytes 262176 | tf_op jit(solution)/shard_map/ppermute | solution.py:323
  222.2 3.8 fusion.153
  226.0 3.0 fusion.7
  232.5 3.7 fusion.29
  241.7 8.0 %collective-permute-done.63 = bf16[192,1024]{1,0:T(8,128)(2,1)S(1)} collective-permute-done((bf16[192,1024]{1,0:T(8,128)(2,1)S(1)}, bf16[192,1024]{1,0:T(8,128)(2,1)S(1)}, u32[]{:S(2)}, u32[]{:S(2)}) %collective-permute-start.63) | collective-permute-done | bytes 393248 | tf_op jit(solution)/shard_map/ppermute | solution.py:323
  254.4 17.4 %collective-permute-done.64 = bf16[96,1024]{1,0:T(8,128)(2,1)S(1)} collective-permute-done((bf16[96,1024]{1,0:T(8,128)(2,1)S(1)}, bf16[96,1024]{1,0:T(8,128)(2,1)S(1)}, u32[]{:S(2)}, u32[]{:S(2)}) %collective-permute-start.64) | collective-permute-done | bytes 196640 | tf_op jit(solution)/shard_map/ppermute | solution.py:323
  273.3 3.5 collective-permute-start.67
  286.6 6.1 %collective-permute-start.40 = (bf16[2,128,1024]{2,1,0:T(8,128)(2,1)S(1)}, bf16[2,128,1024]{2,1,0:T(8,128)(2,1)S(1)}, u32[]{:S(2)}, u32[]{:S(2)}) collective-permute-start(bf16[2,128,1024]{2,1,0:T(8,128)(2,1)S(1)} %get-tuple-element.114), channel_id=1, source_target_pairs={{0,1},{1,0},{2,3},{3,2},{4,5},{5,4},{6,7},{7,6},{8,9},{9,8},{10,11... | collective-permute-start | bytes 1572872 | tf_op jit(solution)/shard_map/ppermute | solution.py:327
  319.2 3.0 fusion.74
  331.4 4.9 %collective-permute-done.61 = bf16[64,1536]{1,0:T(8,128)(2,1)S(1)} collective-permute-done((bf16[64,1536]{1,0:T(8,128)(2,1)S(1)}, bf16[64,1536]{1,0:T(8,128)(2,1)S(1)}, u32[]{:S(2)}, u32[]{:S(2)}) %collective-permute-start.61) | collective-permute-done | bytes 196640 | tf_op jit(solution)/shard_map/ppermute | solution.py:323
  339.9 11.2 %collective-permute-done.51 = bf16[64,1024]{1,0:T(8,128)(2,1)S(1)} collective-permute-done((bf16[64,1024]{1,0:T(8,128)(2,1)S(1)}, bf16[64,1024]{1,0:T(8,128)(2,1)S(1)}, u32[]{:S(2)}, u32[]{:S(2)}) %collective-permute-start.51) | collective-permute-done | bytes 131104 | tf_op jit(solution)/shard_map/ppermute | solution.py:323
  351.7 3.2 collective-permute-done.53
  355.0 3.7 collective-permute-start.54
  369.4 5.1 %collective-permute-start.69 = (bf16[16,144]{1,0:T(8,128)(2,1)S(1)}, bf16[16,144]{1,0:T(8,128)(2,1)S(1)}, u32[]{:S(2)}, u32[]{:S(2)}) collective-permute-start(bf16[16,144]{1,0:T(8,128)(2,1)S(1)} %convert_element_type.583), channel_id=1, source_target_pairs={{0,1},{1,0},{2,3},{3,2},{4,5},{5,4},{6,7},{7,6},{8,9},{9,8},{10,11... | collective-permute-start | bytes 13832 | tf_op jit(solution)/shard_map/ppermute | solution.py:327
  387.8 6.8 %collective-permute-done.47 = bf16[128,1024]{1,0:T(8,128)(2,1)S(1)} collective-permute-done((bf16[128,1024]{1,0:T(8,128)(2,1)S(1)}, bf16[128,1024]{1,0:T(8,128)(2,1)S(1)}, u32[]{:S(2)}, u32[]{:S(2)}) %collective-permute-start.47) | collective-permute-done | bytes 262176 | tf_op jit(solution)/shard_map/ppermute | solution.py:323
  395.3 3.2 collective-permute-done.48
  398.6 2.6 collective-permute-start.49
  (587 shorter events, 225.4 us)
Async XLA Ops:
  3.4 41.9 %collective-permute-start.6 = (bf16[64,1024]{1,0:T(8,128)(2,1)}, bf16[64,1024]{1,0:T(8,128)(2,1)S(1)}, u32[]{:S(2)}, u32[]{:S(2)}) collective-permute-start(bf16[64,1024]{1,0:T(8,128)(2,1)} %pad_maximum_fusion.50), channel_id=1, source_target_pairs={{0,8},{2,10},{4,12},{6,14},{8,0},{10,2},{12,4},{14,6},{16,24},{18,... | collective-permute-start | bytes 393224 | tf_op jit(solution)/shard_map/ppermute | solution.py:323
  6.3 17.8 %collective-permute-start = (bf16[1,144]{1,0:T(2,128)(2,1)S(1)}, bf16[1,144]{1,0:T(2,128)(2,1)S(1)}, u32[]{:S(2)}, u32[]{:S(2)}) collective-permute-start(bf16[1,144]{1,0:T(2,128)(2,1)S(1)} %broadcast_in_dim.45), channel_id=1, source_target_pairs={{0,8},{2,10},{4,12},{6,14},{8,0},{10,2},{12,4},{14,6},{16,24},{18,... | collective-permute-start | bytes 872 | tf_op jit(solution)/shard_map/ppermute | solution.py:323
  6.3 15.1 %collective-permute-start.12 = (s32[1,4]{1,0:T(1,128)}, s32[1,4]{1,0:T(1,128)S(1)}, u32[]{:S(2)}, u32[]{:S(2)}) collective-permute-start(s32[1,4]{1,0:T(1,128)} %param.22), channel_id=1, source_target_pairs={{0,8},{2,10},{4,12},{6,14},{8,0},{10,2},{12,4},{14,6},{16,24},{18,... | collective-permute-start | bytes 56 | tf_op jit(solution)/shard_map/ppermute | solution.py:323
  9.5 37.5 %collective-permute-start.13 = (bf16[128,1024]{1,0:T(8,128)(2,1)}, bf16[128,1024]{1,0:T(8,128)(2,1)}, u32[]{:S(2)}, u32[]{:S(2)}) collective-permute-start(bf16[128,1024]{1,0:T(8,128)(2,1)} %convert_element_type.470), channel_id=1, source_target_pairs={{0,16},{2,18},{4,20},{6,22},{8,24},{10,26},{12,28},{14,30},{17,1},... | collective-permute-start | bytes 786440 | tf_op jit(solution)/shard_map/ppermute | solution.py:340
  12.8 34.1 %collective-permute-start.22 = (bf16[64,1536]{1,0:T(8,128)(2,1)}, bf16[64,1536]{1,0:T(8,128)(2,1)S(1)}, u32[]{:S(2)}, u32[]{:S(2)}) collective-permute-start(bf16[64,1536]{1,0:T(8,128)(2,1)} %pad_maximum_fusion.49), channel_id=1, source_target_pairs={{0,8},{2,10},{4,12},{6,14},{8,0},{10,2},{12,4},{14,6},{16,24},{18,... | collective-permute-start | bytes 589832 | tf_op jit(solution)/shard_map/ppermute | solution.py:323
  21.3 52.0 %collective-permute-start.28 = (bf16[192,1024]{1,0:T(8,128)(2,1)S(1)}, bf16[192,1024]{1,0:T(8,128)(2,1)S(1)}, u32[]{:S(2)}, u32[]{:S(2)}) collective-permute-start(bf16[192,1024]{1,0:T(8,128)(2,1)S(1)} %convert_element_type.481), channel_id=1, source_target_pairs={{0,16},{2,18},{4,20},{6,22},{8,24},{10,26},{12,28},{14,30},{17,1},... | collective-permute-start | bytes 1179656 | tf_op jit(solution)/shard_map/ppermute | solution.py:340
  47.0 29.3 %collective-permute-start.23 = (bf16[128,1536]{1,0:T(8,128)(2,1)S(1)}, bf16[128,1536]{1,0:T(8,128)(2,1)S(1)}, u32[]{:S(2)}, u32[]{:S(2)}) collective-permute-start(bf16[128,1536]{1,0:T(8,128)(2,1)S(1)} %pad_maximum_fusion.22), channel_id=1, source_target_pairs={{0,16},{2,18},{4,20},{6,22},{8,24},{10,26},{12,28},{14,30},{16,0},... | collective-permute-start | bytes 1179656 | tf_op jit(solution)/shard_map/ppermute | solution.py:323
  50.6 21.9 %collective-permute-start.16 = (bf16[64,1024]{1,0:T(8,128)(2,1)S(1)}, bf16[64,1024]{1,0:T(8,128)(2,1)S(1)}, u32[]{:S(2)}, u32[]{:S(2)}) collective-permute-start(bf16[64,1024]{1,0:T(8,128)(2,1)S(1)} %get-tuple-element.161), channel_id=1, source_target_pairs={{0,2},{2,0},{4,6},{6,4},{8,10},{10,8},{12,14},{14,12},{16,18},{18,... | collective-permute-start | bytes 393224 | tf_op jit(solution)/shard_map/ppermute | solution.py:323
  56.8 15.8 %collective-permute-start.14 = (bf16[64,1024]{1,0:T(8,128)(2,1)S(1)}, bf16[64,1024]{1,0:T(8,128)(2,1)S(1)}, u32[]{:S(2)}, u32[]{:S(2)}) collective-permute-start(bf16[64,1024]{1,0:T(8,128)(2,1)S(1)} %get-tuple-element.163), channel_id=1, source_target_pairs={{0,4},{2,6},{4,0},{6,2},{8,12},{10,14},{12,8},{14,10},{16,20},{18,... | collective-permute-start | bytes 393224 | tf_op jit(solution)/shard_map/ppermute | solution.py:323
  58.5 43.5 %collective-permute-start.36 = (bf16[2,128,1024]{2,1,0:T(8,128)(2,1)S(1)}, bf16[2,128,1024]{2,1,0:T(8,128)(2,1)S(1)}, u32[]{:S(2)}, u32[]{:S(2)}) collective-permute-start(bf16[2,128,1024]{2,1,0:T(8,128)(2,1)S(1)} %get-tuple-element.117), channel_id=1, source_target_pairs={{0,1},{1,0},{2,3},{3,2},{4,5},{5,4},{6,7},{7,6},{8,9},{9,8},{10,11... | collective-permute-start | bytes 1572872 | tf_op jit(solution)/shard_map/ppermute | solution.py:327
  72.5 31.6 %collective-permute-start.5 = (bf16[2,128,1024]{2,1,0:T(8,128)(2,1)S(1)}, bf16[2,128,1024]{2,1,0:T(8,128)(2,1)S(1)}, u32[]{:S(2)}, u32[]{:S(2)}) collective-permute-start(bf16[2,128,1024]{2,1,0:T(8,128)(2,1)S(1)} %get-tuple-element.125), channel_id=1, source_target_pairs={{0,1},{1,0},{2,3},{3,2},{4,5},{5,4},{6,7},{7,6},{8,9},{9,8},{10,11... | collective-permute-start | bytes 1572872 | tf_op jit(solution)/shard_map/ppermute | solution.py:327
  72.7 27.9 %collective-permute-start.10 = (bf16[128,1024]{1,0:T(8,128)(2,1)S(1)}, bf16[128,1024]{1,0:T(8,128)(2,1)S(1)}, u32[]{:S(2)}, u32[]{:S(2)}) collective-permute-start(bf16[128,1024]{1,0:T(8,128)(2,1)S(1)} %pad_maximum_fusion.38), channel_id=1, source_target_pairs={{0,2},{2,0},{4,6},{6,4},{8,10},{10,8},{12,14},{14,12},{16,18},{18,... | collective-permute-start | bytes 786440 | tf_op jit(solution)/shard_map/ppermute | solution.py:323
  73.3 28.1 %collective-permute-start.8 = (bf16[128,1024]{1,0:T(8,128)(2,1)S(1)}, bf16[128,1024]{1,0:T(8,128)(2,1)S(1)}, u32[]{:S(2)}, u32[]{:S(2)}) collective-permute-start(bf16[128,1024]{1,0:T(8,128)(2,1)S(1)} %pad_maximum_fusion.37), channel_id=1, source_target_pairs={{0,4},{2,6},{4,0},{6,2},{8,12},{10,14},{12,8},{14,10},{16,20},{18,... | collective-permute-start | bytes 786440 | tf_op jit(solution)/shard_map/ppermute | solution.py:323
  104.1 22.0 %collective-permute-start.11 = (bf16[256,1024]{1,0:T(8,128)(2,1)S(1)}, bf16[256,1024]{1,0:T(8,128)(2,1)S(1)}, u32[]{:S(2)}, u32[]{:S(2)}) collective-permute-start(bf16[256,1024]{1,0:T(8,128)(2,1)S(1)} %pad_maximum_fusion.14), channel_id=1, source_target_pairs={{0,4},{2,6},{4,0},{6,2},{8,12},{10,14},{12,8},{14,10},{16,20},{18,... | collective-permute-start | bytes 1572872 | tf_op jit(solution)/shard_map/ppermute | solution.py:323
  106.2 17.7 %collective-permute-start.9 = (bf16[256,1024]{1,0:T(8,128)(2,1)S(1)}, bf16[256,1024]{1,0:T(8,128)(2,1)S(1)}, u32[]{:S(2)}, u32[]{:S(2)}) collective-permute-start(bf16[256,1024]{1,0:T(8,128)(2,1)S(1)} %pad_maximum_fusion.13), channel_id=1, source_target_pairs={{0,2},{2,0},{4,6},{6,4},{8,10},{10,8},{12,14},{14,12},{16,18},{18,... | collective-permute-start | bytes 1572872 | tf_op jit(solution)/shard_map/ppermute | solution.py:323
  108.2 90.7 %collective-permute-start.27 = (bf16[256,1536]{1,0:T(8,128)(2,1)}, bf16[256,1536]{1,0:T(8,128)(2,1)}, u32[]{:S(2)}, u32[]{:S(2)}) collective-permute-start(bf16[256,1536]{1,0:T(8,128)(2,1)} %pad_maximum_fusion.9), channel_id=1, source_target_pairs={{0,4},{2,6},{4,0},{6,2},{8,12},{10,14},{12,8},{14,10},{16,20},{18,... | collective-permute-start | bytes 2359304 | tf_op jit(solution)/shard_map/ppermute | solution.py:323
  112.7 83.8 %collective-permute-start.25 = (bf16[256,1536]{1,0:T(8,128)(2,1)}, bf16[256,1536]{1,0:T(8,128)(2,1)}, u32[]{:S(2)}, u32[]{:S(2)}) collective-permute-start(bf16[256,1536]{1,0:T(8,128)(2,1)} %pad_maximum_fusion.8), channel_id=1, source_target_pairs={{0,2},{2,0},{4,6},{6,4},{8,10},{10,8},{12,14},{14,12},{16,18},{18,... | collective-permute-start | bytes 2359304 | tf_op jit(solution)/shard_map/ppermute | solution.py:323
  175.8 19.0 %collective-permute-start.18 = (bf16[2,128,1024]{2,1,0:T(8,128)(2,1)}, bf16[2,128,1024]{2,1,0:T(8,128)(2,1)}, u32[]{:S(2)}, u32[]{:S(2)}) collective-permute-start(bf16[2,128,1024]{2,1,0:T(8,128)(2,1)} %fusion.57), channel_id=1, source_target_pairs={{0,1},{1,0},{2,3},{3,2},{4,5},{5,4},{6,7},{7,6},{8,9},{9,8},{10,11... | collective-permute-start | bytes 1572872 | tf_op jit(solution)/shard_map/ppermute | solution.py:327
  196.4 14.0 %collective-permute-start.19 = (bf16[128,1024]{1,0:T(8,128)(2,1)S(1)}, bf16[128,1024]{1,0:T(8,128)(2,1)S(1)}, u32[]{:S(2)}, u32[]{:S(2)}) collective-permute-start(bf16[128,1024]{1,0:T(8,128)(2,1)S(1)} %fusion.79), channel_id=1, source_target_pairs={{0,8},{2,10},{4,12},{6,14},{8,0},{10,2},{12,4},{14,6},{16,24},{18,... | collective-permute-start | bytes 786440 | tf_op jit(solution)/shard_map/ppermute | solution.py:323
  238.3 14.5 %collective-permute-start.37 = (bf16[2,128,1024]{2,1,0:T(8,128)(2,1)S(1)}, bf16[2,128,1024]{2,1,0:T(8,128)(2,1)S(1)}, u32[]{:S(2)}, u32[]{:S(2)}) collective-permute-start(bf16[2,128,1024]{2,1,0:T(8,128)(2,1)S(1)} %fusion.59), channel_id=1, source_target_pairs={{0,1},{1,0},{2,3},{3,2},{4,5},{5,4},{6,7},{7,6},{8,9},{9,8},{10,11... | collective-permute-start | bytes 1572872 | tf_op jit(solution)/shard_map/ppermute | solution.py:327
  241.1 39.1 %collective-permute-start.56 = (bf16[256,1536]{1,0:T(8,128)(2,1)S(1)}, bf16[256,1536]{1,0:T(8,128)(2,1)S(1)}, u32[]{:S(2)}, u32[]{:S(2)}) collective-permute-start(bf16[256,1536]{1,0:T(8,128)(2,1)S(1)} %pad_maximum_fusion.10), channel_id=1, source_target_pairs={{0,2},{2,0},{4,6},{6,4},{8,10},{10,8},{12,14},{14,12},{16,18},{18,... | collective-permute-start | bytes 2359304 | tf_op jit(solution)/shard_map/ppermute | solution.py:323
  249.8 31.2 %collective-permute-start.58 = (bf16[256,1536]{1,0:T(8,128)(2,1)S(1)}, bf16[256,1536]{1,0:T(8,128)(2,1)S(1)}, u32[]{:S(2)}, u32[]{:S(2)}) collective-permute-start(bf16[256,1536]{1,0:T(8,128)(2,1)S(1)} %pad_maximum_fusion.11), channel_id=1, source_target_pairs={{0,4},{2,6},{4,0},{6,2},{8,12},{10,14},{12,8},{14,10},{16,20},{18,... | collective-permute-start | bytes 2359304 | tf_op jit(solution)/shard_map/ppermute | solution.py:323
  250.6 21.2 %collective-permute-start.64 = (bf16[96,1024]{1,0:T(8,128)(2,1)S(1)}, bf16[96,1024]{1,0:T(8,128)(2,1)S(1)}, u32[]{:S(2)}, u32[]{:S(2)}) collective-permute-start(bf16[96,1024]{1,0:T(8,128)(2,1)S(1)} %slice.645), channel_id=1, source_target_pairs={{0,4},{2,6},{4,0},{6,2},{8,12},{10,14},{12,8},{14,10},{16,20},{18,... | collective-permute-start | bytes 589832 | tf_op jit(solution)/shard_map/ppermute | solution.py:323
  251.7 21.6 %collective-permute-start.66 = (bf16[96,1024]{1,0:T(8,128)(2,1)S(1)}, bf16[96,1024]{1,0:T(8,128)(2,1)S(1)}, u32[]{:S(2)}, u32[]{:S(2)}) collective-permute-start(bf16[96,1024]{1,0:T(8,128)(2,1)S(1)} %slice.647), channel_id=1, source_target_pairs={{0,2},{2,0},{4,6},{6,4},{8,10},{10,8},{12,14},{14,12},{16,18},{18,... | collective-permute-start | bytes 589832 | tf_op jit(solution)/shard_map/ppermute | solution.py:323
  252.8 24.8 %collective-permute-start.34 = (bf16[128,1024]{1,0:T(8,128)(2,1)S(1)}, bf16[128,1024]{1,0:T(8,128)(2,1)S(1)}, u32[]{:S(2)}, u32[]{:S(2)}) collective-permute-start(bf16[128,1024]{1,0:T(8,128)(2,1)S(1)} %fusion.81), channel_id=1, source_target_pairs={{0,8},{2,10},{4,12},{6,14},{8,0},{10,2},{12,4},{14,6},{16,24},{18,... | collective-permute-start | bytes 786440 | tf_op jit(solution)/shard_map/ppermute | solution.py:323
  295.1 33.5 %collective-permute-start.60 = (bf16[128,1536]{1,0:T(8,128)(2,1)}, bf16[128,1536]{1,0:T(8,128)(2,1)}, u32[]{:S(2)}, u32[]{:S(2)}) collective-permute-start(bf16[128,1536]{1,0:T(8,128)(2,1)} %pad_maximum_fusion.28), channel_id=1, source_target_pairs={{0,16},{2,18},{4,20},{6,22},{8,24},{10,26},{12,28},{14,30},{16,0},... | collective-permute-start | bytes 1179656 | tf_op jit(solution)/shard_map/ppermute | solution.py:323
  322.3 36.4 %collective-permute-start.41 = (bf16[2,128,1024]{2,1,0:T(8,128)(2,1)S(1)}, bf16[2,128,1024]{2,1,0:T(8,128)(2,1)S(1)}, u32[]{:S(2)}, u32[]{:S(2)}) collective-permute-start(bf16[2,128,1024]{2,1,0:T(8,128)(2,1)S(1)} %fusion.60), channel_id=1, source_target_pairs={{0,1},{1,0},{2,3},{3,2},{4,5},{5,4},{6,7},{7,6},{8,9},{9,8},{10,11... | collective-permute-start | bytes 1572872 | tf_op jit(solution)/shard_map/ppermute | solution.py:327
  330.7 28.9 %collective-permute-start.43 = (bf16[256,1024]{1,0:T(8,128)(2,1)S(1)}, bf16[256,1024]{1,0:T(8,128)(2,1)S(1)}, u32[]{:S(2)}, u32[]{:S(2)}) collective-permute-start(bf16[256,1024]{1,0:T(8,128)(2,1)S(1)} %pad_maximum_fusion.18), channel_id=1, source_target_pairs={{0,2},{2,0},{4,6},{6,4},{8,10},{10,8},{12,14},{14,12},{16,18},{18,... | collective-permute-start | bytes 1572872 | tf_op jit(solution)/shard_map/ppermute | solution.py:323
  336.3 24.6 %collective-permute-start.45 = (bf16[256,1024]{1,0:T(8,128)(2,1)S(1)}, bf16[256,1024]{1,0:T(8,128)(2,1)S(1)}, u32[]{:S(2)}, u32[]{:S(2)}) collective-permute-start(bf16[256,1024]{1,0:T(8,128)(2,1)S(1)} %pad_maximum_fusion.19), channel_id=1, source_target_pairs={{0,4},{2,6},{4,0},{6,2},{8,12},{10,14},{12,8},{14,10},{16,20},{18,... | collective-permute-start | bytes 1572872 | tf_op jit(solution)/shard_map/ppermute | solution.py:323
  337.1 25.4 %collective-permute-start.62 = (bf16[2,64,1536]{2,1,0:T(8,128)(2,1)S(1)}, bf16[2,64,1536]{2,1,0:T(8,128)(2,1)S(1)}, u32[]{:S(2)}, u32[]{:S(2)}) collective-permute-start(bf16[2,64,1536]{2,1,0:T(8,128)(2,1)S(1)} %pad_maximum_fusion.29), channel_id=1, source_target_pairs={{0,1},{1,0},{2,3},{3,2},{4,5},{5,4},{6,7},{7,6},{8,9},{9,8},{10,11... | collective-permute-start | bytes 1179656 | tf_op jit(solution)/shard_map/ppermute | solution.py:327
  366.9 34.3 %collective-permute-start.55 = (bf16[128,1024]{1,0:T(8,128)(2,1)}, bf16[128,1024]{1,0:T(8,128)(2,1)}, u32[]{:S(2)}, u32[]{:S(2)}) collective-permute-start(bf16[128,1024]{1,0:T(8,128)(2,1)} %add_convert_fusion.10), channel_id=1, source_target_pairs={{0,1},{2,3},{4,5},{6,7},{8,9},{10,11},{12,13},{14,15},{17,16},{19,... | collective-permute-start | bytes 786440 | tf_op jit(solution)/shard_map/ppermute | solution.py:443
  380.5 14.1 %collective-permute-start.47 = (bf16[128,1024]{1,0:T(8,128)(2,1)S(1)}, bf16[128,1024]{1,0:T(8,128)(2,1)S(1)}, u32[]{:S(2)}, u32[]{:S(2)}) collective-permute-start(bf16[128,1024]{1,0:T(8,128)(2,1)S(1)} %pad_maximum_fusion.43), channel_id=1, source_target_pairs={{0,16},{2,18},{4,20},{6,22},{8,24},{10,26},{12,28},{14,30},{16,0},... | collective-permute-start | bytes 786440 | tf_op jit(solution)/shard_map/ppermute | solution.py:323
  (124 other events, 1204.5 us)

commit v2 on v0

--- a/solution.py
+++ b/solution.py
@@ -1,6 +1,8 @@
 import jax
 import jax.numpy as jnp
 from jax import lax
+from jax.experimental import pallas as pl
+from jax.experimental.pallas import tpu as pltpu
 from jax.sharding import PartitionSpec as P
 
 EPSILON = 1e-06
@@ -123,7 +125,7 @@
     return (updates, new_moments)
 
 
-def body(
+def general_body(
     hidden_in,
     cotangent,
     block_order,
@@ -315,7 +317,633 @@
     return (layer_out, input_grad) + tuple(updates) + tuple(new_moments)
 
 
+X_BIT, Y_BIT, P_BIT, H_BIT = 1, 2, 4, 8
+LOW = jnp.bfloat16
+WIDE = jnp.float32
+VMEM_BYTES = 48 * 1024 * 1024
+COLUMN_GROUPS = ((0, Y_BIT), (X_BIT, Y_BIT), (P_BIT, X_BIT), (P_BIT + Y_BIT, X_BIT))
+ROW_GROUPS = ((0, Y_BIT, 0), (X_BIT, Y_BIT, 0), (0, X_BIT, 1), (Y_BIT, X_BIT, 1))
+
+
+def swap(values, bit):
+    return lax.ppermute(values, "dp", [(i, i ^ bit) for i in range(16)])
+
+
+def swap_core(values):
+    return lax.ppermute(values, "ctx", [(0, 1), (1, 0)])
+
+
+def h_of(index):
+    return (index // H_BIT) % 2
+
+
+def row_cross(values, to_owner):
+    pairs = []
+    for index in range(16):
+        for core in range(2):
+            if (core == h_of(index)) != to_owner:
+                pairs.append((index * 2 + core, (index ^ H_BIT) * 2 + core))
+    return lax.ppermute(values, ("dp", "ctx"), pairs)
+
+
+def gather_column_slices(own, give):
+    rows = own.shape[0]
+    got = swap(give, P_BIT)
+    far = swap(jnp.concatenate([own, got]), H_BIT)
+    first = jnp.concatenate([own, far[:rows]])
+    second = jnp.concatenate([got, far[rows:]])
+    first = jnp.concatenate([first, swap(first, Y_BIT)])
+    second = jnp.concatenate([second, swap(second, X_BIT)])
+    return first, swap(first, X_BIT), second, swap(second, Y_BIT)
+
+
+def gather_row_slices(own, mine):
+    rows = own.shape[0] // 2
+    held = jnp.where(mine, own, row_cross(own, False))
+    first, second = held[:rows], held[rows:]
+    first = jnp.concatenate([first, swap(first, Y_BIT)])
+    second = jnp.concatenate([second, swap(second, X_BIT)])
+    return first, swap(first, X_BIT), second, swap(second, Y_BIT)
+
+
+def add_low(left, right):
+    return (left.astype(WIDE) + right.astype(WIDE)).astype(LOW)
+
+
+def scatter_column_slices(keep_one, send_one, keep_two, send_two):
+    rows = keep_one.shape[0] // 4
+    first = add_low(keep_one, swap(send_one, X_BIT))
+    second = add_low(keep_two, swap(send_two, Y_BIT))
+    first = add_low(first[: 2 * rows], swap(first[2 * rows :], Y_BIT))
+    second = add_low(second[: 2 * rows], swap(second[2 * rows :], X_BIT))
+    near = jnp.concatenate([first[:rows], second[:rows]])
+    far = jnp.concatenate([first[rows:], second[rows:]])
+    near = add_low(near, swap(far, H_BIT))
+    return near[:rows], swap(near[rows:], P_BIT)
+
+
+def scatter_row_slices(keep_one, send_one, keep_two, send_two, mine):
+    rows = keep_one.shape[0] // 2
+    first = add_low(keep_one, swap(send_one, X_BIT))
+    second = add_low(keep_two, swap(send_two, Y_BIT))
+    first = add_low(first[:rows], swap(first[rows:], Y_BIT))
+    second = add_low(second[:rows], swap(second[rows:], X_BIT))
+    held = jnp.concatenate([first, second])
+    summed = add_low(held, row_cross(held, True))
+    pairs = [(i * 2 + h_of(i), i * 2 + 1 - h_of(i)) for i in range(16)]
+    return jnp.where(mine, summed, lax.ppermute(summed, ("dp", "ctx"), pairs))
+
+
+def join_column_slices(own, partner, p_index, core):
+    low_pair = jnp.where(p_index == 0, own, partner)
+    high_pair = jnp.where(p_index == 0, partner, own)
+    pair = jnp.stack([low_pair, high_pair])
+    other = swap_core(pair)
+    lower = jnp.where(core == 0, pair, other)
+    upper = jnp.where(core == 0, other, pair)
+    return [lower[0], lower[1], upper[0], upper[1]]
+
+
+def gather_tokens(own):
+    same = jnp.stack([own, swap(own, P_BIT)])
+    return same, swap_core(same)
+
+
+def sum_tokens(same, sibling):
+    pair = same.astype(WIDE) + swap_core(sibling).astype(WIDE)
+    return pair[0] + swap(pair[1].astype(LOW), P_BIT).astype(WIDE)
+
+
+VM = pl.BlockSpec(memory_space=pltpu.VMEM)
+SM = pl.BlockSpec(memory_space=pltpu.SMEM)
+HB = pl.BlockSpec(memory_space=pl.ANY)
+
+
+def call(kernel, in_specs, outs, out_specs, scratch, flops, moved):
+    return pl.pallas_call(
+        kernel,
+        in_specs=in_specs,
+        out_specs=out_specs,
+        out_shape=[jax.ShapeDtypeStruct(shape, dtype) for shape, dtype in outs],
+        scratch_shapes=scratch,
+        compiler_params=pltpu.CompilerParams(vmem_limit_bytes=VMEM_BYTES),
+        cost_estimate=pl.CostEstimate(flops=flops, bytes_accessed=moved, transcendentals=0),
+    )
+
+
+def column_copies(index, parts, whole, sems, outward):
+    copies = []
+    rows = whole.shape[0] // 16
+    for part, (base, outer) in zip(parts, COLUMN_GROUPS):
+        for place in range(4):
+            relative = base + (place // 2) * outer + (place % 2) * H_BIT
+            start = pl.multiple_of((index ^ relative) * rows, rows)
+            block = part.at[pl.ds(place * rows, rows)]
+            inside = whole.at[pl.ds(start, rows)]
+            ends = (inside, block) if outward else (block, inside)
+            copies.append(pltpu.make_async_copy(*ends, sems.at[len(copies)]))
+    return copies
+
+
+def row_copies(index, parts, whole, sems, outward):
+    copies = []
+    rows = whole.shape[0] // 8
+    for part, (base, outer, half) in zip(parts, ROW_GROUPS):
+        for place in range(2):
+            relative = base + place * outer
+            start = pl.multiple_of((((index ^ relative) % 4) * 2 + half) * rows, rows)
+            block = part.at[pl.ds(place * rows, rows)]
+            inside = whole.at[pl.ds(start, rows)]
+            ends = (inside, block) if outward else (block, inside)
+            copies.append(pltpu.make_async_copy(*ends, sems.at[len(copies)]))
+    return copies
+
+
+def start_all(copies):
+    for copy in copies:
+        copy.start()
+
+
+def wait_all(copies):
+    for copy in copies:
+        copy.wait()
+
+
+def load_tokens(same, sibling):
+    return jnp.concatenate([same[0], sibling[0], same[1], sibling[1]])
+
+
+def store_tokens(values, same, sibling):
+    count = same.shape[1]
+    for sequence in range(2):
+        at = 2 * count * sequence
+        same[sequence] = values[at : at + count].astype(same.dtype)
+        sibling[sequence] = values[at + count : at + 2 * count].astype(sibling.dtype)
+
+
+def place_of(scalars, sequence, at):
+    block = jnp.where(
+        at < 128,
+        jnp.where(at < 64, scalars[1 + 4 * sequence], scalars[2 + 4 * sequence]),
+        jnp.where(at < 192, scalars[3 + 4 * sequence], scalars[4 + 4 * sequence]),
+    )
+    return block * 64 + at % 64
+
+
+def allowed_of(scalars, sequence):
+    rows = place_of(scalars, sequence, lax.broadcasted_iota(jnp.int32, (256, 1), 0))
+    cols = place_of(scalars, sequence, lax.broadcasted_iota(jnp.int32, (1, 256), 1))
+    return rows >= cols
+
+
+def fill_tables(scalars, cosine, sine, cos_rows, sin_rows):
+    for slot in range(8):
+        start = pl.multiple_of(scalars[1 + slot] * 64, 64)
+        cos_rows[slot * 64 : slot * 64 + 64] = cosine[pl.ds(start, 64)]
+        sin_rows[slot * 64 : slot * 64 + 64] = sine[pl.ds(start, 64)]
+
+
+def attend_kernel(
+    scalars, same, sibling, part_a, part_b, part_c, part_d, cosine, sine, gains,
+    mixture, pre, rotated, values_out, log_total, whole, cos_rows, sin_rows, sems,
+):
+    copies = column_copies(scalars[0], (part_a, part_b, part_c, part_d), whole, sems, False)
+    start_all(copies)
+    fill_tables(scalars, cosine, sine, cos_rows, sin_rows)
+    tokens = load_tokens(same, sibling)
+    wait_all(copies)
+    projected = matmul(tokens, whole[...])
+    pre[...] = projected[:, :768]
+    values_out[...] = projected[:, 768:].astype(LOW)
+    for head in range(6):
+        cut = slice(head * 128, head * 128 + 128)
+        raw = pre[:, cut]
+        gain = gains[0:1] if head < 4 else gains[1:2]
+        scale = lax.rsqrt(jnp.mean(raw * raw, axis=-1, keepdims=True) + EPSILON)
+        unit = raw * scale * gain
+        turned = pltpu.roll(unit, 64, 1)
+        rotated[:, cut] = (unit * cos_rows[...] + turned * sin_rows[...]).astype(LOW)
+    for sequence in range(2):
+        rows = slice(sequence * 256, sequence * 256 + 256)
+        allowed = allowed_of(scalars, sequence)
+        tops = []
+        for head in range(4):
+            group = head // 2
+            queries = rotated[rows, head * 128 : head * 128 + 128]
+            keys = rotated[rows, 512 + group * 128 : 640 + group * 128]
+            scores = jnp.where(allowed, contract_cols(queries, keys) * (128**-0.5), -1e30)
+            top = jnp.max(scores, axis=-1, keepdims=True)
+            weights = jnp.exp(scores - top)
+            total = jnp.sum(weights, axis=-1, keepdims=True)
+            probs = (weights / total).astype(LOW)
+            mixed = matmul(probs, values_out[rows, group * 128 : group * 128 + 128])
+            mixture[rows, head * 128 : head * 128 + 128] = mixed.astype(LOW)
+            tops.append(jnp.broadcast_to(top + jnp.log(total), (256, 128)))
+        lane = lax.broadcasted_iota(jnp.int32, (256, 128), 1)
+        log_total[rows] = jnp.where(
+            lane < 2, jnp.where(lane < 1, tops[0], tops[1]), jnp.where(lane < 3, tops[2], tops[3])
+        )
+
+
+def attend(scalars, tokens, parts, tables, gains):
+    return call(
+        attend_kernel,
+        [SM, VM, VM, HB, HB, HB, HB, VM, VM, VM],
+        [((512, 512), LOW), ((512, 768), WIDE), ((512, 768), LOW), ((512, 256), LOW), ((512, 128), WIDE)],
+        [VM] * 5,
+        [
+            pltpu.VMEM((1024, 1024), LOW),
+            pltpu.VMEM((512, 128), WIDE),
+            pltpu.VMEM((512, 128), WIDE),
+            pltpu.SemaphoreType.DMA((16,)),
+        ],
+        2 * 10**9,
+        8 * 10**6,
+    )(scalars, *tokens, *parts, *tables, gains)
+
+
+def output_kernel(scalars, mixture, part_a, part_b, part_c, part_d, same, sibling, whole, sems):
+    copies = row_copies(scalars[0], (part_a, part_b, part_c, part_d), whole, sems, False)
+    start_all(copies)
+    wait_all(copies)
+    store_tokens(matmul(mixture[...], whole[...]), same, sibling)
+
+
+def row_product(scalars, left, parts):
+    depth = left.shape[1]
+    return call(
+        output_kernel,
+        [SM, VM, HB, HB, HB, HB],
+        [((2, 128, 1024), LOW)] * 2,
+        [VM] * 2,
+        [pltpu.VMEM((depth, 1024), LOW), pltpu.SemaphoreType.DMA((8,))],
+        2 * 512 * 1024 * depth,
+        4 * 10**6,
+    )(scalars, left, *parts)
+
+
+def gate_kernel(
+    scalars, same, sibling, part_a, part_b, part_c, part_d, gate_up, active, whole, sems
+):
+    copies = column_copies(scalars[0], (part_a, part_b, part_c, part_d), whole, sems, False)
+    start_all(copies)
+    tokens = load_tokens(same, sibling)
+    wait_all(copies)
+    for at in range(0, 768, 256):
+        gate = matmul(tokens, whole[:, at : at + 256])
+        upward = matmul(tokens, whole[:, 768 + at : 1024 + at])
+        gate_up[:, at : at + 256] = gate
+        gate_up[:, 768 + at : 1024 + at] = upward
+        active[:, at : at + 256] = (gate * jax.nn.sigmoid(gate) * upward).astype(LOW)
+
+
+def gate_product(scalars, tokens, parts):
+    return call(
+        gate_kernel,
+        [SM, VM, VM, HB, HB, HB, HB],
+        [((512, 1536), WIDE), ((512, 768), LOW)],
+        [VM] * 2,
+        [pltpu.VMEM((1024, 1536), LOW), pltpu.SemaphoreType.DMA((16,))],
+        2 * 512 * 1024 * 1536,
+        10 * 10**6,
+    )(scalars, *tokens, *parts)
+
+
+def swiglu_back_kernel(
+    scalars, same, sibling, gate_up, row_a, row_b, row_c, row_d, col_a, col_b, col_c, col_d,
+    grad_gate_up, grad_same, grad_sibling, down, both, row_sems, col_sems,
+):
+    down_copies = row_copies(scalars[0], (row_a, row_b, row_c, row_d), down, row_sems, False)
+    both_copies = column_copies(scalars[0], (col_a, col_b, col_c, col_d), both, col_sems, False)
+    start_all(down_copies)
+    start_all(both_copies)
+    grad_out = load_tokens(same, sibling)
+    wait_all(down_copies)
+    for at in range(0, 768, 256):
+        grad_active = contract_cols(grad_out, down[at : at + 256])
+        gate = gate_up[:, at : at + 256]
+        upward = gate_up[:, 768 + at : 1024 + at]
+        sigmoid = jax.nn.sigmoid(gate)
+        grad_gate_up[:, at : at + 256] = (
+            grad_active * upward * (sigmoid * (1.0 + gate * (1.0 - sigmoid)))
+        ).astype(LOW)
+        grad_gate_up[:, 768 + at : 1024 + at] = (grad_active * (gate * sigmoid)).astype(LOW)
+    wait_all(both_copies)
+    store_tokens(contract_cols(grad_gate_up[...], both[...]), grad_same, grad_sibling)
+
+
+def swiglu_back(scalars, grad_out, gate_up, down_parts, gate_up_parts):
+    return call(
+        swiglu_back_kernel,
+        [SM, VM, VM, VM] + [HB] * 8,
+        [((512, 1536), LOW), ((2, 128, 1024), LOW), ((2, 128, 1024), LOW)],
+        [VM] * 3,
+        [
+            pltpu.VMEM((768, 1024), LOW),
+            pltpu.VMEM((1024, 1536), LOW),
+            pltpu.SemaphoreType.DMA((8,)),
+            pltpu.SemaphoreType.DMA((16,)),
+        ],
+        2 * 512 * 1024 * 2304,
+        12 * 10**6,
+    )(scalars, *grad_out, gate_up, *down_parts, *gate_up_parts)
+
+
+def attend_back_kernel(
+    scalars, same, sibling, part_a, part_b, part_c, part_d, pre, rotated, values, log_total,
+    cosine, sine, gains, grad_all, grad_gains, whole, cos_rows, sin_rows, grad_rot, sems,
+):
+    copies = row_copies(scalars[0], (part_a, part_b, part_c, part_d), whole, sems, False)
+    start_all(copies)
+    fill_tables(scalars, cosine, sine, cos_rows, sin_rows)
+    branch = load_tokens(same, sibling)
+    wait_all(copies)
+    grad_mixed = contract_cols(branch, whole[...]).astype(LOW)
+    scaling = 128**-0.5
+    for sequence in range(2):
+        rows = slice(sequence * 256, sequence * 256 + 256)
+        allowed = allowed_of(scalars, sequence)
+        for group in range(2):
+            keys = rotated[rows, 512 + group * 128 : 640 + group * 128]
+            value_rows = values[rows, group * 128 : group * 128 + 128]
+            grad_keys = jnp.zeros((256, 128), WIDE)
+            grad_values = jnp.zeros((256, 128), WIDE)
+            for head in (2 * group, 2 * group + 1):
+                cut = slice(head * 128, head * 128 + 128)
+                queries = rotated[rows, cut]
+                grad_mix = grad_mixed[rows, cut]
+                scores = jnp.where(allowed, contract_cols(queries, keys) * scaling, -1e30)
+                probs = jnp.exp(scores - log_total[rows, head : head + 1])
+                grad_values += contract_rows(probs.astype(LOW), grad_mix)
+                grad_probs = contract_cols(grad_mix, value_rows)
+                inner = jnp.sum(probs * grad_probs, axis=-1, keepdims=True)
+                grad_scores = (probs * (grad_probs - inner)).astype(LOW)
+                grad_rot[rows, cut] = matmul(grad_scores, keys) * scaling
+                grad_keys += contract_rows(grad_scores, queries)
+            grad_rot[rows, 512 + group * 128 : 640 + group * 128] = grad_keys * scaling
+            grad_all[rows, 768 + group * 128 : 896 + group * 128] = grad_values.astype(LOW)
+    gain_sums = [jnp.zeros((1, 128), WIDE), jnp.zeros((1, 128), WIDE)]
+    for head in range(6):
+        cut = slice(head * 128, head * 128 + 128)
+        which = 0 if head < 4 else 1
+        raw = pre[:, cut]
+        scale = lax.rsqrt(jnp.mean(raw * raw, axis=-1, keepdims=True) + EPSILON)
+        unit = raw * scale
+        coming = grad_rot[:, cut]
+        back = coming * cos_rows[...] - pltpu.roll(coming, 64, 1) * sin_rows[...]
+        gain_sums[which] += jnp.sum(back * unit, axis=0, keepdims=True)
+        back = back * gains[which : which + 1]
+        along = jnp.mean(back * unit, axis=-1, keepdims=True)
+        grad_all[:, cut] = (scale * (back - unit * along)).astype(LOW)
+    grad_gains[...] = jnp.zeros((8, 128), WIDE)
+    grad_gains[0:1] = gain_sums[0]
+    grad_gains[1:2] = gain_sums[1]
+
+
+def attend_back_call(scalars, branch, parts, pre, rotated, values, log_total, tables, gains):
+    return call(
+        attend_back_kernel,
+        [SM, VM, VM, HB, HB, HB, HB] + [VM] * 7,
+        [((512, 1024), LOW), ((8, 128), WIDE)],
+        [VM] * 2,
+        [
+            pltpu.VMEM((512, 1024), LOW),
+            pltpu.VMEM((512, 128), WIDE),
+            pltpu.VMEM((512, 128), WIDE),
+            pltpu.VMEM((512, 768), WIDE),
+            pltpu.SemaphoreType.DMA((8,)),
+        ],
+        2 * 10**9,
+        8 * 10**6,
+    )(scalars, *branch, *parts, pre, rotated, values, log_total, *tables, gains)
+
+
+def column_back_kernel(scalars, grads, part_a, part_b, part_c, part_d, same, sibling, whole, sems):
+    copies = column_copies(scalars[0], (part_a, part_b, part_c, part_d), whole, sems, False)
+    start_all(copies)
+    wait_all(copies)
+    store_tokens(contract_cols(grads[...], whole[...]), same, sibling)
+
+
+def column_back(scalars, grads, parts):
+    width = grads.shape[1]
+    return call(
+        column_back_kernel,
+        [SM, VM, HB, HB, HB, HB],
+        [((2, 128, 1024), LOW)] * 2,
+        [VM] * 2,
+        [pltpu.VMEM((1024, width), LOW), pltpu.SemaphoreType.DMA((16,))],
+        2 * 512 * 1024 * width,
+        5 * 10**6,
+    )(scalars, grads, *parts)
+
+
+def column_grad_kernel(
+    scalars, same, sibling, grads, keep_one, send_one, keep_two, send_two, whole, sems
+):
+    for at in range(0, 1024, 256):
+        cut = slice(at, at + 256)
+        left = jnp.concatenate(
+            [same[0, :, cut], sibling[0, :, cut], same[1, :, cut], sibling[1, :, cut]]
+        )
+        whole[cut] = contract_rows(left, grads[...]).astype(LOW)
+    copies = column_copies(
+        scalars[0], (keep_one, send_one, keep_two, send_two), whole, sems, True
+    )
+    start_all(copies)
+    wait_all(copies)
+
+
+def column_grad(scalars, tokens, grads):
+    width = grads.shape[1]
+    return call(
+        column_grad_kernel,
+        [SM, VM, VM, VM],
+        [((256, width), LOW)] * 4,
+        [HB] * 4,
+        [pltpu.VMEM((1024, width), LOW), pltpu.SemaphoreType.DMA((16,))],
+        2 * 512 * 1024 * width,
+        6 * 10**6,
+    )(scalars, *tokens, grads)
+
+
+def row_grad_kernel(
+    scalars, left, same, sibling, keep_one, send_one, keep_two, send_two, whole, sems
+):
+    right = load_tokens(same, sibling)
+    for at in range(0, whole.shape[0], 256):
+        cut = slice(at, at + 256)
+        whole[cut] = contract_rows(left[:, cut], right).astype(LOW)
+    copies = row_copies(scalars[0], (keep_one, send_one, keep_two, send_two), whole, sems, True)
+    start_all(copies)
+    wait_all(copies)
+
+
+def row_grad(scalars, left, tokens):
+    depth = left.shape[1]
+    return call(
+        row_grad_kernel,
+        [SM, VM, VM, VM],
+        [((depth // 4, 1024), LOW)] * 4,
+        [HB] * 4,
+        [pltpu.VMEM((depth, 1024), LOW), pltpu.SemaphoreType.DMA((8,))],
+        2 * 512 * 1024 * depth,
+        4 * 10**6,
+    )(scalars, left, *tokens)
+
+
+def fast_body(
+    hidden_in,
+    cotangent,
+    block_order,
+    w_query,
+    key_weight,
+    value_weight,
+    w_output,
+    w_gate,
+    w_up,
+    w_down,
+    norm_gains,
+    momentum_query,
+    key_momentum,
+    value_momentum,
+    momentum_output,
+    momentum_gate,
+    momentum_up,
+    momentum_down,
+    momentum_gains,
+):
+    index = lax.axis_index("dp")
+    core = lax.axis_index("ctx")
+    p_index = (index // P_BIT) % 2
+    mine = h_of(index) == core
+    slice_own = 2 * core + p_index
+    slice_give = 2 * core + 1 - p_index
+
+    def column_slice(weight, which):
+        size = weight.shape[1] // 4
+        return lax.dynamic_slice_in_dim(weight, which * size, size, axis=1).astype(LOW)
+
+    def column_pack(weights, which):
+        return jnp.concatenate([column_slice(weight, which) for weight in weights], axis=1)
+
+    gains_low = norm_gains.astype(LOW)[None]
+    for bit in (P_BIT, H_BIT, Y_BIT, X_BIT):
+        gains_low = jnp.concatenate([gains_low, swap(gains_low, bit)])
+    order = [0]
+    for bit in (P_BIT, H_BIT, Y_BIT, X_BIT):
+        order = order + [o ^ bit for o in order]
+    inverse = [0] * 16
+    for at, relative in enumerate(order):
+        inverse[relative] = at
+    lookup = jnp.array(inverse, jnp.int32)[index ^ jnp.arange(16)]
+    gains_all = jnp.take(gains_low, lookup, axis=0).reshape(-1).astype(WIDE)
+
+    width = hidden_in.shape[2]
+    head_size = 128
+    gain_attn = gains_all[:width]
+    gain_mlp = gains_all[width : 2 * width]
+    head_gains = gains_all[2 * width :].reshape(2, head_size)
+
+    qkv = (w_query, key_weight, value_weight)
+    qkv_parts = gather_column_slices(column_pack(qkv, slice_own), column_pack(qkv, slice_give))
+    output_parts = gather_row_slices(w_output.astype(LOW), mine)
+    gate_up = (w_gate, w_up)
+    gate_up_parts = gather_column_slices(
+        column_pack(gate_up, slice_own), column_pack(gate_up, slice_give)
+    )
+    down_parts = gather_row_slices(w_down.astype(LOW), mine)
+
+    tokens_own = hidden_in[0]
+    count = tokens_own.shape[0]
+    orders = jnp.concatenate([block_order, swap(block_order, P_BIT)])
+    orders = jnp.where(core == 0, orders, jnp.roll(orders, 2, axis=1))
+    scalars = jnp.concatenate([index[None], orders.reshape(-1)]).astype(jnp.int32)
+    cosine, sine_table = rotary_tables(jnp.arange(2 * count, dtype=jnp.int32), head_size)
+    sign = jnp.where(jnp.arange(head_size) < head_size // 2, -1.0, 1.0)
+    tables = (cosine, sine_table * sign)
+
+    tokens_f = tokens_own.astype(WIDE)
+    normed_f, norm_pull = jax.vjp(rms_norm, tokens_f, gain_attn)
+    normed = gather_tokens(normed_f.astype(LOW))
+    grad_out = gather_tokens(cotangent[0])
+
+    mixed_low, pre, rotated, value_low, log_total = attend(
+        scalars, normed, qkv_parts, tables, head_gains
+    )
+    attended = sum_tokens(*row_product(scalars, mixed_low, output_parts))
+    middle = tokens_f + attended
+    normed_two_f, norm_two_pull = jax.vjp(rms_norm, middle, gain_mlp)
+    normed_two = gather_tokens(normed_two_f.astype(LOW))
+    gate_up_act, active = gate_product(scalars, normed_two, gate_up_parts)
+    grad_down = row_grad(scalars, active, grad_out)
+    grad_gate_up, back_same, back_sibling = swiglu_back(
+        scalars, grad_out, gate_up_act, down_parts, gate_up_parts
+    )
+    grad_normed_two = sum_tokens(back_same, back_sibling)
+    grad_gate_up_mat = column_grad(scalars, normed_two, grad_gate_up)
+    layer_sum = sum_tokens(*row_product(scalars, active, down_parts))
+    layer_out = (middle + layer_sum).astype(LOW)[None]
+
+    grad_middle_norm, grad_gain_mlp = norm_two_pull(grad_normed_two)
+    grad_middle = cotangent[0].astype(WIDE) + grad_middle_norm
+    grad_branch = gather_tokens(grad_middle.astype(LOW))
+    grad_output_mat = row_grad(scalars, mixed_low, grad_branch)
+    grad_qkv, grad_head_gains = attend_back_call(
+        scalars, grad_branch, output_parts, pre, rotated, value_low, log_total, tables, head_gains
+    )
+    grad_qkv_mat = column_grad(scalars, normed, grad_qkv)
+    grad_normed = sum_tokens(*column_back(scalars, grad_qkv, qkv_parts))
+    grad_tokens_norm, grad_gain_attn = norm_pull(grad_normed)
+    input_grad = (grad_middle + grad_tokens_norm).astype(LOW)[None]
+
+    grad_gains = jnp.concatenate([grad_gain_attn, grad_gain_mlp, grad_head_gains[:2].reshape(-1)])
+    grad_gains = grad_gains.reshape(16, -1)
+    grad_gains = grad_gains + swap_core(grad_gains.astype(LOW)).astype(WIDE)
+    for bit in (P_BIT, H_BIT, Y_BIT, X_BIT):
+        grad_gains = grad_gains + swap(grad_gains.astype(LOW), bit).astype(WIDE)
+    grad_gains = lax.dynamic_index_in_dim(grad_gains, index, keepdims=False)
+
+    down_sum = scatter_row_slices(*grad_down, mine)
+    gate_up_sum = join_column_slices(*scatter_column_slices(*grad_gate_up_mat), p_index, core)
+    output_sum = scatter_row_slices(*grad_output_mat, mine)
+    qkv_sum = join_column_slices(*scatter_column_slices(*grad_qkv_mat), p_index, core)
+
+    def columns(parts, start, size):
+        return jnp.concatenate([part[:, start : start + size] for part in parts], axis=1)
+
+    query_width = w_query.shape[1] // 4
+    kv_width = key_weight.shape[1] // 4
+    hidden_units = w_gate.shape[1] // 4
+    sums = (
+        columns(qkv_sum, 0, query_width),
+        columns(qkv_sum, query_width, kv_width),
+        columns(qkv_sum, query_width + kv_width, kv_width),
+        output_sum,
+        columns(gate_up_sum, 0, hidden_units),
+        columns(gate_up_sum, hidden_units, hidden_units),
+        down_sum,
+        grad_gains,
+    )
+    masters = (w_query, key_weight, value_weight, w_output, w_gate, w_up, w_down, norm_gains)
+    moments = (
+        momentum_query,
+        key_momentum,
+        value_momentum,
+        momentum_output,
+        momentum_gate,
+        momentum_up,
+        momentum_down,
+        momentum_gains,
+    )
+    norm_scale = lax.rsqrt(jnp.float32(16 * 2 * count))
+    summed = tuple(part.astype(WIDE) for part in sums)
+    updates, new_moments = lion_step(masters, moments, summed, norm_scale)
+    return (layer_out, input_grad) + tuple(updates) + tuple(new_moments)
+
+
 def solution(mesh):
+    body = fast_body if dict(mesh.shape) == {"dp": 16, "ctx": 2} else general_body
     return jax.shard_map(
         body,
         mesh=mesh,

time: 1570 us -> 331 us (0.21)
  waiting for transfers between devices: 1240 us -> 140 us
  matrix products: 141 us -> 0 us
  blocking collectives: 87.2 us -> 0 us
  starting transfers between devices: 1.19 us -> 86.4 us
  Pallas kernels: 0 us -> 65.7 us
  local copies, waits for them, and re-layouts: 44.3 us -> 13.5 us
    reduce_scatter x7 -> x0, waiting for transfers between devices: 773 us -> none  [the longest x1 151 us: body(): lax.psum_scatter(grad_up_mat.astype(jnp.bfloat16), 'dp', scatter_dimensio...]
    all_gather x7 -> x0, waiting for transfers between devices: 454 us -> none  [the longest x1 92.8 us: body(): lax.all_gather(w_gate.astype(jnp.bfloat16), 'dp', axis=0, tiled=True)]
    dot_general x77 -> x0, matrix products: 141 us -> none  [the longest x7 25.6 us: matmul(): return jnp.dot(left, right, preferred_element_type=jnp.float32)]
    ppermute x0 -> x74, waiting for transfers between devices: none -> 140 us  [the longest x57 112 us: swap(): return lax.ppermute(values, 'dp', [(i, i ^ bit) for i in range(16)])]
    ppermute x0 -> x74, starting transfers between devices: none -> 86.4 us  [the longest x57 50.3 us: swap(): return lax.ppermute(values, 'dp', [(i, i ^ bit) for i in range(16)])]
    unnamed x2 -> x0, blocking collectives: 70.2 us -> none
    pallas_call x0 -> x11, Pallas kernels: none -> 65.7 us  [the longest x2 11.7 us: column_grad(): call(column_grad_kernel, [SM, VM, VM, VM], [((256, width), LOW)] * 4, [HB...]
  transfers between devices with their start and end apart: 17 -> 74, of which waited for: 16 -> 37; matrix products, arithmetic and copies ran while one was open for 7% -> 8% of each run, Pallas kernels for 0% -> 16%
where the time goes in v2:
time: 331 us; the launch traced here: 330 us
  waiting for transfers between devices  140 us (42%)
  starting transfers between devices  86.4 us (26%)
  Pallas kernels  65.7 us (20%)
  other arithmetic  23 us (7%)
  local copies, waits for them, and re-layouts  13.5 us (4%)
    ppermute x57, waiting for transfers between devices, swap(): return lax.ppermute(values, 'dp', [(i, i ^ bit) for i in range(16)])  112 us
    ppermute x57, starting transfers between devices, swap(): return lax.ppermute(values, 'dp', [(i, i ^ bit) for i in range(16)])  50.3 us
    ppermute x11, starting transfers between devices, swap_core(): return lax.ppermute(values, 'ctx', [(0, 1), (1, 0)])  23.7 us
    ppermute x4, waiting for transfers between devices, row_cross(): return lax.ppermute(values, ('dp', 'ctx'), pairs)  14.3 us
    ppermute x2, waiting for transfers between devices, scatter_row_slices(): return jnp.where(mine, summed, lax.ppermute(summed, ('dp', 'ctx'), pairs))  12.9 us
    pallas_call x2, Pallas kernels, column_grad(): call(column_grad_kernel, [SM, VM, VM, VM], [((256, width), LOW)] * 4, [HB...  11.7 us
    pallas_call x1, Pallas kernels, swiglu_back(): call(swiglu_back_kernel, [SM, VM, VM, VM] + [HB] * 8, [((512, 1536), LOW)...  10.8 us
    add x8, other arithmetic, lion_step(): new_moments.append(BETA_TWO * moment_arr + (1.0 - BETA_TWO) * scaled)  10.1 us
  transfers between devices with their start and end apart: 74, of which 37 were waited for; matrix products, arithmetic and copies ran while one was open for 8% of the time, Pallas kernels for 16%

profile of v2, /device:TPU:1, one launch (start us, length us, event | category | flops | bytes accessed | tf_op | source)
XLA Modules:
  0.0 330.5 jit_solution(12364923288565152838)
XLA Ops:
  29.2 5.2 %collective-permute-done.8 = bf16[128,1024]{1,0:T(8,128)(2,1)S(1)} collective-permute-done((bf16[128,1024]{1,0:T(8,128)(2,1)S(1)}, bf16[128,1024]{1,0:T(8,128)(2,1)S(1)}, u32[]{:S(2)}, u32[]{:S(2)}) %collective-permute-start.8) | collective-permute-done | bytes 262176 | tf_op jit(solution)/shard_map/ppermute | solution.py:329
  37.6 3.4 %collective-permute-done.11 = bf16[128,1024]{1,0:T(8,128)(2,1)S(1)} collective-permute-done((bf16[128,1024]{1,0:T(8,128)(2,1)S(1)}, bf16[128,1024]{1,0:T(8,128)(2,1)S(1)}, u32[]{:S(2)}, u32[]{:S(2)}) %collective-permute-start.11) | collective-permute-done | bytes 262176 | tf_op jit(solution)/shard_map/ppermute | solution.py:329
  41.0 8.4 %collective-permute-start.6 = (bf16[2,128,1024]{2,1,0:T(8,128)(2,1)S(1)}, bf16[2,128,1024]{2,1,0:T(8,128)(2,1)S(1)}, u32[]{:S(2)}, u32[]{:S(2)}) collective-permute-start(bf16[2,128,1024]{2,1,0:T(8,128)(2,1)S(1)} %pad_maximum_fusion.2.same), channel_id=1, source_target_pairs={{0,1},{1,0},{2,3},{3,2},{4,5},{5,4},{6,7},{7,6},{8,9},{9,8},{10,11... | collective-permute-start | bytes 1572872 | tf_op jit(solution)/shard_map/ppermute | solution.py:333
  53.9 9.2 %collective-permute-done.12.part_d = bf16[256,1024]{1,0:T(8,128)(2,1)S(1)} collective-permute-done((bf16[256,1024]{1,0:T(8,128)(2,1)S(1)}, bf16[256,1024]{1,0:T(8,128)(2,1)S(1)}, u32[]{:S(2)}, u32[]{:S(2)}) %collective-permute-start.12) | collective-permute-done | bytes 524320 | tf_op jit(solution)/shard_map/ppermute | solution.py:329
  63.2 8.0 %shard_map.331 = (bf16[512,512]{1,0:T(8,128)(2,1)S(1)}, f32[512,768]{1,0:T(8,128)}, bf16[512,768]{1,0:T(8,128)(2,1)S(1)}, bf16[512,256]{1,0:T(8,128)(2,1)S(1)}, f32[512,128]{1,0:T(8,128)S(1)}) custom-call(s32[9]{0:T(128)S(1)} %pad_add_fusion.1.scalars, bf16[2,128,1024]{2,1,0:T(8,128)(2,1)S(1)} %pad_maximum_fusion.2.same, ...), custom_call_target="tpu_custom_call" | custom-call | flops 2000000000 | bytes 8000000 | tf_op jit(solution)/shard_map/pallas_call | solution.py:549
  79.9 7.7 %collective-permute-done.26 = bf16[128,1536]{1,0:T(8,128)(2,1)S(1)} collective-permute-done((bf16[128,1536]{1,0:T(8,128)(2,1)S(1)}, bf16[128,1536]{1,0:T(8,128)(2,1)S(1)}, u32[]{:S(2)}, u32[]{:S(2)}) %collective-permute-start.26) | collective-permute-done | bytes 393248 | tf_op jit(solution)/shard_map/ppermute | solution.py:329
  91.2 5.0 %collective-permute-done.20 = bf16[128,1024]{1,0:T(8,128)(2,1)S(1)} collective-permute-done((bf16[128,1024]{1,0:T(8,128)(2,1)S(1)}, bf16[128,1024]{1,0:T(8,128)(2,1)S(1)}, u32[]{:S(2)}, u32[]{:S(2)}) %collective-permute-start.20) | collective-permute-done | bytes 262176 | tf_op jit(solution)/shard_map/ppermute | solution.py:329
  98.4 8.4 %collective-permute-done.27.part_d.col_d = bf16[256,1536]{1,0:T(8,128)(2,1)S(1)} collective-permute-done((bf16[256,1536]{1,0:T(8,128)(2,1)S(1)}, bf16[256,1536]{1,0:T(8,128)(2,1)S(1)}, u32[]{:S(2)}, u32[]{:S(2)}) %collective-permute-start.27) | collective-permute-done | bytes 786464 | tf_op jit(solution)/shard_map/ppermute | solution.py:329
  107.0 8.6 %shard_map.333 = (f32[512,1536]{1,0:T(8,128)}, bf16[512,768]{1,0:T(8,128)(2,1)S(1)}) custom-call(s32[9]{0:T(128)S(1)} %pad_add_fusion.1.scalars, bf16[2,128,1024]{2,1,0:T(8,128)(2,1)S(1)} %pad_maximum_fusion.5.same, bf16[2,128,1024]{2,1,0:T(8,128)(2,1)S(1)} %collective-permute-done.21.sibling, bf16[256,1536]{1,0:T(8,128)(2,1)S(1)} %pad_maximum_fusion.part_a.col_a, ...), custom_call_target="tpu_custom_call" | custom-call | flops 1610612736 | bytes 10000000 | tf_op jit(solution)/shard_map/pallas_call | solution.py:601
  115.6 3.7 %shard_map.341 = (bf16[192,1024]{1,0:T(8,128)(2,1)S(1)}, bf16[192,1024]{1,0:T(8,128)(2,1)S(1)}, bf16[192,1024]{1,0:T(8,128)(2,1)S(1)}, bf16[192,1024]{1,0:T(8,128)(2,1)S(1)}) custom-call(s32[9]{0:T(128)S(1)} %pad_add_fusion.1.scalars, bf16[512,768]{1,0:T(8,128)(2,1)S(1)} %get-tuple-element.55.mixture.left, bf16[2,128,1024]{2,1,0:T(8,128)(2,1)S(1)} %pad_maximum_fusion.6.same, ...), custom_call_target="tpu_custom_call" | custom-call | flops 805306368 | bytes 4000000 | tf_op jit(solution)/shard_map/pallas_call | solution.py:784
  122.0 5.2 %collective-permute-done.63 = bf16[192,1024]{1,0:T(8,128)(2,1)S(1)} collective-permute-done((bf16[192,1024]{1,0:T(8,128)(2,1)S(1)}, bf16[192,1024]{1,0:T(8,128)(2,1)S(1)}, u32[]{:S(2)}, u32[]{:S(2)}) %collective-permute-start.63) | collective-permute-done | bytes 393248 | tf_op jit(solution)/shard_map/ppermute | solution.py:329
  137.5 4.7 %collective-permute-done.67 = bf16[192,1024]{1,0:T(8,128)(2,1)S(1)} collective-permute-done((bf16[192,1024]{1,0:T(8,128)(2,1)S(1)}, bf16[192,1024]{1,0:T(8,128)(2,1)S(1)}, u32[]{:S(2)}, u32[]{:S(2)}) %collective-permute-start.67) | collective-permute-done | bytes 393248 | tf_op jit(solution)/shard_map/ppermute | solution.py:346
  143.8 12.9 %collective-permute-done.68 = bf16[192,1024]{1,0:T(8,128)(2,1)S(1)} collective-permute-done((bf16[192,1024]{1,0:T(8,128)(2,1)S(1)}, bf16[192,1024]{1,0:T(8,128)(2,1)S(1)}, u32[]{:S(2)}, u32[]{:S(2)}) %collective-permute-start.68) | collective-permute-done | bytes 393248 | tf_op jit(solution)/shard_map/ppermute | solution.py:394
  159.5 9.6 %collective-permute-done.28 = bf16[192,1024]{1,0:T(8,128)(2,1)S(1)} collective-permute-done((bf16[192,1024]{1,0:T(8,128)(2,1)S(1)}, bf16[192,1024]{1,0:T(8,128)(2,1)S(1)}, u32[]{:S(2)}, u32[]{:S(2)}) %collective-permute-start.28) | collective-permute-done | bytes 393248 | tf_op jit(solution)/shard_map/ppermute | solution.py:346
  170.2 3.9 %collective-permute-done.29 = bf16[96,1024]{1,0:T(8,128)(2,1)S(1)} collective-permute-done((bf16[96,1024]{1,0:T(8,128)(2,1)S(1)}, bf16[96,1024]{1,0:T(8,128)(2,1)S(1)}, u32[]{:S(2)}, u32[]{:S(2)}) %collective-permute-start.29) | collective-permute-done | bytes 196640 | tf_op jit(solution)/shard_map/ppermute | solution.py:329
  175.3 8.4 %collective-permute-done.30.part_b.row_b = bf16[192,1024]{1,0:T(8,128)(2,1)S(1)} collective-permute-done((bf16[192,1024]{1,0:T(8,128)(2,1)S(1)}, bf16[192,1024]{1,0:T(8,128)(2,1)S(1)}, u32[]{:S(2)}, u32[]{:S(2)}) %collective-permute-start.30) | collective-permute-done | bytes 393248 | tf_op jit(solution)/shard_map/ppermute | solution.py:329
  186.0 10.8 %shard_map.335 = (bf16[512,1536]{1,0:T(8,128)(2,1)}, bf16[2,128,1024]{2,1,0:T(8,128)(2,1)S(1)}, bf16[2,128,1024]{2,1,0:T(8,128)(2,1)S(1)}) custom-call(s32[9]{0:T(128)S(1)} %pad_add_fusion.1.scalars, bf16[2,128,1024]{2,1,0:T(8,128)(2,1)S(1)} %pad_maximum_fusion.6.same, bf16[2,128,1024]{2,1,0:T(8,128)(2,1)S(1)} %collective-permute-done.36.sibling, ...), custom_call_target="tpu_custom_call" | custom-call | flops 2415919104 | bytes 12000000 | tf_op jit(solution)/shard_map/pallas_call | solution.py:636
  197.5 3.7 %shard_map.334 = (bf16[2,128,1024]{2,1,0:T(8,128)(2,1)S(1)}, bf16[2,128,1024]{2,1,0:T(8,128)(2,1)S(1)}) custom-call(s32[9]{0:T(128)S(1)} %pad_add_fusion.1.scalars, bf16[512,768]{1,0:T(8,128)(2,1)S(1)} %get-tuple-element.55.mixture.left, bf16[192,1024]{1,0:T(8,128)(2,1)S(1)} %pad_maximum_fusion.12.part_a.row_a, ...), custom_call_target="tpu_custom_call" | custom-call | flops 805306368 | bytes 4000000 | tf_op jit(solution)/shard_map/pallas_call | solution.py:574
  201.3 6.8 %shard_map.340 = (bf16[256,1536]{1,0:T(8,128)(2,1)S(1)}, bf16[256,1536]{1,0:T(8,128)(2,1)S(1)}, bf16[256,1536]{1,0:T(8,128)(2,1)S(1)}, bf16[256,1536]{1,0:T(8,128)(2,1)S(1)}) custom-call(s32[9]{0:T(128)S(1)} %pad_add_fusion.1.scalars, bf16[2,128,1024]{2,1,0:T(8,128)(2,1)S(1)} %pad_maximum_fusion.5.same, ...), custom_call_target="tpu_custom_call" | custom-call | flops 1610612736 | bytes 6000000 | tf_op jit(solution)/shard_map/pallas_call | solution.py:759
  211.5 5.0 %collective-permute-done.38 = bf16[128,1024]{1,0:T(8,128)(2,1)S(1)} collective-permute-done((bf16[128,1024]{1,0:T(8,128)(2,1)S(1)}, bf16[128,1024]{1,0:T(8,128)(2,1)S(1)}, u32[]{:S(2)}, u32[]{:S(2)}) %collective-permute-start.38) | collective-permute-done | bytes 262176 | tf_op jit(solution)/shard_map/ppermute | solution.py:329
  216.8 5.4 %collective-permute-done.34 = bf16[128,1024]{1,0:T(8,128)(2,1)S(1)} collective-permute-done((bf16[128,1024]{1,0:T(8,128)(2,1)S(1)}, bf16[128,1024]{1,0:T(8,128)(2,1)S(1)}, u32[]{:S(2)}, u32[]{:S(2)}) %collective-permute-start.34) | collective-permute-done | bytes 262176 | tf_op jit(solution)/shard_map/ppermute | solution.py:329
  223.6 3.2 collective-permute-done.56
  232.1 4.3 %collective-permute-done.57 = bf16[128,1536]{1,0:T(8,128)(2,1)S(1)} collective-permute-done((bf16[128,1536]{1,0:T(8,128)(2,1)S(1)}, bf16[128,1536]{1,0:T(8,128)(2,1)S(1)}, u32[]{:S(2)}, u32[]{:S(2)}) %collective-permute-start.57) | collective-permute-done | bytes 393248 | tf_op jit(solution)/shard_map/ppermute | solution.py:329
  239.9 3.3 %shard_map.339 = (bf16[128,1024]{1,0:T(8,128)(2,1)S(1)}, bf16[128,1024]{1,0:T(8,128)(2,1)S(1)}, bf16[128,1024]{1,0:T(8,128)(2,1)S(1)}, bf16[128,1024]{1,0:T(8,128)(2,1)S(1)}) custom-call(s32[9]{0:T(128)S(1)} %pad_add_fusion.1.scalars, bf16[512,512]{1,0:T(8,128)(2,1)S(1)} %copy-done.11, bf16[2,128,1024]{2,1,0:T(8,128)(2,1)S(1)} %pad_maximum_fusion.7.same, ...), custom_call_target="tpu_custom_call" | custom-call | flops 536870912 | bytes 4000000 | tf_op jit(solution)/shard_map/pallas_call | solution.py:784
  245.2 8.4 %shard_map.336 = (bf16[512,1024]{1,0:T(8,128)(2,1)S(1)}, f32[8,128]{1,0:T(8,128)S(1)}) custom-call(s32[9]{0:T(128)S(1)} %pad_add_fusion.1.scalars, bf16[2,128,1024]{2,1,0:T(8,128)(2,1)S(1)} %pad_maximum_fusion.7.same, bf16[2,128,1024]{2,1,0:T(8,128)(2,1)} %collective-permute-done.40.sibling, bf16[128,1024]{1,0:T(8,128)(2,1)S(1)} %pad_maximum_fusion.23.part_a, ...), custom_call_target="tpu_custom_call" | custom-call | flops 2000000000 | bytes 8000000 | tf_op jit(solution)/shard_map/pallas_call | solution.py:704
  253.7 4.9 %shard_map.338 = (bf16[256,1024]{1,0:T(8,128)(2,1)S(1)}, bf16[256,1024]{1,0:T(8,128)(2,1)S(1)}, bf16[256,1024]{1,0:T(8,128)(2,1)S(1)}, bf16[256,1024]{1,0:T(8,128)(2,1)S(1)}) custom-call(s32[9]{0:T(128)S(1)} %pad_add_fusion.1.scalars, bf16[2,128,1024]{2,1,0:T(8,128)(2,1)S(1)} %pad_maximum_fusion.2.same, bf16[2,128,1024]{2,1,0:T(8,128)(2,1)S(1)} %copy-done.4, ...), custom_call_target="tpu_custom_call" | custom-call | flops 1073741824 | bytes 6000000 | tf_op jit(solution)/shard_map/pallas_call | solution.py:759
  262.0 4.9 %shard_map.337 = (bf16[2,128,1024]{2,1,0:T(8,128)(2,1)S(1)}, bf16[2,128,1024]{2,1,0:T(8,128)(2,1)S(1)}) custom-call(s32[9]{0:T(128)S(1)} %pad_add_fusion.1.scalars, bf16[512,1024]{1,0:T(8,128)(2,1)S(1)} %get-tuple-element.65.grads, bf16[256,1024]{1,0:T(8,128)(2,1)S(1)} %pad_maximum_fusion.3.part_a, bf16[256,1024]{1,0:T(8,128)(2,1)S(1)} %copy-done.2, ...), custom_call_target="tpu_custom_call" | custom-call | flops 1073741824 | bytes 5000000 | tf_op jit(solution)/shard_map/pallas_call | solution.py:730
  266.9 3.8 %collective-permute-start.41 = (bf16[2,128,1024]{2,1,0:T(8,128)(2,1)S(1)}, bf16[2,128,1024]{2,1,0:T(8,128)(2,1)S(1)}, u32[]{:S(2)}, u32[]{:S(2)}) collective-permute-start(bf16[2,128,1024]{2,1,0:T(8,128)(2,1)S(1)} %get-tuple-element.67), channel_id=1, source_target_pairs={{0,1},{1,0},{2,3},{3,2},{4,5},{5,4},{6,7},{7,6},{8,9},{9,8},{10,11... | collective-permute-start | bytes 1572872 | tf_op jit(solution)/shard_map/ppermute | solution.py:333
  272.0 3.6 %collective-permute-done.51 = bf16[64,1024]{1,0:T(8,128)(2,1)S(1)} collective-permute-done((bf16[64,1024]{1,0:T(8,128)(2,1)S(1)}, bf16[64,1024]{1,0:T(8,128)(2,1)S(1)}, u32[]{:S(2)}, u32[]{:S(2)}) %collective-permute-start.51) | collective-permute-done | bytes 131104 | tf_op jit(solution)/shard_map/ppermute | solution.py:329
  279.5 3.8 %collective-permute-start.54 = (bf16[128,1024]{1,0:T(8,128)(2,1)S(1)}, bf16[128,1024]{1,0:T(8,128)(2,1)S(1)}, u32[]{:S(2)}, u32[]{:S(2)}) collective-permute-start(bf16[128,1024]{1,0:T(8,128)(2,1)S(1)} %pad_maximum_fusion.28), channel_id=1, source_target_pairs={{1,17},{3,19},{5,21},{7,23},{9,25},{11,27},{13,29},{15,31},{16,0},... | collective-permute-start | bytes 786440 | tf_op jit(solution)/shard_map/ppermute | solution.py:346
  309.9 8.1 %collective-permute-done.47 = bf16[128,1024]{1,0:T(8,128)(2,1)S(1)} collective-permute-done((bf16[128,1024]{1,0:T(8,128)(2,1)S(1)}, bf16[128,1024]{1,0:T(8,128)(2,1)S(1)}, u32[]{:S(2)}, u32[]{:S(2)}) %collective-permute-start.47) | collective-permute-done | bytes 262176 | tf_op jit(solution)/shard_map/ppermute | solution.py:329
  318.8 3.2 collective-permute-done.48
  (393 shorter events, 132.8 us)
Async XLA Ops:
  0.7 12.5 %collective-permute-start = (s32[1,4]{1,0:T(1,128)}, s32[1,4]{1,0:T(1,128)S(1)}, u32[]{:S(2)}, u32[]{:S(2)}) collective-permute-start(s32[1,4]{1,0:T(1,128)} %param.22), channel_id=1, source_target_pairs={{0,8},{2,10},{4,12},{6,14},{8,0},{10,2},{12,4},{14,6},{16,24},{18,... | collective-permute-start | bytes 56 | tf_op jit(solution)/shard_map/ppermute | solution.py:329
  5.6 19.6 %collective-permute-start.7 = (bf16[64,1024]{1,0:T(8,128)(2,1)S(1)}, bf16[64,1024]{1,0:T(8,128)(2,1)S(1)}, u32[]{:S(2)}, u32[]{:S(2)}) collective-permute-start(bf16[64,1024]{1,0:T(8,128)(2,1)S(1)} %pad_maximum_fusion.30), channel_id=1, source_target_pairs={{0,8},{2,10},{4,12},{6,14},{8,0},{10,2},{12,4},{14,6},{16,24},{18,... | collective-permute-start | bytes 393224 | tf_op jit(solution)/shard_map/ppermute | solution.py:329
  8.2 20.9 %collective-permute-start.13 = (bf16[128,1024]{1,0:T(8,128)(2,1)S(1)}, bf16[128,1024]{1,0:T(8,128)(2,1)S(1)}, u32[]{:S(2)}, u32[]{:S(2)}) collective-permute-start(bf16[128,1024]{1,0:T(8,128)(2,1)S(1)} %convert_element_type.387), channel_id=1, source_target_pairs={{0,16},{2,18},{4,20},{6,22},{8,24},{10,26},{12,28},{14,30},{17,1},... | collective-permute-start | bytes 786440 | tf_op jit(solution)/shard_map/ppermute | solution.py:346
  11.5 38.4 %collective-permute-start.22 = (bf16[64,1536]{1,0:T(8,128)(2,1)}, bf16[64,1536]{1,0:T(8,128)(2,1)S(1)}, u32[]{:S(2)}, u32[]{:S(2)}) collective-permute-start(bf16[64,1536]{1,0:T(8,128)(2,1)} %pad_maximum_fusion.29), channel_id=1, source_target_pairs={{0,8},{2,10},{4,12},{6,14},{8,0},{10,2},{12,4},{14,6},{16,24},{18,... | collective-permute-start | bytes 589832 | tf_op jit(solution)/shard_map/ppermute | solution.py:329
  34.4 15.1 %collective-permute-start.9 = (bf16[128,1024]{1,0:T(8,128)(2,1)S(1)}, bf16[128,1024]{1,0:T(8,128)(2,1)S(1)}, u32[]{:S(2)}, u32[]{:S(2)}) collective-permute-start(bf16[128,1024]{1,0:T(8,128)(2,1)S(1)} %pad_maximum_fusion.21), channel_id=1, source_target_pairs={{0,4},{2,6},{4,0},{6,2},{8,12},{10,14},{12,8},{14,10},{16,20},{18,... | collective-permute-start | bytes 786440 | tf_op jit(solution)/shard_map/ppermute | solution.py:329
  37.0 14.3 %collective-permute-start.16 = (bf16[64,1024]{1,0:T(8,128)(2,1)S(1)}, bf16[64,1024]{1,0:T(8,128)(2,1)S(1)}, u32[]{:S(2)}, u32[]{:S(2)}) collective-permute-start(bf16[64,1024]{1,0:T(8,128)(2,1)S(1)} %get-tuple-element.148), channel_id=1, source_target_pairs={{0,2},{2,0},{4,6},{6,4},{8,10},{10,8},{12,14},{14,12},{16,18},{18,... | collective-permute-start | bytes 393224 | tf_op jit(solution)/shard_map/ppermute | solution.py:329
  37.3 13.8 %collective-permute-start.14 = (bf16[64,1024]{1,0:T(8,128)(2,1)S(1)}, bf16[64,1024]{1,0:T(8,128)(2,1)S(1)}, u32[]{:S(2)}, u32[]{:S(2)}) collective-permute-start(bf16[64,1024]{1,0:T(8,128)(2,1)S(1)} %get-tuple-element.149), channel_id=1, source_target_pairs={{0,4},{2,6},{4,0},{6,2},{8,12},{10,14},{12,8},{14,10},{16,20},{18,... | collective-permute-start | bytes 393224 | tf_op jit(solution)/shard_map/ppermute | solution.py:329
  49.5 13.6 %collective-permute-start.12 = (bf16[256,1024]{1,0:T(8,128)(2,1)S(1)}, bf16[256,1024]{1,0:T(8,128)(2,1)S(1)}, u32[]{:S(2)}, u32[]{:S(2)}) collective-permute-start(bf16[256,1024]{1,0:T(8,128)(2,1)S(1)} %pad_maximum_fusion.4.part_c), channel_id=1, source_target_pairs={{0,4},{2,6},{4,0},{6,2},{8,12},{10,14},{12,8},{14,10},{16,20},{18,... | collective-permute-start | bytes 1572872 | tf_op jit(solution)/shard_map/ppermute | solution.py:329
  49.9 13.3 %collective-permute-start.10 = (bf16[256,1024]{1,0:T(8,128)(2,1)S(1)}, bf16[256,1024]{1,0:T(8,128)(2,1)S(1)}, u32[]{:S(2)}, u32[]{:S(2)}) collective-permute-start(bf16[256,1024]{1,0:T(8,128)(2,1)S(1)} %pad_maximum_fusion.3.part_a), channel_id=1, source_target_pairs={{0,2},{2,0},{4,6},{6,4},{8,10},{10,8},{12,14},{14,12},{16,18},{18,... | collective-permute-start | bytes 1572872 | tf_op jit(solution)/shard_map/ppermute | solution.py:329
  51.2 25.5 %collective-permute-start.23 = (bf16[128,1536]{1,0:T(8,128)(2,1)S(1)}, bf16[128,1536]{1,0:T(8,128)(2,1)S(1)}, u32[]{:S(2)}, u32[]{:S(2)}) collective-permute-start(bf16[128,1536]{1,0:T(8,128)(2,1)S(1)} %pad_maximum_fusion.8), channel_id=1, source_target_pairs={{0,16},{2,18},{4,20},{6,22},{8,24},{10,26},{12,28},{14,30},{16,0},... | collective-permute-start | bytes 1179656 | tf_op jit(solution)/shard_map/ppermute | solution.py:329
  51.3 20.7 %collective-permute-start.15 = (bf16[128,1024]{1,0:T(8,128)(2,1)S(1)}, bf16[128,1024]{1,0:T(8,128)(2,1)S(1)}, u32[]{:S(2)}, u32[]{:S(2)}) collective-permute-start(bf16[128,1024]{1,0:T(8,128)(2,1)S(1)} %pad_maximum_fusion.23.part_a), channel_id=1, source_target_pairs={{0,2},{2,0},{4,6},{6,4},{8,10},{10,8},{12,14},{14,12},{16,18},{18,... | collective-permute-start | bytes 786440 | tf_op jit(solution)/shard_map/ppermute | solution.py:329
  51.9 20.2 %collective-permute-start.17 = (bf16[128,1024]{1,0:T(8,128)(2,1)S(1)}, bf16[128,1024]{1,0:T(8,128)(2,1)S(1)}, u32[]{:S(2)}, u32[]{:S(2)}) collective-permute-start(bf16[128,1024]{1,0:T(8,128)(2,1)S(1)} %pad_maximum_fusion.24.part_c), channel_id=1, source_target_pairs={{0,4},{2,6},{4,0},{6,2},{8,12},{10,14},{12,8},{14,10},{16,20},{18,... | collective-permute-start | bytes 786440 | tf_op jit(solution)/shard_map/ppermute | solution.py:329
  63.1 35.1 %collective-permute-start.35 = (bf16[128,1024]{1,0:T(8,128)(2,1)S(1)}, bf16[128,1024]{1,0:T(8,128)(2,1)S(1)}, u32[]{:S(2)}, u32[]{:S(2)}) collective-permute-start(bf16[128,1024]{1,0:T(8,128)(2,1)S(1)} %bitcast.128), channel_id=1, source_target_pairs={{0,8},{2,10},{4,12},{6,14},{8,0},{10,2},{12,4},{14,6},{16,24},{18,... | collective-permute-start | bytes 786440 | tf_op jit(solution)/shard_map/ppermute | solution.py:329
  87.7 19.1 %collective-permute-start.27 = (bf16[256,1536]{1,0:T(8,128)(2,1)S(1)}, bf16[256,1536]{1,0:T(8,128)(2,1)S(1)}, u32[]{:S(2)}, u32[]{:S(2)}) collective-permute-start(bf16[256,1536]{1,0:T(8,128)(2,1)S(1)} %pad_maximum_fusion.1.part_c.col_c), channel_id=1, source_target_pairs={{0,4},{2,6},{4,0},{6,2},{8,12},{10,14},{12,8},{14,10},{16,20},{18,... | collective-permute-start | bytes 2359304 | tf_op jit(solution)/shard_map/ppermute | solution.py:329
  89.8 17.3 %collective-permute-start.25 = (bf16[256,1536]{1,0:T(8,128)(2,1)S(1)}, bf16[256,1536]{1,0:T(8,128)(2,1)S(1)}, u32[]{:S(2)}, u32[]{:S(2)}) collective-permute-start(bf16[256,1536]{1,0:T(8,128)(2,1)S(1)} %pad_maximum_fusion.part_a.col_a), channel_id=1, source_target_pairs={{0,2},{2,0},{4,6},{6,4},{8,10},{10,8},{12,14},{14,12},{16,18},{18,... | collective-permute-start | bytes 2359304 | tf_op jit(solution)/shard_map/ppermute | solution.py:329
  98.3 17.3 %collective-permute-start.36 = (bf16[2,128,1024]{2,1,0:T(8,128)(2,1)S(1)}, bf16[2,128,1024]{2,1,0:T(8,128)(2,1)S(1)}, u32[]{:S(2)}, u32[]{:S(2)}) collective-permute-start(bf16[2,128,1024]{2,1,0:T(8,128)(2,1)S(1)} %pad_maximum_fusion.6.same), channel_id=1, source_target_pairs={{0,1},{1,0},{2,3},{3,2},{4,5},{5,4},{6,7},{7,6},{8,9},{9,8},{10,11... | collective-permute-start | bytes 1572872 | tf_op jit(solution)/shard_map/ppermute | solution.py:333
  142.3 14.4 %collective-permute-start.68 = (bf16[192,1024]{1,0:T(8,128)(2,1)S(1)}, bf16[192,1024]{1,0:T(8,128)(2,1)S(1)}, u32[]{:S(2)}, u32[]{:S(2)}) collective-permute-start(bf16[192,1024]{1,0:T(8,128)(2,1)S(1)} %add_convert_fusion.4), channel_id=1, source_target_pairs={{0,1},{2,3},{4,5},{6,7},{8,9},{10,11},{12,13},{14,15},{17,16},{19,... | collective-permute-start | bytes 1179656 | tf_op jit(solution)/shard_map/ppermute | solution.py:394
  196.9 12.6 %collective-permute-start.37 = (bf16[2,128,1024]{2,1,0:T(8,128)(2,1)S(1)}, bf16[2,128,1024]{2,1,0:T(8,128)(2,1)S(1)}, u32[]{:S(2)}, u32[]{:S(2)}) collective-permute-start(bf16[2,128,1024]{2,1,0:T(8,128)(2,1)S(1)} %get-tuple-element.60), channel_id=1, source_target_pairs={{0,1},{1,0},{2,3},{3,2},{4,5},{5,4},{6,7},{7,6},{8,9},{9,8},{10,11... | collective-permute-start | bytes 1572872 | tf_op jit(solution)/shard_map/ppermute | solution.py:333
  208.2 18.7 %collective-permute-start.56 = (bf16[256,1536]{1,0:T(8,128)(2,1)S(1)}, bf16[256,1536]{1,0:T(8,128)(2,1)S(1)}, u32[]{:S(2)}, u32[]{:S(2)}) collective-permute-start(bf16[256,1536]{1,0:T(8,128)(2,1)S(1)} %get-tuple-element.78), channel_id=1, source_target_pairs={{0,2},{2,0},{4,6},{6,4},{8,10},{10,8},{12,14},{14,12},{16,18},{18,... | collective-permute-start | bytes 2359304 | tf_op jit(solution)/shard_map/ppermute | solution.py:329
  208.2 18.9 %collective-permute-start.58 = (bf16[256,1536]{1,0:T(8,128)(2,1)S(1)}, bf16[256,1536]{1,0:T(8,128)(2,1)S(1)}, u32[]{:S(2)}, u32[]{:S(2)}) collective-permute-start(bf16[256,1536]{1,0:T(8,128)(2,1)S(1)} %get-tuple-element.80), channel_id=1, source_target_pairs={{0,4},{2,6},{4,0},{6,2},{8,12},{10,14},{12,8},{14,10},{16,20},{18,... | collective-permute-start | bytes 2359304 | tf_op jit(solution)/shard_map/ppermute | solution.py:329
  210.0 12.1 %collective-permute-start.34 = (bf16[128,1024]{1,0:T(8,128)(2,1)S(1)}, bf16[128,1024]{1,0:T(8,128)(2,1)S(1)}, u32[]{:S(2)}, u32[]{:S(2)}) collective-permute-start(bf16[128,1024]{1,0:T(8,128)(2,1)S(1)} %fusion.38), channel_id=1, source_target_pairs={{0,8},{2,10},{4,12},{6,14},{8,0},{10,2},{12,4},{14,6},{16,24},{18,... | collective-permute-start | bytes 786440 | tf_op jit(solution)/shard_map/ppermute | solution.py:329
  238.8 20.9 %collective-permute-start.60 = (bf16[128,1536]{1,0:T(8,128)(2,1)}, bf16[128,1536]{1,0:T(8,128)(2,1)}, u32[]{:S(2)}, u32[]{:S(2)}) collective-permute-start(bf16[128,1536]{1,0:T(8,128)(2,1)} %pad_maximum_fusion.14), channel_id=1, source_target_pairs={{0,16},{2,18},{4,20},{6,22},{8,24},{10,26},{12,28},{14,30},{16,0},... | collective-permute-start | bytes 1179656 | tf_op jit(solution)/shard_map/ppermute | solution.py:329
  243.3 27.5 %collective-permute-start.50 = (bf16[128,1024]{1,0:T(8,128)(2,1)S(1)}, bf16[128,1024]{1,0:T(8,128)(2,1)S(1)}, u32[]{:S(2)}, u32[]{:S(2)}) collective-permute-start(bf16[128,1024]{1,0:T(8,128)(2,1)S(1)} %get-tuple-element.73), channel_id=1, source_target_pairs={{0,2},{2,0},{4,6},{6,4},{8,10},{10,8},{12,14},{14,12},{16,18},{18,... | collective-permute-start | bytes 786440 | tf_op jit(solution)/shard_map/ppermute | solution.py:329
  244.5 26.5 %collective-permute-start.52 = (bf16[128,1024]{1,0:T(8,128)(2,1)S(1)}, bf16[128,1024]{1,0:T(8,128)(2,1)S(1)}, u32[]{:S(2)}, u32[]{:S(2)}) collective-permute-start(bf16[128,1024]{1,0:T(8,128)(2,1)S(1)} %get-tuple-element.75), channel_id=1, source_target_pairs={{0,4},{2,6},{4,0},{6,2},{8,12},{10,14},{12,8},{14,10},{16,20},{18,... | collective-permute-start | bytes 786440 | tf_op jit(solution)/shard_map/ppermute | solution.py:329
  258.6 24.8 %collective-permute-start.43 = (bf16[256,1024]{1,0:T(8,128)(2,1)S(1)}, bf16[256,1024]{1,0:T(8,128)(2,1)S(1)}, u32[]{:S(2)}, u32[]{:S(2)}) collective-permute-start(bf16[256,1024]{1,0:T(8,128)(2,1)S(1)} %get-tuple-element.69), channel_id=1, source_target_pairs={{0,2},{2,0},{4,6},{6,4},{8,10},{10,8},{12,14},{14,12},{16,18},{18,... | collective-permute-start | bytes 1572872 | tf_op jit(solution)/shard_map/ppermute | solution.py:329
  259.0 26.2 %collective-permute-start.45 = (bf16[256,1024]{1,0:T(8,128)(2,1)S(1)}, bf16[256,1024]{1,0:T(8,128)(2,1)S(1)}, u32[]{:S(2)}, u32[]{:S(2)}) collective-permute-start(bf16[256,1024]{1,0:T(8,128)(2,1)S(1)} %get-tuple-element.71), channel_id=1, source_target_pairs={{0,4},{2,6},{4,0},{6,2},{8,12},{10,14},{12,8},{14,10},{16,20},{18,... | collective-permute-start | bytes 1572872 | tf_op jit(solution)/shard_map/ppermute | solution.py:329
  266.9 19.6 %collective-permute-start.41 = (bf16[2,128,1024]{2,1,0:T(8,128)(2,1)S(1)}, bf16[2,128,1024]{2,1,0:T(8,128)(2,1)S(1)}, u32[]{:S(2)}, u32[]{:S(2)}) collective-permute-start(bf16[2,128,1024]{2,1,0:T(8,128)(2,1)S(1)} %get-tuple-element.67), channel_id=1, source_target_pairs={{0,1},{1,0},{2,3},{3,2},{4,5},{5,4},{6,7},{7,6},{8,9},{9,8},{10,11... | collective-permute-start | bytes 1572872 | tf_op jit(solution)/shard_map/ppermute | solution.py:333
  270.8 17.0 %collective-permute-start.62 = (bf16[2,64,1536]{2,1,0:T(8,128)(2,1)S(1)}, bf16[2,64,1536]{2,1,0:T(8,128)(2,1)S(1)}, u32[]{:S(2)}, u32[]{:S(2)}) collective-permute-start(bf16[2,64,1536]{2,1,0:T(8,128)(2,1)S(1)} %pad_maximum_fusion.15), channel_id=1, source_target_pairs={{0,1},{1,0},{2,3},{3,2},{4,5},{5,4},{6,7},{7,6},{8,9},{9,8},{10,11... | collective-permute-start | bytes 1179656 | tf_op jit(solution)/shard_map/ppermute | solution.py:333
  279.5 13.0 %collective-permute-start.54 = (bf16[128,1024]{1,0:T(8,128)(2,1)S(1)}, bf16[128,1024]{1,0:T(8,128)(2,1)S(1)}, u32[]{:S(2)}, u32[]{:S(2)}) collective-permute-start(bf16[128,1024]{1,0:T(8,128)(2,1)S(1)} %pad_maximum_fusion.28), channel_id=1, source_target_pairs={{1,17},{3,19},{5,21},{7,23},{9,25},{11,27},{13,29},{15,31},{16,0},... | collective-permute-start | bytes 786440 | tf_op jit(solution)/shard_map/ppermute | solution.py:346
  284.2 13.4 %collective-permute-start.44 = (bf16[128,1024]{1,0:T(8,128)(2,1)}, bf16[128,1024]{1,0:T(8,128)(2,1)S(1)}, u32[]{:S(2)}, u32[]{:S(2)}) collective-permute-start(bf16[128,1024]{1,0:T(8,128)(2,1)} %slice.347), channel_id=1, source_target_pairs={{0,4},{2,6},{4,0},{6,2},{8,12},{10,14},{12,8},{14,10},{16,20},{18,... | collective-permute-start | bytes 786440 | tf_op jit(solution)/shard_map/ppermute | solution.py:329
  292.5 31.8 %collective-permute-start.55 = (bf16[128,1024]{1,0:T(8,128)(2,1)S(1)}, bf16[128,1024]{1,0:T(8,128)(2,1)}, u32[]{:S(2)}, u32[]{:S(2)}) collective-permute-start(bf16[128,1024]{1,0:T(8,128)(2,1)S(1)} %add_convert_fusion.10), channel_id=1, source_target_pairs={{0,1},{2,3},{4,5},{6,7},{8,9},{10,11},{12,13},{14,15},{17,16},{19,... | collective-permute-start | bytes 786440 | tf_op jit(solution)/shard_map/ppermute | solution.py:394
  303.7 14.3 %collective-permute-start.47 = (bf16[128,1024]{1,0:T(8,128)(2,1)S(1)}, bf16[128,1024]{1,0:T(8,128)(2,1)S(1)}, u32[]{:S(2)}, u32[]{:S(2)}) collective-permute-start(bf16[128,1024]{1,0:T(8,128)(2,1)S(1)} %pad_maximum_fusion.25), channel_id=1, source_target_pairs={{0,16},{2,18},{4,20},{6,22},{8,24},{10,26},{12,28},{14,30},{16,0},... | collective-permute-start | bytes 786440 | tf_op jit(solution)/shard_map/ppermute | solution.py:329
  (96 other events, 760.1 us)

commit v3 on v2

--- a/solution.py
+++ b/solution.py
@@ -357,13 +357,16 @@
     return first, swap(first, X_BIT), second, swap(second, Y_BIT)
 
 
-def gather_row_slices(own, mine):
+def gather_row_slices(own, mine, stages=False):
     rows = own.shape[0] // 2
-    held = jnp.where(mine, own, row_cross(own, False))
+    far = row_cross(own, False)
+    held = jnp.where(mine, own, far)
     first, second = held[:rows], held[rows:]
-    first = jnp.concatenate([first, swap(first, Y_BIT)])
-    second = jnp.concatenate([second, swap(second, X_BIT)])
-    return first, swap(first, X_BIT), second, swap(second, Y_BIT)
+    came_y, came_x = swap(first, Y_BIT), swap(second, X_BIT)
+    first = jnp.concatenate([first, came_y])
+    second = jnp.concatenate([second, came_x])
+    parts = first, swap(first, X_BIT), second, swap(second, Y_BIT)
+    return (parts, [far], [came_y, came_x]) if stages else parts
 
 
 def add_low(left, right):
@@ -419,16 +422,22 @@
 HB = pl.BlockSpec(memory_space=pl.ANY)
 
 
-def call(kernel, in_specs, outs, out_specs, scratch, flops, moved):
-    return pl.pallas_call(
-        kernel,
-        in_specs=in_specs,
+def call(kernel, in_specs, outs, out_specs, scratch, flops, moved, after=()):
+    held, late = len(in_specs), len(after)
+
+    def body(*refs):
+        kernel(*refs[:held], *refs[held + late :])
+
+    made = pl.pallas_call(
+        body,
+        in_specs=in_specs + [HB] * late,
         out_specs=out_specs,
         out_shape=[jax.ShapeDtypeStruct(shape, dtype) for shape, dtype in outs],
         scratch_shapes=scratch,
         compiler_params=pltpu.CompilerParams(vmem_limit_bytes=VMEM_BYTES),
         cost_estimate=pl.CostEstimate(flops=flops, bytes_accessed=moved, transcendentals=0),
     )
+    return lambda *operands: made(*operands, *after)
 
 
 def column_copies(index, parts, whole, sems, outward):
@@ -545,7 +554,7 @@
         )
 
 
-def attend(scalars, tokens, parts, tables, gains):
+def attend(scalars, tokens, parts, tables, gains, after=()):
     return call(
         attend_kernel,
         [SM, VM, VM, HB, HB, HB, HB, VM, VM, VM],
@@ -559,6 +568,7 @@
         ],
         2 * 10**9,
         8 * 10**6,
+        after,
     )(scalars, *tokens, *parts, *tables, gains)
 
 
@@ -569,7 +579,7 @@
     store_tokens(matmul(mixture[...], whole[...]), same, sibling)
 
 
-def row_product(scalars, left, parts):
+def row_product(scalars, left, parts, after=()):
     depth = left.shape[1]
     return call(
         output_kernel,
@@ -579,6 +589,7 @@
         [pltpu.VMEM((depth, 1024), LOW), pltpu.SemaphoreType.DMA((8,))],
         2 * 512 * 1024 * depth,
         4 * 10**6,
+        after,
     )(scalars, left, *parts)
 
 
@@ -597,7 +608,7 @@
         active[:, at : at + 256] = (gate * jax.nn.sigmoid(gate) * upward).astype(LOW)
 
 
-def gate_product(scalars, tokens, parts):
+def gate_product(scalars, tokens, parts, after=()):
     return call(
         gate_kernel,
         [SM, VM, VM, HB, HB, HB, HB],
@@ -606,6 +617,7 @@
         [pltpu.VMEM((1024, 1536), LOW), pltpu.SemaphoreType.DMA((16,))],
         2 * 512 * 1024 * 1536,
         10 * 10**6,
+        after,
     )(scalars, *tokens, *parts)
 
 
@@ -632,7 +644,7 @@
     store_tokens(contract_cols(grad_gate_up[...], both[...]), grad_same, grad_sibling)
 
 
-def swiglu_back(scalars, grad_out, gate_up, down_parts, gate_up_parts):
+def swiglu_back(scalars, grad_out, gate_up, down_parts, gate_up_parts, after=()):
     return call(
         swiglu_back_kernel,
         [SM, VM, VM, VM] + [HB] * 8,
@@ -646,6 +658,7 @@
         ],
         2 * 512 * 1024 * 2304,
         12 * 10**6,
+        after,
     )(scalars, *grad_out, gate_up, *down_parts, *gate_up_parts)
 
 
@@ -700,7 +713,7 @@
     grad_gains[1:2] = gain_sums[1]
 
 
-def attend_back_call(scalars, branch, parts, pre, rotated, values, log_total, tables, gains):
+def attend_back_call(scalars, branch, parts, pre, rotated, values, log_total, tables, gains, after=()):
     return call(
         attend_back_kernel,
         [SM, VM, VM, HB, HB, HB, HB] + [VM] * 7,
@@ -715,6 +728,7 @@
         ],
         2 * 10**9,
         8 * 10**6,
+        after,
     )(scalars, *branch, *parts, pre, rotated, values, log_total, *tables, gains)
 
 
@@ -725,7 +739,7 @@
     store_tokens(contract_cols(grads[...], whole[...]), same, sibling)
 
 
-def column_back(scalars, grads, parts):
+def column_back(scalars, grads, parts, after=()):
     width = grads.shape[1]
     return call(
         column_back_kernel,
@@ -735,6 +749,7 @@
         [pltpu.VMEM((1024, width), LOW), pltpu.SemaphoreType.DMA((16,))],
         2 * 512 * 1024 * width,
         5 * 10**6,
+        after,
     )(scalars, grads, *parts)
 
 
@@ -754,7 +769,7 @@
     wait_all(copies)
 
 
-def column_grad(scalars, tokens, grads):
+def column_grad(scalars, tokens, grads, after=()):
     width = grads.shape[1]
     return call(
         column_grad_kernel,
@@ -764,6 +779,7 @@
         [pltpu.VMEM((1024, width), LOW), pltpu.SemaphoreType.DMA((16,))],
         2 * 512 * 1024 * width,
         6 * 10**6,
+        after,
     )(scalars, *tokens, grads)
 
 
@@ -779,7 +795,7 @@
     wait_all(copies)
 
 
-def row_grad(scalars, left, tokens):
+def row_grad(scalars, left, tokens, after=()):
     depth = left.shape[1]
     return call(
         row_grad_kernel,
@@ -789,6 +805,7 @@
         [pltpu.VMEM((depth, 1024), LOW), pltpu.SemaphoreType.DMA((8,))],
         2 * 512 * 1024 * depth,
         4 * 10**6,
+        after,
     )(scalars, left, *tokens)
 
 
@@ -852,7 +869,7 @@
     gate_up_parts = gather_column_slices(
         column_pack(gate_up, slice_own), column_pack(gate_up, slice_give)
     )
-    down_parts = gather_row_slices(w_down.astype(LOW), mine)
+    down_parts, _, down_first = gather_row_slices(w_down.astype(LOW), mine, True)
 
     tokens_own = hidden_in[0]
     count = tokens_own.shape[0]
@@ -871,32 +888,32 @@
     mixed_low, pre, rotated, value_low, log_total = attend(
         scalars, normed, qkv_parts, tables, head_gains
     )
-    attended = sum_tokens(*row_product(scalars, mixed_low, output_parts))
+    attended = sum_tokens(*row_product(scalars, mixed_low, output_parts, down_first))
     middle = tokens_f + attended
     normed_two_f, norm_two_pull = jax.vjp(rms_norm, middle, gain_mlp)
     normed_two = gather_tokens(normed_two_f.astype(LOW))
-    gate_up_act, active = gate_product(scalars, normed_two, gate_up_parts)
-    grad_down = row_grad(scalars, active, grad_out)
+    gate_up_act, active = gate_product(scalars, normed_two, gate_up_parts, down_parts)
     grad_gate_up, back_same, back_sibling = swiglu_back(
         scalars, grad_out, gate_up_act, down_parts, gate_up_parts
     )
+    grad_down = row_grad(scalars, active, grad_out, [back_same])
     grad_normed_two = sum_tokens(back_same, back_sibling)
-    grad_gate_up_mat = column_grad(scalars, normed_two, grad_gate_up)
-    layer_sum = sum_tokens(*row_product(scalars, active, down_parts))
-    layer_out = (middle + layer_sum).astype(LOW)[None]
+    grad_gate_up_mat = column_grad(scalars, normed_two, grad_gate_up, [back_same])
 
     grad_middle_norm, grad_gain_mlp = norm_two_pull(grad_normed_two)
     grad_middle = cotangent[0].astype(WIDE) + grad_middle_norm
     grad_branch = gather_tokens(grad_middle.astype(LOW))
-    grad_output_mat = row_grad(scalars, mixed_low, grad_branch)
     grad_qkv, grad_head_gains = attend_back_call(
         scalars, grad_branch, output_parts, pre, rotated, value_low, log_total, tables, head_gains
     )
-    grad_qkv_mat = column_grad(scalars, normed, grad_qkv)
-    grad_normed = sum_tokens(*column_back(scalars, grad_qkv, qkv_parts))
+    grad_qkv_mat = column_grad(scalars, normed, grad_qkv, ())
+    grad_output_mat = row_grad(scalars, mixed_low, grad_branch, [grad_qkv_mat[0]])
+    grad_normed = sum_tokens(*column_back(scalars, grad_qkv, qkv_parts, [grad_qkv_mat[0]]))
     grad_tokens_norm, grad_gain_attn = norm_pull(grad_normed)
     input_grad = (grad_middle + grad_tokens_norm).astype(LOW)[None]
 
+    layer_sum = sum_tokens(*row_product(scalars, active, down_parts, [grad_qkv_mat[0]]))
+    layer_out = (middle + layer_sum).astype(LOW)[None]
     grad_gains = jnp.concatenate([grad_gain_attn, grad_gain_mlp, grad_head_gains[:2].reshape(-1)])
     grad_gains = grad_gains.reshape(16, -1)
     grad_gains = grad_gains + swap_core(grad_gains.astype(LOW)).astype(WIDE)

time: 331 us -> 316 us (0.955)
  waiting for transfers between devices: 140 us -> 116 us
  other arithmetic: 23 us -> 27.7 us
    ppermute x2, waiting for transfers between devices: 12.9 us -> 0.51 us  [scatter_row_slices(): return jnp.where(mine, summed, lax.ppermute(summed, ('dp', 'ctx'), pairs))]
    ppermute x4, waiting for transfers between devices: 14.3 us -> 4.52 us  [row_cross(): return lax.ppermute(values, ('dp', 'ctx'), pairs)]
    ppermute x11, starting transfers between devices: 23.7 us -> 28.8 us  [swap_core(): return lax.ppermute(values, 'ctx', [(0, 1), (1, 0)])]
    ppermute x57, starting transfers between devices: 50.3 us -> 46.6 us  [swap(): return lax.ppermute(values, 'dp', [(i, i ^ bit) for i in range(16)])]
    unnamed x108 -> x164, local copies, waits for them, and re-layouts: 4.46 us -> 7.94 us
  transfers between devices with their start and end apart: 74 -> 74, of which waited for: 37 -> 22; matrix products, arithmetic and copies ran while one was open for 8% -> 10% of each run, Pallas kernels for 16% -> 16%
where the time goes in v3:
time: 316 us
  waiting for transfers between devices  116 us (37%)
  starting transfers between devices  87.7 us (28%)
  Pallas kernels  65.6 us (21%)
  other arithmetic  27.7 us (9%)
  local copies, waits for them, and re-layouts  15.8 us (5%)
    ppermute x57, waiting for transfers between devices, swap(): return lax.ppermute(values, 'dp', [(i, i ^ bit) for i in range(16)])  110 us
    pallas_call x11, Pallas kernels, call(): return lambda *operands: made(*operands, *after)  65.6 us
    ppermute x57, starting transfers between devices, swap(): return lax.ppermute(values, 'dp', [(i, i ^ bit) for i in range(16)])  46.6 us
    ppermute x11, starting transfers between devices, swap_core(): return lax.ppermute(values, 'ctx', [(0, 1), (1, 0)])  28.8 us
    add x8, other arithmetic, lion_step(): new_moments.append(BETA_TWO * moment_arr + (1.0 - BETA_TWO) * scaled)  10.1 us
    ppermute x4, starting transfers between devices, row_cross(): return lax.ppermute(values, ('dp', 'ctx'), pairs)  9.42 us
    unnamed x164, local copies, waits for them, and re-layouts  7.94 us
  transfers between devices with their start and end apart: 74, of which 22 were waited for; matrix products, arithmetic and copies ran while one was open for 10% of the time, Pallas kernels for 16%

profile of v3, /device:TPU:1, one launch (start us, length us, event | category | flops | bytes accessed | tf_op | source)
XLA Modules:
  0.0 315.6 jit_solution(17358605182367257032)
XLA Ops:
  15.3 3.8 %collective-permute-start.2 = (bf16[2,144]{1,0:T(2,128)(2,1)S(1)}, bf16[2,144]{1,0:T(2,128)(2,1)S(1)}, u32[]{:S(2)}, u32[]{:S(2)}) collective-permute-start(bf16[2,144]{1,0:T(2,128)(2,1)S(1)} %pad_maximum_fusion.37), channel_id=1, source_target_pairs={{0,16},{2,18},{4,20},{6,22},{8,24},{10,26},{12,28},{14,30},{16,0},... | collective-permute-start | bytes 1736 | tf_op jit(solution)/shard_map/ppermute | solution.py:329
  19.2 8.8 %collective-permute-done.2 = bf16[2,144]{1,0:T(2,128)(2,1)S(1)} collective-permute-done((bf16[2,144]{1,0:T(2,128)(2,1)S(1)}, bf16[2,144]{1,0:T(2,128)(2,1)S(1)}, u32[]{:S(2)}, u32[]{:S(2)}) %collective-permute-start.2) | collective-permute-done | bytes 608 | tf_op jit(solution)/shard_map/ppermute | solution.py:329
  37.3 3.6 %collective-permute-done.5 = bf16[128,1024]{1,0:T(8,128)(2,1)S(1)} collective-permute-done((bf16[128,1024]{1,0:T(8,128)(2,1)S(1)}, bf16[128,1024]{1,0:T(8,128)(2,1)S(1)}, u32[]{:S(2)}, u32[]{:S(2)}) %collective-permute-start.5) | collective-permute-done | bytes 262176 | tf_op jit(solution)/shard_map/ppermute | solution.py:329
  41.0 7.5 %collective-permute-start.6 = (bf16[2,128,1024]{2,1,0:T(8,128)(2,1)S(1)}, bf16[2,128,1024]{2,1,0:T(8,128)(2,1)S(1)}, u32[]{:S(2)}, u32[]{:S(2)}) collective-permute-start(bf16[2,128,1024]{2,1,0:T(8,128)(2,1)S(1)} %pad_maximum_fusion.2.refs_1_), channel_id=1, source_target_pairs={{0,1},{1,0},{2,3},{3,2},{4,5},{5,4},{6,7},{7,6},{8,9},{9,8},{10,11... | collective-permute-start | bytes 1572872 | tf_op jit(solution)/shard_map/ppermute | solution.py:333
  52.3 3.2 %collective-permute-done.11 = bf16[128,1024]{1,0:T(8,128)(2,1)S(1)} collective-permute-done((bf16[128,1024]{1,0:T(8,128)(2,1)S(1)}, bf16[128,1024]{1,0:T(8,128)(2,1)S(1)}, u32[]{:S(2)}, u32[]{:S(2)}) %collective-permute-start.11) | collective-permute-done | bytes 262176 | tf_op jit(solution)/shard_map/ppermute | solution.py:329
  59.1 10.6 %collective-permute-done.19.refs_6_ = bf16[96,1024]{1,0:T(8,128)(2,1)S(1)} collective-permute-done((bf16[96,1024]{1,0:T(8,128)(2,1)S(1)}, bf16[96,1024]{1,0:T(8,128)(2,1)S(1)}, u32[]{:S(2)}, u32[]{:S(2)}) %collective-permute-start.19) | collective-permute-done | bytes 196640 | tf_op jit(solution)/shard_map/ppermute | solution.py:329
  71.5 8.1 %shard_map.331 = (bf16[512,512]{1,0:T(8,128)(2,1)S(1)}, f32[512,768]{1,0:T(8,128)}, bf16[512,768]{1,0:T(8,128)(2,1)S(1)}, bf16[512,256]{1,0:T(8,128)(2,1)S(1)}, f32[512,128]{1,0:T(8,128)S(1)}) custom-call(s32[9]{0:T(128)S(1)} %pad_add_fusion.1.refs_0_, bf16[2,128,1024]{2,1,0:T(8,128)(2,1)S(1)} %pad_maximum_fusion.2.refs_1_, ...), custom_call_target="tpu_custom_call" | custom-call | flops 2000000000 | bytes 8000000 | tf_op jit(solution)/shard_map/pallas_call | solution.py:440
  81.6 2.7 shard_map.332
  84.4 6.9 %collective-permute-start.21 = (bf16[2,128,1024]{2,1,0:T(8,128)(2,1)S(1)}, bf16[2,128,1024]{2,1,0:T(8,128)(2,1)S(1)}, u32[]{:S(2)}, u32[]{:S(2)}) collective-permute-start(bf16[2,128,1024]{2,1,0:T(8,128)(2,1)S(1)} %get-tuple-element.54), channel_id=1, source_target_pairs={{0,1},{1,0},{2,3},{3,2},{4,5},{5,4},{6,7},{7,6},{8,9},{9,8},{10,11... | collective-permute-start | bytes 1572872 | tf_op jit(solution)/shard_map/ppermute | solution.py:333
  96.0 6.1 %collective-permute-done.29 = bf16[128,1536]{1,0:T(8,128)(2,1)S(1)} collective-permute-done((bf16[128,1536]{1,0:T(8,128)(2,1)S(1)}, bf16[128,1536]{1,0:T(8,128)(2,1)S(1)}, u32[]{:S(2)}, u32[]{:S(2)}) %collective-permute-start.29) | collective-permute-done | bytes 393248 | tf_op jit(solution)/shard_map/ppermute | solution.py:329
  106.3 4.8 %collective-permute-done.23 = bf16[128,1024]{1,0:T(8,128)(2,1)S(1)} collective-permute-done((bf16[128,1024]{1,0:T(8,128)(2,1)S(1)}, bf16[128,1024]{1,0:T(8,128)(2,1)S(1)}, u32[]{:S(2)}, u32[]{:S(2)}) %collective-permute-start.23) | collective-permute-done | bytes 262176 | tf_op jit(solution)/shard_map/ppermute | solution.py:329
  113.8 16.8 %collective-permute-done.32.refs_10_.refs_7_.refs_5_ = bf16[192,1024]{1,0:T(8,128)(2,1)S(1)} collective-permute-done((bf16[192,1024]{1,0:T(8,128)(2,1)S(1)}, bf16[192,1024]{1,0:T(8,128)(2,1)S(1)}, u32[]{:S(2)}, u32[]{:S(2)}) %collective-permute-start.32) | collective-permute-done | bytes 393248 | tf_op jit(solution)/shard_map/ppermute | solution.py:329
  131.4 8.4 %shard_map.333 = (f32[512,1536]{1,0:T(8,128)}, bf16[512,768]{1,0:T(8,128)(2,1)S(1)}) custom-call(s32[9]{0:T(128)S(1)} %pad_add_fusion.1.refs_0_, bf16[2,128,1024]{2,1,0:T(8,128)(2,1)S(1)} %pad_maximum_fusion.5.refs_1_, bf16[2,128,1024]{2,1,0:T(8,128)(2,1)S(1)} %collective-permute-done.24.refs_2_, bf16[256,1536]{1,0:T(8,128)(2,1)S(1)} %pad_maximum_fusion.refs_3_.refs_8_, ...), custom_call_target="tpu_custom_call" | custom-call | flops 1610612736 | bytes 10000000 | tf_op jit(solution)/shard_map/pallas_call | solution.py:440
  139.9 11.1 %shard_map.334 = (bf16[512,1536]{1,0:T(8,128)(2,1)}, bf16[2,128,1024]{2,1,0:T(8,128)(2,1)S(1)}, bf16[2,128,1024]{2,1,0:T(8,128)(2,1)S(1)}) custom-call(s32[9]{0:T(128)S(1)} %pad_add_fusion.1.refs_0_, bf16[2,128,1024]{2,1,0:T(8,128)(2,1)S(1)} %pad_maximum_fusion.6.refs_1_.refs_2_, bf16[2,128,1024]{2,1,0:T(8,128)(2,1)S(1)} %collective-permute-done.34.refs_2_.refs_3_, ...), custom_call_target="tpu_custom_call" | custom-call | flops 2415919104 | bytes 12000000 | tf_op jit(solution)/shard_map/pallas_call | solution.py:440
  151.1 3.4 %shard_map.341 = (bf16[192,1024]{1,0:T(8,128)(2,1)S(1)}, bf16[192,1024]{1,0:T(8,128)(2,1)}, bf16[192,1024]{1,0:T(8,128)(2,1)S(1)}, bf16[192,1024]{1,0:T(8,128)(2,1)S(1)}) custom-call(s32[9]{0:T(128)S(1)} %pad_add_fusion.1.refs_0_, bf16[512,768]{1,0:T(8,128)(2,1)S(1)} %get-tuple-element.55.refs_1_, ...), custom_call_target="tpu_custom_call" | custom-call | flops 805306368 | bytes 4000000 | tf_op jit(solution)/shard_map/pallas_call | solution.py:440
  160.7 7.7 %shard_map.340 = (bf16[256,1536]{1,0:T(8,128)(2,1)S(1)}, bf16[256,1536]{1,0:T(8,128)(2,1)S(1)}, bf16[256,1536]{1,0:T(8,128)(2,1)S(1)}, bf16[256,1536]{1,0:T(8,128)(2,1)S(1)}) custom-call(s32[9]{0:T(128)S(1)} %pad_add_fusion.1.refs_0_, bf16[2,128,1024]{2,1,0:T(8,128)(2,1)S(1)} %pad_maximum_fusion.5.refs_1_, bf16[2,128,1024]{2,1,0:T(8,128)(2,1)S(1)} %copy-done.21, ...), custom_call_target="tpu_custom_call" | custom-call | flops 1610612736 | bytes 6000000 | tf_op jit(solution)/shard_map/pallas_call | solution.py:440
  174.3 18.6 %collective-permute-done.64 = bf16[96,1024]{1,0:T(8,128)(2,1)S(1)} collective-permute-done((bf16[96,1024]{1,0:T(8,128)(2,1)S(1)}, bf16[96,1024]{1,0:T(8,128)(2,1)S(1)}, u32[]{:S(2)}, u32[]{:S(2)}) %collective-permute-start.64) | collective-permute-done | bytes 196640 | tf_op jit(solution)/shard_map/ppermute | solution.py:329
  193.1 3.5 %collective-permute-start.67 = (bf16[192,1024]{1,0:T(8,128)(2,1)S(1)}, bf16[192,1024]{1,0:T(8,128)(2,1)S(1)}, u32[]{:S(2)}, u32[]{:S(2)}) collective-permute-start(bf16[192,1024]{1,0:T(8,128)(2,1)S(1)} %pad_maximum_fusion.18), channel_id=1, source_target_pairs={{1,17},{3,19},{5,21},{7,23},{9,25},{11,27},{13,29},{15,31},{16,0},... | collective-permute-start | bytes 1179656 | tf_op jit(solution)/shard_map/ppermute | solution.py:346
  199.8 4.5 %collective-permute-done.67 = bf16[192,1024]{1,0:T(8,128)(2,1)S(1)} collective-permute-done((bf16[192,1024]{1,0:T(8,128)(2,1)S(1)}, bf16[192,1024]{1,0:T(8,128)(2,1)S(1)}, u32[]{:S(2)}, u32[]{:S(2)}) %collective-permute-start.67) | collective-permute-done | bytes 393248 | tf_op jit(solution)/shard_map/ppermute | solution.py:346
  205.7 4.1 %collective-permute-done.37 = bf16[128,1024]{1,0:T(8,128)(2,1)S(1)} collective-permute-done((bf16[128,1024]{1,0:T(8,128)(2,1)S(1)}, bf16[128,1024]{1,0:T(8,128)(2,1)S(1)}, u32[]{:S(2)}, u32[]{:S(2)}) %collective-permute-start.37) | collective-permute-done | bytes 262176 | tf_op jit(solution)/shard_map/ppermute | solution.py:329
  213.8 8.0 %shard_map.335 = (bf16[512,1024]{1,0:T(8,128)(2,1)S(1)}, f32[8,128]{1,0:T(8,128)S(1)}) custom-call(s32[9]{0:T(128)S(1)} %pad_add_fusion.1.refs_0_, bf16[2,128,1024]{2,1,0:T(8,128)(2,1)S(1)} %pad_maximum_fusion.7.refs_1_.refs_2_, bf16[2,128,1024]{2,1,0:T(8,128)(2,1)S(1)} %collective-permute-done.38.refs_2_.refs_3_, bf16[128,1024]{1,0:T(8,128)(2,1)S(1)} %copy-done.9, ...), custom_call_target="tpu_custom_call" | custom-call | flops 2000000000 | bytes 8000000 | tf_op jit(solution)/shard_map/pallas_call | solution.py:440
  221.9 4.9 %shard_map.336 = (bf16[256,1024]{1,0:T(8,128)(2,1)S(1)}, bf16[256,1024]{1,0:T(8,128)(2,1)S(1)}, bf16[256,1024]{1,0:T(8,128)(2,1)S(1)}, bf16[256,1024]{1,0:T(8,128)(2,1)S(1)}) custom-call(s32[9]{0:T(128)S(1)} %pad_add_fusion.1.refs_0_, bf16[2,128,1024]{2,1,0:T(8,128)(2,1)S(1)} %pad_maximum_fusion.2.refs_1_, bf16[2,128,1024]{2,1,0:T(8,128)(2,1)S(1)} %copy-done.17, ...), custom_call_target="tpu_custom_call" | custom-call | flops 1073741824 | bytes 6000000 | tf_op jit(solution)/shard_map/pallas_call | solution.py:440
  226.8 2.7 shard_map.339
  232.5 3.7 %shard_map.337 = (bf16[2,128,1024]{2,1,0:T(8,128)(2,1)S(1)}, bf16[2,128,1024]{2,1,0:T(8,128)(2,1)S(1)}) custom-call(s32[9]{0:T(128)S(1)} %pad_add_fusion.1.refs_0_, bf16[512,768]{1,0:T(8,128)(2,1)S(1)} %copy-done.33, bf16[192,1024]{1,0:T(8,128)(2,1)S(1)} %pad_maximum_fusion.12.refs_7_.refs_4_.refs_2_, bf16[192,1024]{1,0:T(8,128)(2,1)S(1)} %copy-done.24, ...), custom_call_target="tpu_custom_call" | custom-call | flops 805306368 | bytes 4000000 | tf_op jit(solution)/shard_map/pallas_call | solution.py:440
  236.2 4.9 %shard_map.338 = (bf16[2,128,1024]{2,1,0:T(8,128)(2,1)S(1)}, bf16[2,128,1024]{2,1,0:T(8,128)(2,1)S(1)}) custom-call(s32[9]{0:T(128)S(1)} %pad_add_fusion.1.refs_0_, bf16[512,1024]{1,0:T(8,128)(2,1)S(1)} %get-tuple-element.63.refs_3_.refs_1_, bf16[256,1024]{1,0:T(8,128)(2,1)S(1)} %pad_maximum_fusion.3.refs_3_.refs_2_, bf16[256,1024]{1,0:T(8,128)(2,1)S(1)} %copy-done.19, ...), custom_call_target="tpu_custom_call" | custom-call | flops 1073741824 | bytes 5000000 | tf_op jit(solution)/shard_map/pallas_call | solution.py:440
  241.3 5.2 %collective-permute-done.61 = bf16[64,1536]{1,0:T(8,128)(2,1)S(1)} collective-permute-done((bf16[64,1536]{1,0:T(8,128)(2,1)S(1)}, bf16[64,1536]{1,0:T(8,128)(2,1)S(1)}, u32[]{:S(2)}, u32[]{:S(2)}) %collective-permute-start.61) | collective-permute-done | bytes 196640 | tf_op jit(solution)/shard_map/ppermute | solution.py:329
  249.3 4.3 %collective-permute-done.51 = bf16[64,1024]{1,0:T(8,128)(2,1)S(1)} collective-permute-done((bf16[64,1024]{1,0:T(8,128)(2,1)S(1)}, bf16[64,1024]{1,0:T(8,128)(2,1)S(1)}, u32[]{:S(2)}, u32[]{:S(2)}) %collective-permute-start.51) | collective-permute-done | bytes 131104 | tf_op jit(solution)/shard_map/ppermute | solution.py:329
  253.7 3.6 %collective-permute-done.53 = bf16[64,1024]{1,0:T(8,128)(2,1)S(1)} collective-permute-done((bf16[64,1024]{1,0:T(8,128)(2,1)S(1)}, bf16[64,1024]{1,0:T(8,128)(2,1)S(1)}, u32[]{:S(2)}, u32[]{:S(2)}) %collective-permute-start.53) | collective-permute-done | bytes 131104 | tf_op jit(solution)/shard_map/ppermute | solution.py:329
  260.0 3.3 %collective-permute-start.54 = (bf16[128,1024]{1,0:T(8,128)(2,1)S(1)}, bf16[128,1024]{1,0:T(8,128)(2,1)S(1)}, u32[]{:S(2)}, u32[]{:S(2)}) collective-permute-start(bf16[128,1024]{1,0:T(8,128)(2,1)S(1)} %pad_maximum_fusion.28), channel_id=1, source_target_pairs={{1,17},{3,19},{5,21},{7,23},{9,25},{11,27},{13,29},{15,31},{16,0},... | collective-permute-start | bytes 786440 | tf_op jit(solution)/shard_map/ppermute | solution.py:346
  284.3 11.2 %collective-permute-done.71 = bf16[16,144]{1,0:T(8,128)(2,1)S(1)} collective-permute-done((bf16[16,144]{1,0:T(8,128)(2,1)S(1)}, bf16[16,144]{1,0:T(8,128)(2,1)S(1)}, u32[]{:S(2)}, u32[]{:S(2)}) %collective-permute-start.71) | collective-permute-done | bytes 4640 | tf_op jit(solution)/shard_map/ppermute | solution.py:329
  302.6 3.2 %collective-permute-done.48 = bf16[64,1024]{1,0:T(8,128)(2,1)S(1)} collective-permute-done((bf16[64,1024]{1,0:T(8,128)(2,1)S(1)}, bf16[64,1024]{1,0:T(8,128)(2,1)S(1)}, u32[]{:S(2)}, u32[]{:S(2)}) %collective-permute-start.48) | collective-permute-done | bytes 131104 | tf_op jit(solution)/shard_map/ppermute | solution.py:329
  305.8 3.6 %collective-permute-start.49 = (bf16[2,64,1024]{2,1,0:T(8,128)(2,1)S(1)}, bf16[2,64,1024]{2,1,0:T(8,128)(2,1)S(1)}, u32[]{:S(2)}, u32[]{:S(2)}) collective-permute-start(bf16[2,64,1024]{2,1,0:T(8,128)(2,1)S(1)} %pad_maximum_fusion.26), channel_id=1, source_target_pairs={{0,1},{1,0},{2,3},{3,2},{4,5},{5,4},{6,7},{7,6},{8,9},{9,8},{10,11... | collective-permute-start | bytes 786440 | tf_op jit(solution)/shard_map/ppermute | solution.py:333
  (451 shorter events, 110.0 us)
Async XLA Ops:
  6.2 28.3 %collective-permute-start.7 = (bf16[64,1024]{1,0:T(8,128)(2,1)}, bf16[64,1024]{1,0:T(8,128)(2,1)S(1)}, u32[]{:S(2)}, u32[]{:S(2)}) collective-permute-start(bf16[64,1024]{1,0:T(8,128)(2,1)} %pad_maximum_fusion.30), channel_id=1, source_target_pairs={{0,8},{2,10},{4,12},{6,14},{8,0},{10,2},{12,4},{14,6},{16,24},{18,... | collective-permute-start | bytes 393224 | tf_op jit(solution)/shard_map/ppermute | solution.py:329
  8.8 25.9 %collective-permute-start.13 = (bf16[128,1024]{1,0:T(8,128)(2,1)S(1)}, bf16[128,1024]{1,0:T(8,128)(2,1)S(1)}, u32[]{:S(2)}, u32[]{:S(2)}) collective-permute-start(bf16[128,1024]{1,0:T(8,128)(2,1)S(1)} %convert_element_type.387), channel_id=1, source_target_pairs={{0,16},{2,18},{4,20},{6,22},{8,24},{10,26},{12,28},{14,30},{17,1},... | collective-permute-start | bytes 786440 | tf_op jit(solution)/shard_map/ppermute | solution.py:346
  11.4 23.2 %collective-permute-start.25 = (bf16[64,1536]{1,0:T(8,128)(2,1)S(1)}, bf16[64,1536]{1,0:T(8,128)(2,1)S(1)}, u32[]{:S(2)}, u32[]{:S(2)}) collective-permute-start(bf16[64,1536]{1,0:T(8,128)(2,1)S(1)} %pad_maximum_fusion.29), channel_id=1, source_target_pairs={{0,8},{2,10},{4,12},{6,14},{8,0},{10,2},{12,4},{14,6},{16,24},{18,... | collective-permute-start | bytes 589832 | tf_op jit(solution)/shard_map/ppermute | solution.py:329
  14.0 35.9 %collective-permute-start.18 = (bf16[192,1024]{1,0:T(8,128)(2,1)}, bf16[192,1024]{1,0:T(8,128)(2,1)}, u32[]{:S(2)}, u32[]{:S(2)}) collective-permute-start(bf16[192,1024]{1,0:T(8,128)(2,1)} %convert_element_type.388), channel_id=1, source_target_pairs={{0,16},{2,18},{4,20},{6,22},{8,24},{10,26},{12,28},{14,30},{17,1},... | collective-permute-start | bytes 1179656 | tf_op jit(solution)/shard_map/ppermute | solution.py:346
  34.8 22.4 %collective-permute-start.16 = (bf16[64,1024]{1,0:T(8,128)(2,1)S(1)}, bf16[64,1024]{1,0:T(8,128)(2,1)S(1)}, u32[]{:S(2)}, u32[]{:S(2)}) collective-permute-start(bf16[64,1024]{1,0:T(8,128)(2,1)S(1)} %get-tuple-element.146), channel_id=1, source_target_pairs={{0,2},{2,0},{4,6},{6,4},{8,10},{10,8},{12,14},{14,12},{16,18},{18,... | collective-permute-start | bytes 393224 | tf_op jit(solution)/shard_map/ppermute | solution.py:329
  36.1 22.5 %collective-permute-start.14 = (bf16[64,1024]{1,0:T(8,128)(2,1)S(1)}, bf16[64,1024]{1,0:T(8,128)(2,1)S(1)}, u32[]{:S(2)}, u32[]{:S(2)}) collective-permute-start(bf16[64,1024]{1,0:T(8,128)(2,1)S(1)} %get-tuple-element.147), channel_id=1, source_target_pairs={{0,4},{2,6},{4,0},{6,2},{8,12},{10,14},{12,8},{14,10},{16,20},{18,... | collective-permute-start | bytes 393224 | tf_op jit(solution)/shard_map/ppermute | solution.py:329
  41.0 29.9 %collective-permute-start.6 = (bf16[2,128,1024]{2,1,0:T(8,128)(2,1)S(1)}, bf16[2,128,1024]{2,1,0:T(8,128)(2,1)S(1)}, u32[]{:S(2)}, u32[]{:S(2)}) collective-permute-start(bf16[2,128,1024]{2,1,0:T(8,128)(2,1)S(1)} %pad_maximum_fusion.2.refs_1_), channel_id=1, source_target_pairs={{0,1},{1,0},{2,3},{3,2},{4,5},{5,4},{6,7},{7,6},{8,9},{9,8},{10,11... | collective-permute-start | bytes 1572872 | tf_op jit(solution)/shard_map/ppermute | solution.py:333
  55.6 15.5 %collective-permute-start.12 = (bf16[256,1024]{1,0:T(8,128)(2,1)S(1)}, bf16[256,1024]{1,0:T(8,128)(2,1)S(1)}, u32[]{:S(2)}, u32[]{:S(2)}) collective-permute-start(bf16[256,1024]{1,0:T(8,128)(2,1)S(1)} %pad_maximum_fusion.4.refs_5_.refs_4_), channel_id=1, source_target_pairs={{0,4},{2,6},{4,0},{6,2},{8,12},{10,14},{12,8},{14,10},{16,20},{18,... | collective-permute-start | bytes 1572872 | tf_op jit(solution)/shard_map/ppermute | solution.py:329
  58.6 32.7 %collective-permute-start.26 = (bf16[128,1536]{1,0:T(8,128)(2,1)S(1)}, bf16[128,1536]{1,0:T(8,128)(2,1)S(1)}, u32[]{:S(2)}, u32[]{:S(2)}) collective-permute-start(bf16[128,1536]{1,0:T(8,128)(2,1)S(1)} %pad_maximum_fusion.8), channel_id=1, source_target_pairs={{0,16},{2,18},{4,20},{6,22},{8,24},{10,26},{12,28},{14,30},{16,0},... | collective-permute-start | bytes 1179656 | tf_op jit(solution)/shard_map/ppermute | solution.py:329
  71.4 41.8 %collective-permute-start.33 = (bf16[128,1024]{1,0:T(8,128)(2,1)S(1)}, bf16[128,1024]{1,0:T(8,128)(2,1)S(1)}, u32[]{:S(2)}, u32[]{:S(2)}) collective-permute-start(bf16[128,1024]{1,0:T(8,128)(2,1)S(1)} %bitcast.128), channel_id=1, source_target_pairs={{0,8},{2,10},{4,12},{6,14},{8,0},{10,2},{12,4},{14,6},{16,24},{18,... | collective-permute-start | bytes 786440 | tf_op jit(solution)/shard_map/ppermute | solution.py:329
  80.4 33.0 %collective-permute-start.31 = (bf16[192,1024]{1,0:T(8,128)(2,1)S(1)}, bf16[192,1024]{1,0:T(8,128)(2,1)S(1)}, u32[]{:S(2)}, u32[]{:S(2)}) collective-permute-start(bf16[192,1024]{1,0:T(8,128)(2,1)S(1)} %pad_maximum_fusion.12.refs_7_.refs_4_.refs_2_), channel_id=1, source_target_pairs={{0,2},{2,0},{4,6},{6,4},{8,10},{10,8},{12,14},{14,12},{16,18},{18,... | collective-permute-start | bytes 1179656 | tf_op jit(solution)/shard_map/ppermute | solution.py:329
  102.2 28.3 %collective-permute-start.30 = (bf16[256,1536]{1,0:T(8,128)(2,1)S(1)}, bf16[256,1536]{1,0:T(8,128)(2,1)S(1)}, u32[]{:S(2)}, u32[]{:S(2)}) collective-permute-start(bf16[256,1536]{1,0:T(8,128)(2,1)S(1)} %pad_maximum_fusion.1.refs_5_.refs_10_), channel_id=1, source_target_pairs={{0,4},{2,6},{4,0},{6,2},{8,12},{10,14},{12,8},{14,10},{16,20},{18,... | collective-permute-start | bytes 2359304 | tf_op jit(solution)/shard_map/ppermute | solution.py:329
  105.6 24.9 %collective-permute-start.28 = (bf16[256,1536]{1,0:T(8,128)(2,1)S(1)}, bf16[256,1536]{1,0:T(8,128)(2,1)S(1)}, u32[]{:S(2)}, u32[]{:S(2)}) collective-permute-start(bf16[256,1536]{1,0:T(8,128)(2,1)S(1)} %pad_maximum_fusion.refs_3_.refs_8_), channel_id=1, source_target_pairs={{0,2},{2,0},{4,6},{6,4},{8,10},{10,8},{12,14},{14,12},{16,18},{18,... | collective-permute-start | bytes 2359304 | tf_op jit(solution)/shard_map/ppermute | solution.py:329
  111.1 19.4 %collective-permute-start.24 = (bf16[2,128,1024]{2,1,0:T(8,128)(2,1)S(1)}, bf16[2,128,1024]{2,1,0:T(8,128)(2,1)S(1)}, u32[]{:S(2)}, u32[]{:S(2)}) collective-permute-start(bf16[2,128,1024]{2,1,0:T(8,128)(2,1)S(1)} %pad_maximum_fusion.5.refs_1_), channel_id=1, source_target_pairs={{0,1},{1,0},{2,3},{3,2},{4,5},{5,4},{6,7},{7,6},{8,9},{9,8},{10,11... | collective-permute-start | bytes 1572872 | tf_op jit(solution)/shard_map/ppermute | solution.py:333
  113.2 17.3 %collective-permute-start.32 = (bf16[192,1024]{1,0:T(8,128)(2,1)S(1)}, bf16[192,1024]{1,0:T(8,128)(2,1)S(1)}, u32[]{:S(2)}, u32[]{:S(2)}) collective-permute-start(bf16[192,1024]{1,0:T(8,128)(2,1)S(1)} %pad_maximum_fusion.13.refs_9_.refs_6_.refs_4_), channel_id=1, source_target_pairs={{0,4},{2,6},{4,0},{6,2},{8,12},{10,14},{12,8},{14,10},{16,20},{18,... | collective-permute-start | bytes 1179656 | tf_op jit(solution)/shard_map/ppermute | solution.py:329
  113.4 26.5 %collective-permute-start.34 = (bf16[2,128,1024]{2,1,0:T(8,128)(2,1)S(1)}, bf16[2,128,1024]{2,1,0:T(8,128)(2,1)S(1)}, u32[]{:S(2)}, u32[]{:S(2)}) collective-permute-start(bf16[2,128,1024]{2,1,0:T(8,128)(2,1)S(1)} %pad_maximum_fusion.6.refs_1_.refs_2_), channel_id=1, source_target_pairs={{0,1},{1,0},{2,3},{3,2},{4,5},{5,4},{6,7},{7,6},{8,9},{9,8},{10,11... | collective-permute-start | bytes 1572872 | tf_op jit(solution)/shard_map/ppermute | solution.py:333
  156.7 15.9 %collective-permute-start.65 = (bf16[192,1024]{1,0:T(8,128)(2,1)}, bf16[192,1024]{1,0:T(8,128)(2,1)S(1)}, u32[]{:S(2)}, u32[]{:S(2)}) collective-permute-start(bf16[192,1024]{1,0:T(8,128)(2,1)} %copy-done.27), channel_id=1, source_target_pairs={{0,4},{2,6},{4,0},{6,2},{8,12},{10,14},{12,8},{14,10},{16,20},{18,... | collective-permute-start | bytes 1179656 | tf_op jit(solution)/shard_map/ppermute | solution.py:329
  168.5 30.2 %collective-permute-start.56 = (bf16[256,1536]{1,0:T(8,128)(2,1)S(1)}, bf16[256,1536]{1,0:T(8,128)(2,1)S(1)}, u32[]{:S(2)}, u32[]{:S(2)}) collective-permute-start(bf16[256,1536]{1,0:T(8,128)(2,1)S(1)} %get-tuple-element.78), channel_id=1, source_target_pairs={{0,2},{2,0},{4,6},{6,4},{8,10},{10,8},{12,14},{14,12},{16,18},{18,... | collective-permute-start | bytes 2359304 | tf_op jit(solution)/shard_map/ppermute | solution.py:329
  169.9 29.3 %collective-permute-start.58 = (bf16[256,1536]{1,0:T(8,128)(2,1)S(1)}, bf16[256,1536]{1,0:T(8,128)(2,1)S(1)}, u32[]{:S(2)}, u32[]{:S(2)}) collective-permute-start(bf16[256,1536]{1,0:T(8,128)(2,1)S(1)} %get-tuple-element.80), channel_id=1, source_target_pairs={{0,4},{2,6},{4,0},{6,2},{8,12},{10,14},{12,8},{14,10},{16,20},{18,... | collective-permute-start | bytes 2359304 | tf_op jit(solution)/shard_map/ppermute | solution.py:329
  171.3 21.7 %collective-permute-start.64 = (bf16[96,1024]{1,0:T(8,128)(2,1)S(1)}, bf16[96,1024]{1,0:T(8,128)(2,1)S(1)}, u32[]{:S(2)}, u32[]{:S(2)}) collective-permute-start(bf16[96,1024]{1,0:T(8,128)(2,1)S(1)} %slice.399), channel_id=1, source_target_pairs={{0,4},{2,6},{4,0},{6,2},{8,12},{10,14},{12,8},{14,10},{16,20},{18,... | collective-permute-start | bytes 589832 | tf_op jit(solution)/shard_map/ppermute | solution.py:329
  172.8 20.3 %collective-permute-start.66 = (bf16[96,1024]{1,0:T(8,128)(2,1)S(1)}, bf16[96,1024]{1,0:T(8,128)(2,1)S(1)}, u32[]{:S(2)}, u32[]{:S(2)}) collective-permute-start(bf16[96,1024]{1,0:T(8,128)(2,1)S(1)} %slice.401), channel_id=1, source_target_pairs={{0,2},{2,0},{4,6},{6,4},{8,10},{10,8},{12,14},{14,12},{16,18},{18,... | collective-permute-start | bytes 589832 | tf_op jit(solution)/shard_map/ppermute | solution.py:329
  173.2 23.5 %collective-permute-start.36 = (bf16[128,1024]{1,0:T(8,128)(2,1)S(1)}, bf16[128,1024]{1,0:T(8,128)(2,1)S(1)}, u32[]{:S(2)}, u32[]{:S(2)}) collective-permute-start(bf16[128,1024]{1,0:T(8,128)(2,1)S(1)} %fusion.37), channel_id=1, source_target_pairs={{0,8},{2,10},{4,12},{6,14},{8,0},{10,2},{12,4},{14,6},{16,24},{18,... | collective-permute-start | bytes 786440 | tf_op jit(solution)/shard_map/ppermute | solution.py:329
  211.2 30.0 %collective-permute-start.60 = (bf16[128,1536]{1,0:T(8,128)(2,1)S(1)}, bf16[128,1536]{1,0:T(8,128)(2,1)S(1)}, u32[]{:S(2)}, u32[]{:S(2)}) collective-permute-start(bf16[128,1536]{1,0:T(8,128)(2,1)S(1)} %pad_maximum_fusion.14), channel_id=1, source_target_pairs={{0,16},{2,18},{4,20},{6,22},{8,24},{10,26},{12,28},{14,30},{16,0},... | collective-permute-start | bytes 1179656 | tf_op jit(solution)/shard_map/ppermute | solution.py:329
  229.5 19.2 %collective-permute-start.50 = (bf16[128,1024]{1,0:T(8,128)(2,1)S(1)}, bf16[128,1024]{1,0:T(8,128)(2,1)S(1)}, u32[]{:S(2)}, u32[]{:S(2)}) collective-permute-start(bf16[128,1024]{1,0:T(8,128)(2,1)S(1)} %get-tuple-element.73), channel_id=1, source_target_pairs={{0,2},{2,0},{4,6},{6,4},{8,10},{10,8},{12,14},{14,12},{16,18},{18,... | collective-permute-start | bytes 786440 | tf_op jit(solution)/shard_map/ppermute | solution.py:329
  229.7 19.2 %collective-permute-start.52 = (bf16[128,1024]{1,0:T(8,128)(2,1)S(1)}, bf16[128,1024]{1,0:T(8,128)(2,1)S(1)}, u32[]{:S(2)}, u32[]{:S(2)}) collective-permute-start(bf16[128,1024]{1,0:T(8,128)(2,1)S(1)} %get-tuple-element.75), channel_id=1, source_target_pairs={{0,4},{2,6},{4,0},{6,2},{8,12},{10,14},{12,8},{14,10},{16,20},{18,... | collective-permute-start | bytes 786440 | tf_op jit(solution)/shard_map/ppermute | solution.py:329
  230.0 29.9 %collective-permute-start.43 = (bf16[256,1024]{1,0:T(8,128)(2,1)S(1)}, bf16[256,1024]{1,0:T(8,128)(2,1)S(1)}, u32[]{:S(2)}, u32[]{:S(2)}) collective-permute-start(bf16[256,1024]{1,0:T(8,128)(2,1)S(1)} %get-tuple-element.69), channel_id=1, source_target_pairs={{0,2},{2,0},{4,6},{6,4},{8,10},{10,8},{12,14},{14,12},{16,18},{18,... | collective-permute-start | bytes 1572872 | tf_op jit(solution)/shard_map/ppermute | solution.py:329
  231.3 32.9 %collective-permute-start.45 = (bf16[256,1024]{1,0:T(8,128)(2,1)S(1)}, bf16[256,1024]{1,0:T(8,128)(2,1)S(1)}, u32[]{:S(2)}, u32[]{:S(2)}) collective-permute-start(bf16[256,1024]{1,0:T(8,128)(2,1)S(1)} %get-tuple-element.71), channel_id=1, source_target_pairs={{0,4},{2,6},{4,0},{6,2},{8,12},{10,14},{12,8},{14,10},{16,20},{18,... | collective-permute-start | bytes 1572872 | tf_op jit(solution)/shard_map/ppermute | solution.py:329
  246.6 19.4 %collective-permute-start.41 = (bf16[2,128,1024]{2,1,0:T(8,128)(2,1)S(1)}, bf16[2,128,1024]{2,1,0:T(8,128)(2,1)S(1)}, u32[]{:S(2)}, u32[]{:S(2)}) collective-permute-start(bf16[2,128,1024]{2,1,0:T(8,128)(2,1)S(1)} %get-tuple-element.68), channel_id=1, source_target_pairs={{0,1},{1,0},{2,3},{3,2},{4,5},{5,4},{6,7},{7,6},{8,9},{9,8},{10,11... | collective-permute-start | bytes 1572872 | tf_op jit(solution)/shard_map/ppermute | solution.py:333
  248.7 18.1 %collective-permute-start.39 = (bf16[2,128,1024]{2,1,0:T(8,128)(2,1)S(1)}, bf16[2,128,1024]{2,1,0:T(8,128)(2,1)S(1)}, u32[]{:S(2)}, u32[]{:S(2)}) collective-permute-start(bf16[2,128,1024]{2,1,0:T(8,128)(2,1)S(1)} %get-tuple-element.66), channel_id=1, source_target_pairs={{0,1},{1,0},{2,3},{3,2},{4,5},{5,4},{6,7},{7,6},{8,9},{9,8},{10,11... | collective-permute-start | bytes 1572872 | tf_op jit(solution)/shard_map/ppermute | solution.py:333
  268.0 32.0 %collective-permute-start.40 = (bf16[128,1024]{1,0:T(8,128)(2,1)}, bf16[128,1024]{1,0:T(8,128)(2,1)}, u32[]{:S(2)}, u32[]{:S(2)}) collective-permute-start(bf16[128,1024]{1,0:T(8,128)(2,1)} %fusion.39), channel_id=1, source_target_pairs={{0,8},{2,10},{4,12},{6,14},{8,0},{10,2},{12,4},{14,6},{16,24},{18,... | collective-permute-start | bytes 786440 | tf_op jit(solution)/shard_map/ppermute | solution.py:329
  274.7 34.8 %collective-permute-start.55 = (bf16[128,1024]{1,0:T(8,128)(2,1)}, bf16[128,1024]{1,0:T(8,128)(2,1)}, u32[]{:S(2)}, u32[]{:S(2)}) collective-permute-start(bf16[128,1024]{1,0:T(8,128)(2,1)} %add_convert_fusion.10), channel_id=1, source_target_pairs={{0,1},{2,3},{4,5},{6,7},{8,9},{10,11},{12,13},{14,15},{17,16},{19,... | collective-permute-start | bytes 786440 | tf_op jit(solution)/shard_map/ppermute | solution.py:397
  281.0 20.8 %collective-permute-start.47 = (bf16[128,1024]{1,0:T(8,128)(2,1)S(1)}, bf16[128,1024]{1,0:T(8,128)(2,1)S(1)}, u32[]{:S(2)}, u32[]{:S(2)}) collective-permute-start(bf16[128,1024]{1,0:T(8,128)(2,1)S(1)} %pad_maximum_fusion.25), channel_id=1, source_target_pairs={{0,16},{2,18},{4,20},{6,22},{8,24},{10,26},{12,28},{14,30},{16,0},... | collective-permute-start | bytes 786440 | tf_op jit(solution)/shard_map/ppermute | solution.py:329
  (124 other events, 1137.3 us)

commit v4 on v3

--- a/solution.py
+++ b/solution.py
@@ -320,7 +320,7 @@
 X_BIT, Y_BIT, P_BIT, H_BIT = 1, 2, 4, 8
 LOW = jnp.bfloat16
 WIDE = jnp.float32
-VMEM_BYTES = 48 * 1024 * 1024
+VMEM_BYTES = 32 * 1024 * 1024
 COLUMN_GROUPS = ((0, Y_BIT), (X_BIT, Y_BIT), (P_BIT, X_BIT), (P_BIT + Y_BIT, X_BIT))
 ROW_GROUPS = ((0, Y_BIT, 0), (X_BIT, Y_BIT, 0), (0, X_BIT, 1), (Y_BIT, X_BIT, 1))
 

time: 316 us -> 313 us (level)
  Pallas kernels: 65.6 us -> 61.8 us
    pallas_call x11, Pallas kernels: 65.6 us -> 61.8 us  [call(): return lambda *operands: made(*operands, *after)]
    unnamed x164 -> x170, local copies, waits for them, and re-layouts: 7.94 us -> 8.46 us
  transfers between devices with their start and end apart: 74 -> 74, of which waited for: 22 -> 22; matrix products, arithmetic and copies ran while one was open for 10% -> 10% of each run, Pallas kernels for 16% -> 15%
where the time goes in v4:
time: 313 us; the launch traced here: 312 us
  waiting for transfers between devices  114 us (36%)
  starting transfers between devices  89.3 us (29%)
  Pallas kernels  61.8 us (20%)
  other arithmetic  27.7 us (9%)
  local copies, waits for them, and re-layouts  16.3 us (5%)
    ppermute x57, waiting for transfers between devices, swap(): return lax.ppermute(values, 'dp', [(i, i ^ bit) for i in range(16)])  108 us
    pallas_call x11, Pallas kernels, call(): return lambda *operands: made(*operands, *after)  61.8 us
    ppermute x57, starting transfers between devices, swap(): return lax.ppermute(values, 'dp', [(i, i ^ bit) for i in range(16)])  48.1 us
    ppermute x11, starting transfers between devices, swap_core(): return lax.ppermute(values, 'ctx', [(0, 1), (1, 0)])  28.9 us
    add x8, other arithmetic, lion_step(): new_moments.append(BETA_TWO * moment_arr + (1.0 - BETA_TWO) * scaled)  10.1 us
    ppermute x4, starting transfers between devices, row_cross(): return lax.ppermute(values, ('dp', 'ctx'), pairs)  9.45 us
    unnamed x170, local copies, waits for them, and re-layouts  8.46 us
  transfers between devices with their start and end apart: 74, of which 22 were waited for; matrix products, arithmetic and copies ran while one was open for 10% of the time, Pallas kernels for 15%

profile of v4, /device:TPU:1, one launch (start us, length us, event | category | flops | bytes accessed | tf_op | source)
XLA Modules:
  0.0 312.3 jit_solution(3187880915520570647)
XLA Ops:
  15.3 3.8 %collective-permute-start.2 = (bf16[2,144]{1,0:T(2,128)(2,1)S(1)}, bf16[2,144]{1,0:T(2,128)(2,1)S(1)}, u32[]{:S(2)}, u32[]{:S(2)}) collective-permute-start(bf16[2,144]{1,0:T(2,128)(2,1)S(1)} %pad_maximum_fusion.37), channel_id=1, source_target_pairs={{0,16},{2,18},{4,20},{6,22},{8,24},{10,26},{12,28},{14,30},{16,0},... | collective-permute-start | bytes 1736 | tf_op jit(solution)/shard_map/ppermute | solution.py:329
  19.2 8.8 %collective-permute-done.2 = bf16[2,144]{1,0:T(2,128)(2,1)S(1)} collective-permute-done((bf16[2,144]{1,0:T(2,128)(2,1)S(1)}, bf16[2,144]{1,0:T(2,128)(2,1)S(1)}, u32[]{:S(2)}, u32[]{:S(2)}) %collective-permute-start.2) | collective-permute-done | bytes 608 | tf_op jit(solution)/shard_map/ppermute | solution.py:329
  37.3 3.6 %collective-permute-done.5 = bf16[128,1024]{1,0:T(8,128)(2,1)S(1)} collective-permute-done((bf16[128,1024]{1,0:T(8,128)(2,1)S(1)}, bf16[128,1024]{1,0:T(8,128)(2,1)S(1)}, u32[]{:S(2)}, u32[]{:S(2)}) %collective-permute-start.5) | collective-permute-done | bytes 262176 | tf_op jit(solution)/shard_map/ppermute | solution.py:329
  41.0 7.5 %collective-permute-start.6 = (bf16[2,128,1024]{2,1,0:T(8,128)(2,1)S(1)}, bf16[2,128,1024]{2,1,0:T(8,128)(2,1)S(1)}, u32[]{:S(2)}, u32[]{:S(2)}) collective-permute-start(bf16[2,128,1024]{2,1,0:T(8,128)(2,1)S(1)} %pad_maximum_fusion.2.refs_1_), channel_id=1, source_target_pairs={{0,1},{1,0},{2,3},{3,2},{4,5},{5,4},{6,7},{7,6},{8,9},{9,8},{10,11... | collective-permute-start | bytes 1572872 | tf_op jit(solution)/shard_map/ppermute | solution.py:333
  52.3 3.2 %collective-permute-done.11 = bf16[128,1024]{1,0:T(8,128)(2,1)S(1)} collective-permute-done((bf16[128,1024]{1,0:T(8,128)(2,1)S(1)}, bf16[128,1024]{1,0:T(8,128)(2,1)S(1)}, u32[]{:S(2)}, u32[]{:S(2)}) %collective-permute-start.11) | collective-permute-done | bytes 262176 | tf_op jit(solution)/shard_map/ppermute | solution.py:329
  59.1 10.6 %collective-permute-done.19.refs_6_ = bf16[96,1024]{1,0:T(8,128)(2,1)S(1)} collective-permute-done((bf16[96,1024]{1,0:T(8,128)(2,1)S(1)}, bf16[96,1024]{1,0:T(8,128)(2,1)S(1)}, u32[]{:S(2)}, u32[]{:S(2)}) %collective-permute-start.19) | collective-permute-done | bytes 196640 | tf_op jit(solution)/shard_map/ppermute | solution.py:329
  71.5 8.0 %shard_map.331 = (bf16[512,512]{1,0:T(8,128)(2,1)S(1)}, f32[512,768]{1,0:T(8,128)S(1)}, bf16[512,768]{1,0:T(8,128)(2,1)S(1)}, bf16[512,256]{1,0:T(8,128)(2,1)S(1)}, f32[512,128]{1,0:T(8,128)S(1)}) custom-call(s32[9]{0:T(128)S(1)} %pad_add_fusion.1.refs_0_, bf16[2,128,1024]{2,1,0:T(8,128)(2,1)S(1)} %pad_maximum_fusion.2.refs_1_, ...), custom_call_target="tpu_custom_call" | custom-call | flops 2000000000 | bytes 8000000 | tf_op jit(solution)/shard_map/pallas_call | solution.py:440
  81.6 2.7 shard_map.332
  84.3 6.9 %collective-permute-start.21 = (bf16[2,128,1024]{2,1,0:T(8,128)(2,1)S(1)}, bf16[2,128,1024]{2,1,0:T(8,128)(2,1)S(1)}, u32[]{:S(2)}, u32[]{:S(2)}) collective-permute-start(bf16[2,128,1024]{2,1,0:T(8,128)(2,1)S(1)} %get-tuple-element.54), channel_id=1, source_target_pairs={{0,1},{1,0},{2,3},{3,2},{4,5},{5,4},{6,7},{7,6},{8,9},{9,8},{10,11... | collective-permute-start | bytes 1572872 | tf_op jit(solution)/shard_map/ppermute | solution.py:333
  96.0 6.1 %collective-permute-done.29 = bf16[128,1536]{1,0:T(8,128)(2,1)S(1)} collective-permute-done((bf16[128,1536]{1,0:T(8,128)(2,1)S(1)}, bf16[128,1536]{1,0:T(8,128)(2,1)S(1)}, u32[]{:S(2)}, u32[]{:S(2)}) %collective-permute-start.29) | collective-permute-done | bytes 393248 | tf_op jit(solution)/shard_map/ppermute | solution.py:329
  106.3 4.7 %collective-permute-done.23 = bf16[128,1024]{1,0:T(8,128)(2,1)S(1)} collective-permute-done((bf16[128,1024]{1,0:T(8,128)(2,1)S(1)}, bf16[128,1024]{1,0:T(8,128)(2,1)S(1)}, u32[]{:S(2)}, u32[]{:S(2)}) %collective-permute-start.23) | collective-permute-done | bytes 262176 | tf_op jit(solution)/shard_map/ppermute | solution.py:329
  113.8 16.8 %collective-permute-done.32.refs_10_.refs_7_.refs_5_ = bf16[192,1024]{1,0:T(8,128)(2,1)S(1)} collective-permute-done((bf16[192,1024]{1,0:T(8,128)(2,1)S(1)}, bf16[192,1024]{1,0:T(8,128)(2,1)S(1)}, u32[]{:S(2)}, u32[]{:S(2)}) %collective-permute-start.32) | collective-permute-done | bytes 393248 | tf_op jit(solution)/shard_map/ppermute | solution.py:329
  130.6 6.9 %shard_map.333 = (f32[512,1536]{1,0:T(8,128)S(1)}, bf16[512,768]{1,0:T(8,128)(2,1)S(1)}) custom-call(s32[9]{0:T(128)S(1)} %pad_add_fusion.1.refs_0_, bf16[2,128,1024]{2,1,0:T(8,128)(2,1)S(1)} %pad_maximum_fusion.5.refs_1_, bf16[2,128,1024]{2,1,0:T(8,128)(2,1)S(1)} %collective-permute-done.24.refs_2_, bf16[256,1536]{1,0:T(8,128)(2,1)S(1)} %pad_maximum_fusion.refs_3_.refs_8_, ...), custom_call_target="tpu_custom_call" | custom-call | flops 1610612736 | bytes 10000000 | tf_op jit(solution)/shard_map/pallas_call | solution.py:440
  137.5 10.7 %shard_map.334 = (bf16[512,1536]{1,0:T(8,128)(2,1)S(1)}, bf16[2,128,1024]{2,1,0:T(8,128)(2,1)S(1)}, bf16[2,128,1024]{2,1,0:T(8,128)(2,1)S(1)}) custom-call(s32[9]{0:T(128)S(1)} %pad_add_fusion.1.refs_0_, bf16[2,128,1024]{2,1,0:T(8,128)(2,1)S(1)} %pad_maximum_fusion.6.refs_1_.refs_2_, bf16[2,128,1024]{2,1,0:T(8,128)(2,1)S(1)} %collective-permute-done.34.refs_2_.refs_3_, ...), custom_call_target="tpu_custom_call" | custom-call | flops 2415919104 | bytes 12000000 | tf_op jit(solution)/shard_map/pallas_call | solution.py:440
  148.2 3.4 %shard_map.341 = (bf16[192,1024]{1,0:T(8,128)(2,1)S(1)}, bf16[192,1024]{1,0:T(8,128)(2,1)}, bf16[192,1024]{1,0:T(8,128)(2,1)S(1)}, bf16[192,1024]{1,0:T(8,128)(2,1)S(1)}) custom-call(s32[9]{0:T(128)S(1)} %pad_add_fusion.1.refs_0_, bf16[512,768]{1,0:T(8,128)(2,1)S(1)} %get-tuple-element.55.refs_1_, ...), custom_call_target="tpu_custom_call" | custom-call | flops 805306368 | bytes 4000000 | tf_op jit(solution)/shard_map/pallas_call | solution.py:440
  159.3 6.8 %shard_map.340 = (bf16[256,1536]{1,0:T(8,128)(2,1)S(1)}, bf16[256,1536]{1,0:T(8,128)(2,1)S(1)}, bf16[256,1536]{1,0:T(8,128)(2,1)S(1)}, bf16[256,1536]{1,0:T(8,128)(2,1)S(1)}) custom-call(s32[9]{0:T(128)S(1)} %pad_add_fusion.1.refs_0_, bf16[2,128,1024]{2,1,0:T(8,128)(2,1)S(1)} %pad_maximum_fusion.5.refs_1_, bf16[2,128,1024]{2,1,0:T(8,128)(2,1)S(1)} %copy-done.21, ...), custom_call_target="tpu_custom_call" | custom-call | flops 1610612736 | bytes 6000000 | tf_op jit(solution)/shard_map/pallas_call | solution.py:440
  172.0 18.6 %collective-permute-done.64 = bf16[96,1024]{1,0:T(8,128)(2,1)S(1)} collective-permute-done((bf16[96,1024]{1,0:T(8,128)(2,1)S(1)}, bf16[96,1024]{1,0:T(8,128)(2,1)S(1)}, u32[]{:S(2)}, u32[]{:S(2)}) %collective-permute-start.64) | collective-permute-done | bytes 196640 | tf_op jit(solution)/shard_map/ppermute | solution.py:329
  190.8 3.5 %collective-permute-start.67 = (bf16[192,1024]{1,0:T(8,128)(2,1)S(1)}, bf16[192,1024]{1,0:T(8,128)(2,1)S(1)}, u32[]{:S(2)}, u32[]{:S(2)}) collective-permute-start(bf16[192,1024]{1,0:T(8,128)(2,1)S(1)} %pad_maximum_fusion.18), channel_id=1, source_target_pairs={{1,17},{3,19},{5,21},{7,23},{9,25},{11,27},{13,29},{15,31},{16,0},... | collective-permute-start | bytes 1179656 | tf_op jit(solution)/shard_map/ppermute | solution.py:346
  197.4 4.5 %collective-permute-done.67 = bf16[192,1024]{1,0:T(8,128)(2,1)S(1)} collective-permute-done((bf16[192,1024]{1,0:T(8,128)(2,1)S(1)}, bf16[192,1024]{1,0:T(8,128)(2,1)S(1)}, u32[]{:S(2)}, u32[]{:S(2)}) %collective-permute-start.67) | collective-permute-done | bytes 393248 | tf_op jit(solution)/shard_map/ppermute | solution.py:346
  203.4 4.1 %collective-permute-done.37 = bf16[128,1024]{1,0:T(8,128)(2,1)S(1)} collective-permute-done((bf16[128,1024]{1,0:T(8,128)(2,1)S(1)}, bf16[128,1024]{1,0:T(8,128)(2,1)S(1)}, u32[]{:S(2)}, u32[]{:S(2)}) %collective-permute-start.37) | collective-permute-done | bytes 262176 | tf_op jit(solution)/shard_map/ppermute | solution.py:329
  211.5 7.1 %shard_map.335 = (bf16[512,1024]{1,0:T(8,128)(2,1)S(1)}, f32[8,128]{1,0:T(8,128)S(1)}) custom-call(s32[9]{0:T(128)S(1)} %pad_add_fusion.1.refs_0_, bf16[2,128,1024]{2,1,0:T(8,128)(2,1)S(1)} %pad_maximum_fusion.7.refs_1_.refs_2_, bf16[2,128,1024]{2,1,0:T(8,128)(2,1)S(1)} %collective-permute-done.38.refs_2_.refs_3_, bf16[128,1024]{1,0:T(8,128)(2,1)S(1)} %copy-done.9, ...), custom_call_target="tpu_custom_call" | custom-call | flops 2000000000 | bytes 8000000 | tf_op jit(solution)/shard_map/pallas_call | solution.py:440
  218.6 4.9 %shard_map.336 = (bf16[256,1024]{1,0:T(8,128)(2,1)S(1)}, bf16[256,1024]{1,0:T(8,128)(2,1)S(1)}, bf16[256,1024]{1,0:T(8,128)(2,1)S(1)}, bf16[256,1024]{1,0:T(8,128)(2,1)S(1)}) custom-call(s32[9]{0:T(128)S(1)} %pad_add_fusion.1.refs_0_, bf16[2,128,1024]{2,1,0:T(8,128)(2,1)S(1)} %pad_maximum_fusion.2.refs_1_, bf16[2,128,1024]{2,1,0:T(8,128)(2,1)S(1)} %copy-done.17, ...), custom_call_target="tpu_custom_call" | custom-call | flops 1073741824 | bytes 6000000 | tf_op jit(solution)/shard_map/pallas_call | solution.py:440
  223.5 2.7 shard_map.339
  229.3 3.7 %shard_map.337 = (bf16[2,128,1024]{2,1,0:T(8,128)(2,1)S(1)}, bf16[2,128,1024]{2,1,0:T(8,128)(2,1)S(1)}) custom-call(s32[9]{0:T(128)S(1)} %pad_add_fusion.1.refs_0_, bf16[512,768]{1,0:T(8,128)(2,1)S(1)} %copy-done.35, bf16[192,1024]{1,0:T(8,128)(2,1)S(1)} %pad_maximum_fusion.12.refs_7_.refs_4_.refs_2_, bf16[192,1024]{1,0:T(8,128)(2,1)S(1)} %copy-done.24, ...), custom_call_target="tpu_custom_call" | custom-call | flops 805306368 | bytes 4000000 | tf_op jit(solution)/shard_map/pallas_call | solution.py:440
  233.0 4.9 %shard_map.338 = (bf16[2,128,1024]{2,1,0:T(8,128)(2,1)S(1)}, bf16[2,128,1024]{2,1,0:T(8,128)(2,1)S(1)}) custom-call(s32[9]{0:T(128)S(1)} %pad_add_fusion.1.refs_0_, bf16[512,1024]{1,0:T(8,128)(2,1)S(1)} %get-tuple-element.63.refs_3_.refs_1_, bf16[256,1024]{1,0:T(8,128)(2,1)S(1)} %pad_maximum_fusion.3.refs_3_.refs_2_, bf16[256,1024]{1,0:T(8,128)(2,1)S(1)} %copy-done.19, ...), custom_call_target="tpu_custom_call" | custom-call | flops 1073741824 | bytes 5000000 | tf_op jit(solution)/shard_map/pallas_call | solution.py:440
  238.1 5.2 %collective-permute-done.61 = bf16[64,1536]{1,0:T(8,128)(2,1)S(1)} collective-permute-done((bf16[64,1536]{1,0:T(8,128)(2,1)S(1)}, bf16[64,1536]{1,0:T(8,128)(2,1)S(1)}, u32[]{:S(2)}, u32[]{:S(2)}) %collective-permute-start.61) | collective-permute-done | bytes 196640 | tf_op jit(solution)/shard_map/ppermute | solution.py:329
  246.3 4.0 %collective-permute-done.51 = bf16[64,1024]{1,0:T(8,128)(2,1)S(1)} collective-permute-done((bf16[64,1024]{1,0:T(8,128)(2,1)S(1)}, bf16[64,1024]{1,0:T(8,128)(2,1)S(1)}, u32[]{:S(2)}, u32[]{:S(2)}) %collective-permute-start.51) | collective-permute-done | bytes 131104 | tf_op jit(solution)/shard_map/ppermute | solution.py:329
  250.5 3.6 %collective-permute-done.53 = bf16[64,1024]{1,0:T(8,128)(2,1)S(1)} collective-permute-done((bf16[64,1024]{1,0:T(8,128)(2,1)S(1)}, bf16[64,1024]{1,0:T(8,128)(2,1)S(1)}, u32[]{:S(2)}, u32[]{:S(2)}) %collective-permute-start.53) | collective-permute-done | bytes 131104 | tf_op jit(solution)/shard_map/ppermute | solution.py:329
  256.7 3.3 %collective-permute-start.54 = (bf16[128,1024]{1,0:T(8,128)(2,1)S(1)}, bf16[128,1024]{1,0:T(8,128)(2,1)S(1)}, u32[]{:S(2)}, u32[]{:S(2)}) collective-permute-start(bf16[128,1024]{1,0:T(8,128)(2,1)S(1)} %pad_maximum_fusion.28), channel_id=1, source_target_pairs={{1,17},{3,19},{5,21},{7,23},{9,25},{11,27},{13,29},{15,31},{16,0},... | collective-permute-start | bytes 786440 | tf_op jit(solution)/shard_map/ppermute | solution.py:346
  281.8 10.5 %collective-permute-done.71 = bf16[16,144]{1,0:T(8,128)(2,1)S(1)} collective-permute-done((bf16[16,144]{1,0:T(8,128)(2,1)S(1)}, bf16[16,144]{1,0:T(8,128)(2,1)S(1)}, u32[]{:S(2)}, u32[]{:S(2)}) %collective-permute-start.71) | collective-permute-done | bytes 4640 | tf_op jit(solution)/shard_map/ppermute | solution.py:329
  299.3 3.2 %collective-permute-done.48 = bf16[64,1024]{1,0:T(8,128)(2,1)S(1)} collective-permute-done((bf16[64,1024]{1,0:T(8,128)(2,1)S(1)}, bf16[64,1024]{1,0:T(8,128)(2,1)S(1)}, u32[]{:S(2)}, u32[]{:S(2)}) %collective-permute-start.48) | collective-permute-done | bytes 131104 | tf_op jit(solution)/shard_map/ppermute | solution.py:329
  302.6 3.6 %collective-permute-start.49 = (bf16[2,64,1024]{2,1,0:T(8,128)(2,1)S(1)}, bf16[2,64,1024]{2,1,0:T(8,128)(2,1)S(1)}, u32[]{:S(2)}, u32[]{:S(2)}) collective-permute-start(bf16[2,64,1024]{2,1,0:T(8,128)(2,1)S(1)} %pad_maximum_fusion.26), channel_id=1, source_target_pairs={{0,1},{1,0},{2,3},{3,2},{4,5},{5,4},{6,7},{7,6},{8,9},{9,8},{10,11... | collective-permute-start | bytes 786440 | tf_op jit(solution)/shard_map/ppermute | solution.py:333
  (457 shorter events, 111.4 us)
Async XLA Ops:
  6.2 28.3 %collective-permute-start.7 = (bf16[64,1024]{1,0:T(8,128)(2,1)}, bf16[64,1024]{1,0:T(8,128)(2,1)S(1)}, u32[]{:S(2)}, u32[]{:S(2)}) collective-permute-start(bf16[64,1024]{1,0:T(8,128)(2,1)} %pad_maximum_fusion.30), channel_id=1, source_target_pairs={{0,8},{2,10},{4,12},{6,14},{8,0},{10,2},{12,4},{14,6},{16,24},{18,... | collective-permute-start | bytes 393224 | tf_op jit(solution)/shard_map/ppermute | solution.py:329
  8.8 25.9 %collective-permute-start.13 = (bf16[128,1024]{1,0:T(8,128)(2,1)S(1)}, bf16[128,1024]{1,0:T(8,128)(2,1)S(1)}, u32[]{:S(2)}, u32[]{:S(2)}) collective-permute-start(bf16[128,1024]{1,0:T(8,128)(2,1)S(1)} %convert_element_type.387), channel_id=1, source_target_pairs={{0,16},{2,18},{4,20},{6,22},{8,24},{10,26},{12,28},{14,30},{17,1},... | collective-permute-start | bytes 786440 | tf_op jit(solution)/shard_map/ppermute | solution.py:346
  11.4 23.2 %collective-permute-start.25 = (bf16[64,1536]{1,0:T(8,128)(2,1)S(1)}, bf16[64,1536]{1,0:T(8,128)(2,1)S(1)}, u32[]{:S(2)}, u32[]{:S(2)}) collective-permute-start(bf16[64,1536]{1,0:T(8,128)(2,1)S(1)} %pad_maximum_fusion.29), channel_id=1, source_target_pairs={{0,8},{2,10},{4,12},{6,14},{8,0},{10,2},{12,4},{14,6},{16,24},{18,... | collective-permute-start | bytes 589832 | tf_op jit(solution)/shard_map/ppermute | solution.py:329
  14.0 35.9 %collective-permute-start.18 = (bf16[192,1024]{1,0:T(8,128)(2,1)}, bf16[192,1024]{1,0:T(8,128)(2,1)}, u32[]{:S(2)}, u32[]{:S(2)}) collective-permute-start(bf16[192,1024]{1,0:T(8,128)(2,1)} %convert_element_type.388), channel_id=1, source_target_pairs={{0,16},{2,18},{4,20},{6,22},{8,24},{10,26},{12,28},{14,30},{17,1},... | collective-permute-start | bytes 1179656 | tf_op jit(solution)/shard_map/ppermute | solution.py:346
  34.8 22.4 %collective-permute-start.16 = (bf16[64,1024]{1,0:T(8,128)(2,1)S(1)}, bf16[64,1024]{1,0:T(8,128)(2,1)S(1)}, u32[]{:S(2)}, u32[]{:S(2)}) collective-permute-start(bf16[64,1024]{1,0:T(8,128)(2,1)S(1)} %get-tuple-element.146), channel_id=1, source_target_pairs={{0,2},{2,0},{4,6},{6,4},{8,10},{10,8},{12,14},{14,12},{16,18},{18,... | collective-permute-start | bytes 393224 | tf_op jit(solution)/shard_map/ppermute | solution.py:329
  36.1 22.5 %collective-permute-start.14 = (bf16[64,1024]{1,0:T(8,128)(2,1)S(1)}, bf16[64,1024]{1,0:T(8,128)(2,1)S(1)}, u32[]{:S(2)}, u32[]{:S(2)}) collective-permute-start(bf16[64,1024]{1,0:T(8,128)(2,1)S(1)} %get-tuple-element.147), channel_id=1, source_target_pairs={{0,4},{2,6},{4,0},{6,2},{8,12},{10,14},{12,8},{14,10},{16,20},{18,... | collective-permute-start | bytes 393224 | tf_op jit(solution)/shard_map/ppermute | solution.py:329
  41.0 29.9 %collective-permute-start.6 = (bf16[2,128,1024]{2,1,0:T(8,128)(2,1)S(1)}, bf16[2,128,1024]{2,1,0:T(8,128)(2,1)S(1)}, u32[]{:S(2)}, u32[]{:S(2)}) collective-permute-start(bf16[2,128,1024]{2,1,0:T(8,128)(2,1)S(1)} %pad_maximum_fusion.2.refs_1_), channel_id=1, source_target_pairs={{0,1},{1,0},{2,3},{3,2},{4,5},{5,4},{6,7},{7,6},{8,9},{9,8},{10,11... | collective-permute-start | bytes 1572872 | tf_op jit(solution)/shard_map/ppermute | solution.py:333
  58.6 32.6 %collective-permute-start.26 = (bf16[128,1536]{1,0:T(8,128)(2,1)S(1)}, bf16[128,1536]{1,0:T(8,128)(2,1)S(1)}, u32[]{:S(2)}, u32[]{:S(2)}) collective-permute-start(bf16[128,1536]{1,0:T(8,128)(2,1)S(1)} %pad_maximum_fusion.8), channel_id=1, source_target_pairs={{0,16},{2,18},{4,20},{6,22},{8,24},{10,26},{12,28},{14,30},{16,0},... | collective-permute-start | bytes 1179656 | tf_op jit(solution)/shard_map/ppermute | solution.py:329
  71.4 41.8 %collective-permute-start.33 = (bf16[128,1024]{1,0:T(8,128)(2,1)S(1)}, bf16[128,1024]{1,0:T(8,128)(2,1)S(1)}, u32[]{:S(2)}, u32[]{:S(2)}) collective-permute-start(bf16[128,1024]{1,0:T(8,128)(2,1)S(1)} %bitcast.128), channel_id=1, source_target_pairs={{0,8},{2,10},{4,12},{6,14},{8,0},{10,2},{12,4},{14,6},{16,24},{18,... | collective-permute-start | bytes 786440 | tf_op jit(solution)/shard_map/ppermute | solution.py:329
  80.3 33.1 %collective-permute-start.31 = (bf16[192,1024]{1,0:T(8,128)(2,1)S(1)}, bf16[192,1024]{1,0:T(8,128)(2,1)S(1)}, u32[]{:S(2)}, u32[]{:S(2)}) collective-permute-start(bf16[192,1024]{1,0:T(8,128)(2,1)S(1)} %pad_maximum_fusion.12.refs_7_.refs_4_.refs_2_), channel_id=1, source_target_pairs={{0,2},{2,0},{4,6},{6,4},{8,10},{10,8},{12,14},{14,12},{16,18},{18,... | collective-permute-start | bytes 1179656 | tf_op jit(solution)/shard_map/ppermute | solution.py:329
  102.2 28.3 %collective-permute-start.30 = (bf16[256,1536]{1,0:T(8,128)(2,1)S(1)}, bf16[256,1536]{1,0:T(8,128)(2,1)S(1)}, u32[]{:S(2)}, u32[]{:S(2)}) collective-permute-start(bf16[256,1536]{1,0:T(8,128)(2,1)S(1)} %pad_maximum_fusion.1.refs_5_.refs_10_), channel_id=1, source_target_pairs={{0,4},{2,6},{4,0},{6,2},{8,12},{10,14},{12,8},{14,10},{16,20},{18,... | collective-permute-start | bytes 2359304 | tf_op jit(solution)/shard_map/ppermute | solution.py:329
  105.6 24.9 %collective-permute-start.28 = (bf16[256,1536]{1,0:T(8,128)(2,1)S(1)}, bf16[256,1536]{1,0:T(8,128)(2,1)S(1)}, u32[]{:S(2)}, u32[]{:S(2)}) collective-permute-start(bf16[256,1536]{1,0:T(8,128)(2,1)S(1)} %pad_maximum_fusion.refs_3_.refs_8_), channel_id=1, source_target_pairs={{0,2},{2,0},{4,6},{6,4},{8,10},{10,8},{12,14},{14,12},{16,18},{18,... | collective-permute-start | bytes 2359304 | tf_op jit(solution)/shard_map/ppermute | solution.py:329
  111.1 19.4 %collective-permute-start.24 = (bf16[2,128,1024]{2,1,0:T(8,128)(2,1)S(1)}, bf16[2,128,1024]{2,1,0:T(8,128)(2,1)S(1)}, u32[]{:S(2)}, u32[]{:S(2)}) collective-permute-start(bf16[2,128,1024]{2,1,0:T(8,128)(2,1)S(1)} %pad_maximum_fusion.5.refs_1_), channel_id=1, source_target_pairs={{0,1},{1,0},{2,3},{3,2},{4,5},{5,4},{6,7},{7,6},{8,9},{9,8},{10,11... | collective-permute-start | bytes 1572872 | tf_op jit(solution)/shard_map/ppermute | solution.py:333
  113.2 17.3 %collective-permute-start.32 = (bf16[192,1024]{1,0:T(8,128)(2,1)S(1)}, bf16[192,1024]{1,0:T(8,128)(2,1)S(1)}, u32[]{:S(2)}, u32[]{:S(2)}) collective-permute-start(bf16[192,1024]{1,0:T(8,128)(2,1)S(1)} %pad_maximum_fusion.13.refs_9_.refs_6_.refs_4_), channel_id=1, source_target_pairs={{0,4},{2,6},{4,0},{6,2},{8,12},{10,14},{12,8},{14,10},{16,20},{18,... | collective-permute-start | bytes 1179656 | tf_op jit(solution)/shard_map/ppermute | solution.py:329
  113.4 24.1 %collective-permute-start.34 = (bf16[2,128,1024]{2,1,0:T(8,128)(2,1)S(1)}, bf16[2,128,1024]{2,1,0:T(8,128)(2,1)S(1)}, u32[]{:S(2)}, u32[]{:S(2)}) collective-permute-start(bf16[2,128,1024]{2,1,0:T(8,128)(2,1)S(1)} %pad_maximum_fusion.6.refs_1_.refs_2_), channel_id=1, source_target_pairs={{0,1},{1,0},{2,3},{3,2},{4,5},{5,4},{6,7},{7,6},{8,9},{9,8},{10,11... | collective-permute-start | bytes 1572872 | tf_op jit(solution)/shard_map/ppermute | solution.py:333
  153.9 16.4 %collective-permute-start.65 = (bf16[192,1024]{1,0:T(8,128)(2,1)}, bf16[192,1024]{1,0:T(8,128)(2,1)S(1)}, u32[]{:S(2)}, u32[]{:S(2)}) collective-permute-start(bf16[192,1024]{1,0:T(8,128)(2,1)} %copy-done.27), channel_id=1, source_target_pairs={{0,4},{2,6},{4,0},{6,2},{8,12},{10,14},{12,8},{14,10},{16,20},{18,... | collective-permute-start | bytes 1179656 | tf_op jit(solution)/shard_map/ppermute | solution.py:329
  155.0 15.6 %collective-permute-start.35 = (bf16[2,128,1024]{2,1,0:T(8,128)(2,1)}, bf16[2,128,1024]{2,1,0:T(8,128)(2,1)S(1)}, u32[]{:S(2)}, u32[]{:S(2)}) collective-permute-start(bf16[2,128,1024]{2,1,0:T(8,128)(2,1)} %copy-done.22), channel_id=1, source_target_pairs={{0,1},{1,0},{2,3},{3,2},{4,5},{5,4},{6,7},{7,6},{8,9},{9,8},{10,11... | collective-permute-start | bytes 1572872 | tf_op jit(solution)/shard_map/ppermute | solution.py:333
  166.2 30.2 %collective-permute-start.56 = (bf16[256,1536]{1,0:T(8,128)(2,1)S(1)}, bf16[256,1536]{1,0:T(8,128)(2,1)S(1)}, u32[]{:S(2)}, u32[]{:S(2)}) collective-permute-start(bf16[256,1536]{1,0:T(8,128)(2,1)S(1)} %get-tuple-element.78), channel_id=1, source_target_pairs={{0,2},{2,0},{4,6},{6,4},{8,10},{10,8},{12,14},{14,12},{16,18},{18,... | collective-permute-start | bytes 2359304 | tf_op jit(solution)/shard_map/ppermute | solution.py:329
  167.6 29.3 %collective-permute-start.58 = (bf16[256,1536]{1,0:T(8,128)(2,1)S(1)}, bf16[256,1536]{1,0:T(8,128)(2,1)S(1)}, u32[]{:S(2)}, u32[]{:S(2)}) collective-permute-start(bf16[256,1536]{1,0:T(8,128)(2,1)S(1)} %get-tuple-element.80), channel_id=1, source_target_pairs={{0,4},{2,6},{4,0},{6,2},{8,12},{10,14},{12,8},{14,10},{16,20},{18,... | collective-permute-start | bytes 2359304 | tf_op jit(solution)/shard_map/ppermute | solution.py:329
  168.9 21.7 %collective-permute-start.64 = (bf16[96,1024]{1,0:T(8,128)(2,1)S(1)}, bf16[96,1024]{1,0:T(8,128)(2,1)S(1)}, u32[]{:S(2)}, u32[]{:S(2)}) collective-permute-start(bf16[96,1024]{1,0:T(8,128)(2,1)S(1)} %slice.399), channel_id=1, source_target_pairs={{0,4},{2,6},{4,0},{6,2},{8,12},{10,14},{12,8},{14,10},{16,20},{18,... | collective-permute-start | bytes 589832 | tf_op jit(solution)/shard_map/ppermute | solution.py:329
  170.4 20.3 %collective-permute-start.66 = (bf16[96,1024]{1,0:T(8,128)(2,1)S(1)}, bf16[96,1024]{1,0:T(8,128)(2,1)S(1)}, u32[]{:S(2)}, u32[]{:S(2)}) collective-permute-start(bf16[96,1024]{1,0:T(8,128)(2,1)S(1)} %slice.401), channel_id=1, source_target_pairs={{0,2},{2,0},{4,6},{6,4},{8,10},{10,8},{12,14},{14,12},{16,18},{18,... | collective-permute-start | bytes 589832 | tf_op jit(solution)/shard_map/ppermute | solution.py:329
  170.9 23.4 %collective-permute-start.36 = (bf16[128,1024]{1,0:T(8,128)(2,1)S(1)}, bf16[128,1024]{1,0:T(8,128)(2,1)S(1)}, u32[]{:S(2)}, u32[]{:S(2)}) collective-permute-start(bf16[128,1024]{1,0:T(8,128)(2,1)S(1)} %fusion.37), channel_id=1, source_target_pairs={{0,8},{2,10},{4,12},{6,14},{8,0},{10,2},{12,4},{14,6},{16,24},{18,... | collective-permute-start | bytes 786440 | tf_op jit(solution)/shard_map/ppermute | solution.py:329
  208.8 29.1 %collective-permute-start.60 = (bf16[128,1536]{1,0:T(8,128)(2,1)S(1)}, bf16[128,1536]{1,0:T(8,128)(2,1)S(1)}, u32[]{:S(2)}, u32[]{:S(2)}) collective-permute-start(bf16[128,1536]{1,0:T(8,128)(2,1)S(1)} %pad_maximum_fusion.14), channel_id=1, source_target_pairs={{0,16},{2,18},{4,20},{6,22},{8,24},{10,26},{12,28},{14,30},{16,0},... | collective-permute-start | bytes 1179656 | tf_op jit(solution)/shard_map/ppermute | solution.py:329
  226.3 19.2 %collective-permute-start.50 = (bf16[128,1024]{1,0:T(8,128)(2,1)S(1)}, bf16[128,1024]{1,0:T(8,128)(2,1)S(1)}, u32[]{:S(2)}, u32[]{:S(2)}) collective-permute-start(bf16[128,1024]{1,0:T(8,128)(2,1)S(1)} %get-tuple-element.73), channel_id=1, source_target_pairs={{0,2},{2,0},{4,6},{6,4},{8,10},{10,8},{12,14},{14,12},{16,18},{18,... | collective-permute-start | bytes 786440 | tf_op jit(solution)/shard_map/ppermute | solution.py:329
  226.5 19.2 %collective-permute-start.52 = (bf16[128,1024]{1,0:T(8,128)(2,1)S(1)}, bf16[128,1024]{1,0:T(8,128)(2,1)S(1)}, u32[]{:S(2)}, u32[]{:S(2)}) collective-permute-start(bf16[128,1024]{1,0:T(8,128)(2,1)S(1)} %get-tuple-element.75), channel_id=1, source_target_pairs={{0,4},{2,6},{4,0},{6,2},{8,12},{10,14},{12,8},{14,10},{16,20},{18,... | collective-permute-start | bytes 786440 | tf_op jit(solution)/shard_map/ppermute | solution.py:329
  227.5 29.2 %collective-permute-start.43 = (bf16[256,1024]{1,0:T(8,128)(2,1)S(1)}, bf16[256,1024]{1,0:T(8,128)(2,1)S(1)}, u32[]{:S(2)}, u32[]{:S(2)}) collective-permute-start(bf16[256,1024]{1,0:T(8,128)(2,1)S(1)} %get-tuple-element.69), channel_id=1, source_target_pairs={{0,2},{2,0},{4,6},{6,4},{8,10},{10,8},{12,14},{14,12},{16,18},{18,... | collective-permute-start | bytes 1572872 | tf_op jit(solution)/shard_map/ppermute | solution.py:329
  228.1 32.9 %collective-permute-start.45 = (bf16[256,1024]{1,0:T(8,128)(2,1)S(1)}, bf16[256,1024]{1,0:T(8,128)(2,1)S(1)}, u32[]{:S(2)}, u32[]{:S(2)}) collective-permute-start(bf16[256,1024]{1,0:T(8,128)(2,1)S(1)} %get-tuple-element.71), channel_id=1, source_target_pairs={{0,4},{2,6},{4,0},{6,2},{8,12},{10,14},{12,8},{14,10},{16,20},{18,... | collective-permute-start | bytes 1572872 | tf_op jit(solution)/shard_map/ppermute | solution.py:329
  243.3 19.4 %collective-permute-start.41 = (bf16[2,128,1024]{2,1,0:T(8,128)(2,1)S(1)}, bf16[2,128,1024]{2,1,0:T(8,128)(2,1)S(1)}, u32[]{:S(2)}, u32[]{:S(2)}) collective-permute-start(bf16[2,128,1024]{2,1,0:T(8,128)(2,1)S(1)} %get-tuple-element.68), channel_id=1, source_target_pairs={{0,1},{1,0},{2,3},{3,2},{4,5},{5,4},{6,7},{7,6},{8,9},{9,8},{10,11... | collective-permute-start | bytes 1572872 | tf_op jit(solution)/shard_map/ppermute | solution.py:333
  245.5 18.1 %collective-permute-start.39 = (bf16[2,128,1024]{2,1,0:T(8,128)(2,1)S(1)}, bf16[2,128,1024]{2,1,0:T(8,128)(2,1)S(1)}, u32[]{:S(2)}, u32[]{:S(2)}) collective-permute-start(bf16[2,128,1024]{2,1,0:T(8,128)(2,1)S(1)} %get-tuple-element.66), channel_id=1, source_target_pairs={{0,1},{1,0},{2,3},{3,2},{4,5},{5,4},{6,7},{7,6},{8,9},{9,8},{10,11... | collective-permute-start | bytes 1572872 | tf_op jit(solution)/shard_map/ppermute | solution.py:333
  264.8 31.9 %collective-permute-start.40 = (bf16[128,1024]{1,0:T(8,128)(2,1)}, bf16[128,1024]{1,0:T(8,128)(2,1)}, u32[]{:S(2)}, u32[]{:S(2)}) collective-permute-start(bf16[128,1024]{1,0:T(8,128)(2,1)} %fusion.39), channel_id=1, source_target_pairs={{0,8},{2,10},{4,12},{6,14},{8,0},{10,2},{12,4},{14,6},{16,24},{18,... | collective-permute-start | bytes 786440 | tf_op jit(solution)/shard_map/ppermute | solution.py:329
  271.4 34.7 %collective-permute-start.55 = (bf16[128,1024]{1,0:T(8,128)(2,1)}, bf16[128,1024]{1,0:T(8,128)(2,1)}, u32[]{:S(2)}, u32[]{:S(2)}) collective-permute-start(bf16[128,1024]{1,0:T(8,128)(2,1)} %add_convert_fusion.10), channel_id=1, source_target_pairs={{0,1},{2,3},{4,5},{6,7},{8,9},{10,11},{12,13},{14,15},{17,16},{19,... | collective-permute-start | bytes 786440 | tf_op jit(solution)/shard_map/ppermute | solution.py:397
  277.8 20.8 %collective-permute-start.47 = (bf16[128,1024]{1,0:T(8,128)(2,1)S(1)}, bf16[128,1024]{1,0:T(8,128)(2,1)S(1)}, u32[]{:S(2)}, u32[]{:S(2)}) collective-permute-start(bf16[128,1024]{1,0:T(8,128)(2,1)S(1)} %pad_maximum_fusion.25), channel_id=1, source_target_pairs={{0,16},{2,18},{4,20},{6,22},{8,24},{10,26},{12,28},{14,30},{16,0},... | collective-permute-start | bytes 786440 | tf_op jit(solution)/shard_map/ppermute | solution.py:329
  (127 other events, 1146.9 us)

commit v5 on v4

--- a/solution.py
+++ b/solution.py
@@ -320,7 +320,7 @@
 X_BIT, Y_BIT, P_BIT, H_BIT = 1, 2, 4, 8
 LOW = jnp.bfloat16
 WIDE = jnp.float32
-VMEM_BYTES = 32 * 1024 * 1024
+VMEM_BYTES = 24 * 1024 * 1024
 COLUMN_GROUPS = ((0, Y_BIT), (X_BIT, Y_BIT), (P_BIT, X_BIT), (P_BIT + Y_BIT, X_BIT))
 ROW_GROUPS = ((0, Y_BIT, 0), (X_BIT, Y_BIT, 0), (0, X_BIT, 1), (Y_BIT, X_BIT, 1))
 

time: 313 us -> 313 us (level)
  no operation moved by 1% of the time
where the time goes in v5:
time: 313 us; the launch traced here: 312 us
  waiting for transfers between devices  114 us (36%)
  starting transfers between devices  89.3 us (29%)
  Pallas kernels  61.8 us (20%)
  other arithmetic  27.7 us (9%)
  local copies, waits for them, and re-layouts  16.3 us (5%)
    ppermute x57, waiting for transfers between devices, swap(): return lax.ppermute(values, 'dp', [(i, i ^ bit) for i in range(16)])  108 us
    pallas_call x11, Pallas kernels, call(): return lambda *operands: made(*operands, *after)  61.8 us
    ppermute x57, starting transfers between devices, swap(): return lax.ppermute(values, 'dp', [(i, i ^ bit) for i in range(16)])  48.1 us
    ppermute x11, starting transfers between devices, swap_core(): return lax.ppermute(values, 'ctx', [(0, 1), (1, 0)])  28.9 us
    add x8, other arithmetic, lion_step(): new_moments.append(BETA_TWO * moment_arr + (1.0 - BETA_TWO) * scaled)  10.1 us
    ppermute x4, starting transfers between devices, row_cross(): return lax.ppermute(values, ('dp', 'ctx'), pairs)  9.45 us
    unnamed x170, local copies, waits for them, and re-layouts  8.46 us
  transfers between devices with their start and end apart: 74, of which 22 were waited for; matrix products, arithmetic and copies ran while one was open for 10% of the time, Pallas kernels for 15%

profile of v5, /device:TPU:1, one launch (start us, length us, event | category | flops | bytes accessed | tf_op | source)
XLA Modules:
  0.0 312.3 jit_solution(7788890409230101822)
XLA Ops:
  15.3 3.8 %collective-permute-start.2 = (bf16[2,144]{1,0:T(2,128)(2,1)S(1)}, bf16[2,144]{1,0:T(2,128)(2,1)S(1)}, u32[]{:S(2)}, u32[]{:S(2)}) collective-permute-start(bf16[2,144]{1,0:T(2,128)(2,1)S(1)} %pad_maximum_fusion.37), channel_id=1, source_target_pairs={{0,16},{2,18},{4,20},{6,22},{8,24},{10,26},{12,28},{14,30},{16,0},... | collective-permute-start | bytes 1736 | tf_op jit(solution)/shard_map/ppermute | solution.py:329
  19.2 8.8 %collective-permute-done.2 = bf16[2,144]{1,0:T(2,128)(2,1)S(1)} collective-permute-done((bf16[2,144]{1,0:T(2,128)(2,1)S(1)}, bf16[2,144]{1,0:T(2,128)(2,1)S(1)}, u32[]{:S(2)}, u32[]{:S(2)}) %collective-permute-start.2) | collective-permute-done | bytes 608 | tf_op jit(solution)/shard_map/ppermute | solution.py:329
  37.3 3.6 %collective-permute-done.5 = bf16[128,1024]{1,0:T(8,128)(2,1)S(1)} collective-permute-done((bf16[128,1024]{1,0:T(8,128)(2,1)S(1)}, bf16[128,1024]{1,0:T(8,128)(2,1)S(1)}, u32[]{:S(2)}, u32[]{:S(2)}) %collective-permute-start.5) | collective-permute-done | bytes 262176 | tf_op jit(solution)/shard_map/ppermute | solution.py:329
  41.0 7.5 %collective-permute-start.6 = (bf16[2,128,1024]{2,1,0:T(8,128)(2,1)S(1)}, bf16[2,128,1024]{2,1,0:T(8,128)(2,1)S(1)}, u32[]{:S(2)}, u32[]{:S(2)}) collective-permute-start(bf16[2,128,1024]{2,1,0:T(8,128)(2,1)S(1)} %pad_maximum_fusion.2.refs_1_), channel_id=1, source_target_pairs={{0,1},{1,0},{2,3},{3,2},{4,5},{5,4},{6,7},{7,6},{8,9},{9,8},{10,11... | collective-permute-start | bytes 1572872 | tf_op jit(solution)/shard_map/ppermute | solution.py:333
  52.3 3.2 %collective-permute-done.11 = bf16[128,1024]{1,0:T(8,128)(2,1)S(1)} collective-permute-done((bf16[128,1024]{1,0:T(8,128)(2,1)S(1)}, bf16[128,1024]{1,0:T(8,128)(2,1)S(1)}, u32[]{:S(2)}, u32[]{:S(2)}) %collective-permute-start.11) | collective-permute-done | bytes 262176 | tf_op jit(solution)/shard_map/ppermute | solution.py:329
  59.1 10.6 %collective-permute-done.19.refs_6_ = bf16[96,1024]{1,0:T(8,128)(2,1)S(1)} collective-permute-done((bf16[96,1024]{1,0:T(8,128)(2,1)S(1)}, bf16[96,1024]{1,0:T(8,128)(2,1)S(1)}, u32[]{:S(2)}, u32[]{:S(2)}) %collective-permute-start.19) | collective-permute-done | bytes 196640 | tf_op jit(solution)/shard_map/ppermute | solution.py:329
  71.5 8.0 %shard_map.331 = (bf16[512,512]{1,0:T(8,128)(2,1)S(1)}, f32[512,768]{1,0:T(8,128)S(1)}, bf16[512,768]{1,0:T(8,128)(2,1)S(1)}, bf16[512,256]{1,0:T(8,128)(2,1)S(1)}, f32[512,128]{1,0:T(8,128)S(1)}) custom-call(s32[9]{0:T(128)S(1)} %pad_add_fusion.1.refs_0_, bf16[2,128,1024]{2,1,0:T(8,128)(2,1)S(1)} %pad_maximum_fusion.2.refs_1_, ...), custom_call_target="tpu_custom_call" | custom-call | flops 2000000000 | bytes 8000000 | tf_op jit(solution)/shard_map/pallas_call | solution.py:440
  81.6 2.7 shard_map.332
  84.3 6.9 %collective-permute-start.21 = (bf16[2,128,1024]{2,1,0:T(8,128)(2,1)S(1)}, bf16[2,128,1024]{2,1,0:T(8,128)(2,1)S(1)}, u32[]{:S(2)}, u32[]{:S(2)}) collective-permute-start(bf16[2,128,1024]{2,1,0:T(8,128)(2,1)S(1)} %get-tuple-element.54), channel_id=1, source_target_pairs={{0,1},{1,0},{2,3},{3,2},{4,5},{5,4},{6,7},{7,6},{8,9},{9,8},{10,11... | collective-permute-start | bytes 1572872 | tf_op jit(solution)/shard_map/ppermute | solution.py:333
  96.0 6.1 %collective-permute-done.29 = bf16[128,1536]{1,0:T(8,128)(2,1)S(1)} collective-permute-done((bf16[128,1536]{1,0:T(8,128)(2,1)S(1)}, bf16[128,1536]{1,0:T(8,128)(2,1)S(1)}, u32[]{:S(2)}, u32[]{:S(2)}) %collective-permute-start.29) | collective-permute-done | bytes 393248 | tf_op jit(solution)/shard_map/ppermute | solution.py:329
  106.3 4.7 %collective-permute-done.23 = bf16[128,1024]{1,0:T(8,128)(2,1)S(1)} collective-permute-done((bf16[128,1024]{1,0:T(8,128)(2,1)S(1)}, bf16[128,1024]{1,0:T(8,128)(2,1)S(1)}, u32[]{:S(2)}, u32[]{:S(2)}) %collective-permute-start.23) | collective-permute-done | bytes 262176 | tf_op jit(solution)/shard_map/ppermute | solution.py:329
  113.8 16.8 %collective-permute-done.32.refs_10_.refs_7_.refs_5_ = bf16[192,1024]{1,0:T(8,128)(2,1)S(1)} collective-permute-done((bf16[192,1024]{1,0:T(8,128)(2,1)S(1)}, bf16[192,1024]{1,0:T(8,128)(2,1)S(1)}, u32[]{:S(2)}, u32[]{:S(2)}) %collective-permute-start.32) | collective-permute-done | bytes 393248 | tf_op jit(solution)/shard_map/ppermute | solution.py:329
  130.6 6.9 %shard_map.333 = (f32[512,1536]{1,0:T(8,128)S(1)}, bf16[512,768]{1,0:T(8,128)(2,1)S(1)}) custom-call(s32[9]{0:T(128)S(1)} %pad_add_fusion.1.refs_0_, bf16[2,128,1024]{2,1,0:T(8,128)(2,1)S(1)} %pad_maximum_fusion.5.refs_1_, bf16[2,128,1024]{2,1,0:T(8,128)(2,1)S(1)} %collective-permute-done.24.refs_2_, bf16[256,1536]{1,0:T(8,128)(2,1)S(1)} %pad_maximum_fusion.refs_3_.refs_8_, ...), custom_call_target="tpu_custom_call" | custom-call | flops 1610612736 | bytes 10000000 | tf_op jit(solution)/shard_map/pallas_call | solution.py:440
  137.5 10.7 %shard_map.334 = (bf16[512,1536]{1,0:T(8,128)(2,1)S(1)}, bf16[2,128,1024]{2,1,0:T(8,128)(2,1)S(1)}, bf16[2,128,1024]{2,1,0:T(8,128)(2,1)S(1)}) custom-call(s32[9]{0:T(128)S(1)} %pad_add_fusion.1.refs_0_, bf16[2,128,1024]{2,1,0:T(8,128)(2,1)S(1)} %pad_maximum_fusion.6.refs_1_.refs_2_, bf16[2,128,1024]{2,1,0:T(8,128)(2,1)S(1)} %collective-permute-done.34.refs_2_.refs_3_, ...), custom_call_target="tpu_custom_call" | custom-call | flops 2415919104 | bytes 12000000 | tf_op jit(solution)/shard_map/pallas_call | solution.py:440
  148.2 3.4 %shard_map.341 = (bf16[192,1024]{1,0:T(8,128)(2,1)S(1)}, bf16[192,1024]{1,0:T(8,128)(2,1)}, bf16[192,1024]{1,0:T(8,128)(2,1)S(1)}, bf16[192,1024]{1,0:T(8,128)(2,1)S(1)}) custom-call(s32[9]{0:T(128)S(1)} %pad_add_fusion.1.refs_0_, bf16[512,768]{1,0:T(8,128)(2,1)S(1)} %get-tuple-element.55.refs_1_, ...), custom_call_target="tpu_custom_call" | custom-call | flops 805306368 | bytes 4000000 | tf_op jit(solution)/shard_map/pallas_call | solution.py:440
  159.3 6.8 %shard_map.340 = (bf16[256,1536]{1,0:T(8,128)(2,1)S(1)}, bf16[256,1536]{1,0:T(8,128)(2,1)S(1)}, bf16[256,1536]{1,0:T(8,128)(2,1)S(1)}, bf16[256,1536]{1,0:T(8,128)(2,1)S(1)}) custom-call(s32[9]{0:T(128)S(1)} %pad_add_fusion.1.refs_0_, bf16[2,128,1024]{2,1,0:T(8,128)(2,1)S(1)} %pad_maximum_fusion.5.refs_1_, bf16[2,128,1024]{2,1,0:T(8,128)(2,1)S(1)} %copy-done.21, ...), custom_call_target="tpu_custom_call" | custom-call | flops 1610612736 | bytes 6000000 | tf_op jit(solution)/shard_map/pallas_call | solution.py:440
  172.0 18.6 %collective-permute-done.64 = bf16[96,1024]{1,0:T(8,128)(2,1)S(1)} collective-permute-done((bf16[96,1024]{1,0:T(8,128)(2,1)S(1)}, bf16[96,1024]{1,0:T(8,128)(2,1)S(1)}, u32[]{:S(2)}, u32[]{:S(2)}) %collective-permute-start.64) | collective-permute-done | bytes 196640 | tf_op jit(solution)/shard_map/ppermute | solution.py:329
  190.8 3.5 %collective-permute-start.67 = (bf16[192,1024]{1,0:T(8,128)(2,1)S(1)}, bf16[192,1024]{1,0:T(8,128)(2,1)S(1)}, u32[]{:S(2)}, u32[]{:S(2)}) collective-permute-start(bf16[192,1024]{1,0:T(8,128)(2,1)S(1)} %pad_maximum_fusion.18), channel_id=1, source_target_pairs={{1,17},{3,19},{5,21},{7,23},{9,25},{11,27},{13,29},{15,31},{16,0},... | collective-permute-start | bytes 1179656 | tf_op jit(solution)/shard_map/ppermute | solution.py:346
  197.4 4.5 %collective-permute-done.67 = bf16[192,1024]{1,0:T(8,128)(2,1)S(1)} collective-permute-done((bf16[192,1024]{1,0:T(8,128)(2,1)S(1)}, bf16[192,1024]{1,0:T(8,128)(2,1)S(1)}, u32[]{:S(2)}, u32[]{:S(2)}) %collective-permute-start.67) | collective-permute-done | bytes 393248 | tf_op jit(solution)/shard_map/ppermute | solution.py:346
  203.4 4.1 %collective-permute-done.37 = bf16[128,1024]{1,0:T(8,128)(2,1)S(1)} collective-permute-done((bf16[128,1024]{1,0:T(8,128)(2,1)S(1)}, bf16[128,1024]{1,0:T(8,128)(2,1)S(1)}, u32[]{:S(2)}, u32[]{:S(2)}) %collective-permute-start.37) | collective-permute-done | bytes 262176 | tf_op jit(solution)/shard_map/ppermute | solution.py:329
  211.5 7.1 %shard_map.335 = (bf16[512,1024]{1,0:T(8,128)(2,1)S(1)}, f32[8,128]{1,0:T(8,128)S(1)}) custom-call(s32[9]{0:T(128)S(1)} %pad_add_fusion.1.refs_0_, bf16[2,128,1024]{2,1,0:T(8,128)(2,1)S(1)} %pad_maximum_fusion.7.refs_1_.refs_2_, bf16[2,128,1024]{2,1,0:T(8,128)(2,1)S(1)} %collective-permute-done.38.refs_2_.refs_3_, bf16[128,1024]{1,0:T(8,128)(2,1)S(1)} %copy-done.9, ...), custom_call_target="tpu_custom_call" | custom-call | flops 2000000000 | bytes 8000000 | tf_op jit(solution)/shard_map/pallas_call | solution.py:440
  218.6 4.9 %shard_map.336 = (bf16[256,1024]{1,0:T(8,128)(2,1)S(1)}, bf16[256,1024]{1,0:T(8,128)(2,1)S(1)}, bf16[256,1024]{1,0:T(8,128)(2,1)S(1)}, bf16[256,1024]{1,0:T(8,128)(2,1)S(1)}) custom-call(s32[9]{0:T(128)S(1)} %pad_add_fusion.1.refs_0_, bf16[2,128,1024]{2,1,0:T(8,128)(2,1)S(1)} %pad_maximum_fusion.2.refs_1_, bf16[2,128,1024]{2,1,0:T(8,128)(2,1)S(1)} %copy-done.17, ...), custom_call_target="tpu_custom_call" | custom-call | flops 1073741824 | bytes 6000000 | tf_op jit(solution)/shard_map/pallas_call | solution.py:440
  223.5 2.7 shard_map.339
  229.3 3.7 %shard_map.337 = (bf16[2,128,1024]{2,1,0:T(8,128)(2,1)S(1)}, bf16[2,128,1024]{2,1,0:T(8,128)(2,1)S(1)}) custom-call(s32[9]{0:T(128)S(1)} %pad_add_fusion.1.refs_0_, bf16[512,768]{1,0:T(8,128)(2,1)S(1)} %copy-done.35, bf16[192,1024]{1,0:T(8,128)(2,1)S(1)} %pad_maximum_fusion.12.refs_7_.refs_4_.refs_2_, bf16[192,1024]{1,0:T(8,128)(2,1)S(1)} %copy-done.24, ...), custom_call_target="tpu_custom_call" | custom-call | flops 805306368 | bytes 4000000 | tf_op jit(solution)/shard_map/pallas_call | solution.py:440
  233.0 4.9 %shard_map.338 = (bf16[2,128,1024]{2,1,0:T(8,128)(2,1)S(1)}, bf16[2,128,1024]{2,1,0:T(8,128)(2,1)S(1)}) custom-call(s32[9]{0:T(128)S(1)} %pad_add_fusion.1.refs_0_, bf16[512,1024]{1,0:T(8,128)(2,1)S(1)} %get-tuple-element.63.refs_3_.refs_1_, bf16[256,1024]{1,0:T(8,128)(2,1)S(1)} %pad_maximum_fusion.3.refs_3_.refs_2_, bf16[256,1024]{1,0:T(8,128)(2,1)S(1)} %copy-done.19, ...), custom_call_target="tpu_custom_call" | custom-call | flops 1073741824 | bytes 5000000 | tf_op jit(solution)/shard_map/pallas_call | solution.py:440
  238.1 5.2 %collective-permute-done.61 = bf16[64,1536]{1,0:T(8,128)(2,1)S(1)} collective-permute-done((bf16[64,1536]{1,0:T(8,128)(2,1)S(1)}, bf16[64,1536]{1,0:T(8,128)(2,1)S(1)}, u32[]{:S(2)}, u32[]{:S(2)}) %collective-permute-start.61) | collective-permute-done | bytes 196640 | tf_op jit(solution)/shard_map/ppermute | solution.py:329
  246.3 4.0 %collective-permute-done.51 = bf16[64,1024]{1,0:T(8,128)(2,1)S(1)} collective-permute-done((bf16[64,1024]{1,0:T(8,128)(2,1)S(1)}, bf16[64,1024]{1,0:T(8,128)(2,1)S(1)}, u32[]{:S(2)}, u32[]{:S(2)}) %collective-permute-start.51) | collective-permute-done | bytes 131104 | tf_op jit(solution)/shard_map/ppermute | solution.py:329
  250.5 3.6 %collective-permute-done.53 = bf16[64,1024]{1,0:T(8,128)(2,1)S(1)} collective-permute-done((bf16[64,1024]{1,0:T(8,128)(2,1)S(1)}, bf16[64,1024]{1,0:T(8,128)(2,1)S(1)}, u32[]{:S(2)}, u32[]{:S(2)}) %collective-permute-start.53) | collective-permute-done | bytes 131104 | tf_op jit(solution)/shard_map/ppermute | solution.py:329
  256.7 3.3 %collective-permute-start.54 = (bf16[128,1024]{1,0:T(8,128)(2,1)S(1)}, bf16[128,1024]{1,0:T(8,128)(2,1)S(1)}, u32[]{:S(2)}, u32[]{:S(2)}) collective-permute-start(bf16[128,1024]{1,0:T(8,128)(2,1)S(1)} %pad_maximum_fusion.28), channel_id=1, source_target_pairs={{1,17},{3,19},{5,21},{7,23},{9,25},{11,27},{13,29},{15,31},{16,0},... | collective-permute-start | bytes 786440 | tf_op jit(solution)/shard_map/ppermute | solution.py:346
  281.8 10.5 %collective-permute-done.71 = bf16[16,144]{1,0:T(8,128)(2,1)S(1)} collective-permute-done((bf16[16,144]{1,0:T(8,128)(2,1)S(1)}, bf16[16,144]{1,0:T(8,128)(2,1)S(1)}, u32[]{:S(2)}, u32[]{:S(2)}) %collective-permute-start.71) | collective-permute-done | bytes 4640 | tf_op jit(solution)/shard_map/ppermute | solution.py:329
  299.3 3.2 %collective-permute-done.48 = bf16[64,1024]{1,0:T(8,128)(2,1)S(1)} collective-permute-done((bf16[64,1024]{1,0:T(8,128)(2,1)S(1)}, bf16[64,1024]{1,0:T(8,128)(2,1)S(1)}, u32[]{:S(2)}, u32[]{:S(2)}) %collective-permute-start.48) | collective-permute-done | bytes 131104 | tf_op jit(solution)/shard_map/ppermute | solution.py:329
  302.6 3.6 %collective-permute-start.49 = (bf16[2,64,1024]{2,1,0:T(8,128)(2,1)S(1)}, bf16[2,64,1024]{2,1,0:T(8,128)(2,1)S(1)}, u32[]{:S(2)}, u32[]{:S(2)}) collective-permute-start(bf16[2,64,1024]{2,1,0:T(8,128)(2,1)S(1)} %pad_maximum_fusion.26), channel_id=1, source_target_pairs={{0,1},{1,0},{2,3},{3,2},{4,5},{5,4},{6,7},{7,6},{8,9},{9,8},{10,11... | collective-permute-start | bytes 786440 | tf_op jit(solution)/shard_map/ppermute | solution.py:333
  (457 shorter events, 111.4 us)
Async XLA Ops:
  6.2 28.3 %collective-permute-start.7 = (bf16[64,1024]{1,0:T(8,128)(2,1)}, bf16[64,1024]{1,0:T(8,128)(2,1)S(1)}, u32[]{:S(2)}, u32[]{:S(2)}) collective-permute-start(bf16[64,1024]{1,0:T(8,128)(2,1)} %pad_maximum_fusion.30), channel_id=1, source_target_pairs={{0,8},{2,10},{4,12},{6,14},{8,0},{10,2},{12,4},{14,6},{16,24},{18,... | collective-permute-start | bytes 393224 | tf_op jit(solution)/shard_map/ppermute | solution.py:329
  8.8 25.9 %collective-permute-start.13 = (bf16[128,1024]{1,0:T(8,128)(2,1)S(1)}, bf16[128,1024]{1,0:T(8,128)(2,1)S(1)}, u32[]{:S(2)}, u32[]{:S(2)}) collective-permute-start(bf16[128,1024]{1,0:T(8,128)(2,1)S(1)} %convert_element_type.387), channel_id=1, source_target_pairs={{0,16},{2,18},{4,20},{6,22},{8,24},{10,26},{12,28},{14,30},{17,1},... | collective-permute-start | bytes 786440 | tf_op jit(solution)/shard_map/ppermute | solution.py:346
  11.4 23.2 %collective-permute-start.25 = (bf16[64,1536]{1,0:T(8,128)(2,1)S(1)}, bf16[64,1536]{1,0:T(8,128)(2,1)S(1)}, u32[]{:S(2)}, u32[]{:S(2)}) collective-permute-start(bf16[64,1536]{1,0:T(8,128)(2,1)S(1)} %pad_maximum_fusion.29), channel_id=1, source_target_pairs={{0,8},{2,10},{4,12},{6,14},{8,0},{10,2},{12,4},{14,6},{16,24},{18,... | collective-permute-start | bytes 589832 | tf_op jit(solution)/shard_map/ppermute | solution.py:329
  14.0 35.9 %collective-permute-start.18 = (bf16[192,1024]{1,0:T(8,128)(2,1)}, bf16[192,1024]{1,0:T(8,128)(2,1)}, u32[]{:S(2)}, u32[]{:S(2)}) collective-permute-start(bf16[192,1024]{1,0:T(8,128)(2,1)} %convert_element_type.388), channel_id=1, source_target_pairs={{0,16},{2,18},{4,20},{6,22},{8,24},{10,26},{12,28},{14,30},{17,1},... | collective-permute-start | bytes 1179656 | tf_op jit(solution)/shard_map/ppermute | solution.py:346
  34.8 22.4 %collective-permute-start.16 = (bf16[64,1024]{1,0:T(8,128)(2,1)S(1)}, bf16[64,1024]{1,0:T(8,128)(2,1)S(1)}, u32[]{:S(2)}, u32[]{:S(2)}) collective-permute-start(bf16[64,1024]{1,0:T(8,128)(2,1)S(1)} %get-tuple-element.146), channel_id=1, source_target_pairs={{0,2},{2,0},{4,6},{6,4},{8,10},{10,8},{12,14},{14,12},{16,18},{18,... | collective-permute-start | bytes 393224 | tf_op jit(solution)/shard_map/ppermute | solution.py:329
  36.1 22.5 %collective-permute-start.14 = (bf16[64,1024]{1,0:T(8,128)(2,1)S(1)}, bf16[64,1024]{1,0:T(8,128)(2,1)S(1)}, u32[]{:S(2)}, u32[]{:S(2)}) collective-permute-start(bf16[64,1024]{1,0:T(8,128)(2,1)S(1)} %get-tuple-element.147), channel_id=1, source_target_pairs={{0,4},{2,6},{4,0},{6,2},{8,12},{10,14},{12,8},{14,10},{16,20},{18,... | collective-permute-start | bytes 393224 | tf_op jit(solution)/shard_map/ppermute | solution.py:329
  41.0 29.9 %collective-permute-start.6 = (bf16[2,128,1024]{2,1,0:T(8,128)(2,1)S(1)}, bf16[2,128,1024]{2,1,0:T(8,128)(2,1)S(1)}, u32[]{:S(2)}, u32[]{:S(2)}) collective-permute-start(bf16[2,128,1024]{2,1,0:T(8,128)(2,1)S(1)} %pad_maximum_fusion.2.refs_1_), channel_id=1, source_target_pairs={{0,1},{1,0},{2,3},{3,2},{4,5},{5,4},{6,7},{7,6},{8,9},{9,8},{10,11... | collective-permute-start | bytes 1572872 | tf_op jit(solution)/shard_map/ppermute | solution.py:333
  58.6 32.6 %collective-permute-start.26 = (bf16[128,1536]{1,0:T(8,128)(2,1)S(1)}, bf16[128,1536]{1,0:T(8,128)(2,1)S(1)}, u32[]{:S(2)}, u32[]{:S(2)}) collective-permute-start(bf16[128,1536]{1,0:T(8,128)(2,1)S(1)} %pad_maximum_fusion.8), channel_id=1, source_target_pairs={{0,16},{2,18},{4,20},{6,22},{8,24},{10,26},{12,28},{14,30},{16,0},... | collective-permute-start | bytes 1179656 | tf_op jit(solution)/shard_map/ppermute | solution.py:329
  71.4 41.8 %collective-permute-start.33 = (bf16[128,1024]{1,0:T(8,128)(2,1)S(1)}, bf16[128,1024]{1,0:T(8,128)(2,1)S(1)}, u32[]{:S(2)}, u32[]{:S(2)}) collective-permute-start(bf16[128,1024]{1,0:T(8,128)(2,1)S(1)} %bitcast.128), channel_id=1, source_target_pairs={{0,8},{2,10},{4,12},{6,14},{8,0},{10,2},{12,4},{14,6},{16,24},{18,... | collective-permute-start | bytes 786440 | tf_op jit(solution)/shard_map/ppermute | solution.py:329
  80.3 33.1 %collective-permute-start.31 = (bf16[192,1024]{1,0:T(8,128)(2,1)S(1)}, bf16[192,1024]{1,0:T(8,128)(2,1)S(1)}, u32[]{:S(2)}, u32[]{:S(2)}) collective-permute-start(bf16[192,1024]{1,0:T(8,128)(2,1)S(1)} %pad_maximum_fusion.12.refs_7_.refs_4_.refs_2_), channel_id=1, source_target_pairs={{0,2},{2,0},{4,6},{6,4},{8,10},{10,8},{12,14},{14,12},{16,18},{18,... | collective-permute-start | bytes 1179656 | tf_op jit(solution)/shard_map/ppermute | solution.py:329
  102.2 28.3 %collective-permute-start.30 = (bf16[256,1536]{1,0:T(8,128)(2,1)S(1)}, bf16[256,1536]{1,0:T(8,128)(2,1)S(1)}, u32[]{:S(2)}, u32[]{:S(2)}) collective-permute-start(bf16[256,1536]{1,0:T(8,128)(2,1)S(1)} %pad_maximum_fusion.1.refs_5_.refs_10_), channel_id=1, source_target_pairs={{0,4},{2,6},{4,0},{6,2},{8,12},{10,14},{12,8},{14,10},{16,20},{18,... | collective-permute-start | bytes 2359304 | tf_op jit(solution)/shard_map/ppermute | solution.py:329
  105.6 24.9 %collective-permute-start.28 = (bf16[256,1536]{1,0:T(8,128)(2,1)S(1)}, bf16[256,1536]{1,0:T(8,128)(2,1)S(1)}, u32[]{:S(2)}, u32[]{:S(2)}) collective-permute-start(bf16[256,1536]{1,0:T(8,128)(2,1)S(1)} %pad_maximum_fusion.refs_3_.refs_8_), channel_id=1, source_target_pairs={{0,2},{2,0},{4,6},{6,4},{8,10},{10,8},{12,14},{14,12},{16,18},{18,... | collective-permute-start | bytes 2359304 | tf_op jit(solution)/shard_map/ppermute | solution.py:329
  111.1 19.4 %collective-permute-start.24 = (bf16[2,128,1024]{2,1,0:T(8,128)(2,1)S(1)}, bf16[2,128,1024]{2,1,0:T(8,128)(2,1)S(1)}, u32[]{:S(2)}, u32[]{:S(2)}) collective-permute-start(bf16[2,128,1024]{2,1,0:T(8,128)(2,1)S(1)} %pad_maximum_fusion.5.refs_1_), channel_id=1, source_target_pairs={{0,1},{1,0},{2,3},{3,2},{4,5},{5,4},{6,7},{7,6},{8,9},{9,8},{10,11... | collective-permute-start | bytes 1572872 | tf_op jit(solution)/shard_map/ppermute | solution.py:333
  113.2 17.3 %collective-permute-start.32 = (bf16[192,1024]{1,0:T(8,128)(2,1)S(1)}, bf16[192,1024]{1,0:T(8,128)(2,1)S(1)}, u32[]{:S(2)}, u32[]{:S(2)}) collective-permute-start(bf16[192,1024]{1,0:T(8,128)(2,1)S(1)} %pad_maximum_fusion.13.refs_9_.refs_6_.refs_4_), channel_id=1, source_target_pairs={{0,4},{2,6},{4,0},{6,2},{8,12},{10,14},{12,8},{14,10},{16,20},{18,... | collective-permute-start | bytes 1179656 | tf_op jit(solution)/shard_map/ppermute | solution.py:329
  113.4 24.1 %collective-permute-start.34 = (bf16[2,128,1024]{2,1,0:T(8,128)(2,1)S(1)}, bf16[2,128,1024]{2,1,0:T(8,128)(2,1)S(1)}, u32[]{:S(2)}, u32[]{:S(2)}) collective-permute-start(bf16[2,128,1024]{2,1,0:T(8,128)(2,1)S(1)} %pad_maximum_fusion.6.refs_1_.refs_2_), channel_id=1, source_target_pairs={{0,1},{1,0},{2,3},{3,2},{4,5},{5,4},{6,7},{7,6},{8,9},{9,8},{10,11... | collective-permute-start | bytes 1572872 | tf_op jit(solution)/shard_map/ppermute | solution.py:333
  153.9 16.4 %collective-permute-start.65 = (bf16[192,1024]{1,0:T(8,128)(2,1)}, bf16[192,1024]{1,0:T(8,128)(2,1)S(1)}, u32[]{:S(2)}, u32[]{:S(2)}) collective-permute-start(bf16[192,1024]{1,0:T(8,128)(2,1)} %copy-done.27), channel_id=1, source_target_pairs={{0,4},{2,6},{4,0},{6,2},{8,12},{10,14},{12,8},{14,10},{16,20},{18,... | collective-permute-start | bytes 1179656 | tf_op jit(solution)/shard_map/ppermute | solution.py:329
  155.0 15.6 %collective-permute-start.35 = (bf16[2,128,1024]{2,1,0:T(8,128)(2,1)}, bf16[2,128,1024]{2,1,0:T(8,128)(2,1)S(1)}, u32[]{:S(2)}, u32[]{:S(2)}) collective-permute-start(bf16[2,128,1024]{2,1,0:T(8,128)(2,1)} %copy-done.22), channel_id=1, source_target_pairs={{0,1},{1,0},{2,3},{3,2},{4,5},{5,4},{6,7},{7,6},{8,9},{9,8},{10,11... | collective-permute-start | bytes 1572872 | tf_op jit(solution)/shard_map/ppermute | solution.py:333
  166.2 30.2 %collective-permute-start.56 = (bf16[256,1536]{1,0:T(8,128)(2,1)S(1)}, bf16[256,1536]{1,0:T(8,128)(2,1)S(1)}, u32[]{:S(2)}, u32[]{:S(2)}) collective-permute-start(bf16[256,1536]{1,0:T(8,128)(2,1)S(1)} %get-tuple-element.78), channel_id=1, source_target_pairs={{0,2},{2,0},{4,6},{6,4},{8,10},{10,8},{12,14},{14,12},{16,18},{18,... | collective-permute-start | bytes 2359304 | tf_op jit(solution)/shard_map/ppermute | solution.py:329
  167.6 29.3 %collective-permute-start.58 = (bf16[256,1536]{1,0:T(8,128)(2,1)S(1)}, bf16[256,1536]{1,0:T(8,128)(2,1)S(1)}, u32[]{:S(2)}, u32[]{:S(2)}) collective-permute-start(bf16[256,1536]{1,0:T(8,128)(2,1)S(1)} %get-tuple-element.80), channel_id=1, source_target_pairs={{0,4},{2,6},{4,0},{6,2},{8,12},{10,14},{12,8},{14,10},{16,20},{18,... | collective-permute-start | bytes 2359304 | tf_op jit(solution)/shard_map/ppermute | solution.py:329
  168.9 21.7 %collective-permute-start.64 = (bf16[96,1024]{1,0:T(8,128)(2,1)S(1)}, bf16[96,1024]{1,0:T(8,128)(2,1)S(1)}, u32[]{:S(2)}, u32[]{:S(2)}) collective-permute-start(bf16[96,1024]{1,0:T(8,128)(2,1)S(1)} %slice.399), channel_id=1, source_target_pairs={{0,4},{2,6},{4,0},{6,2},{8,12},{10,14},{12,8},{14,10},{16,20},{18,... | collective-permute-start | bytes 589832 | tf_op jit(solution)/shard_map/ppermute | solution.py:329
  170.4 20.3 %collective-permute-start.66 = (bf16[96,1024]{1,0:T(8,128)(2,1)S(1)}, bf16[96,1024]{1,0:T(8,128)(2,1)S(1)}, u32[]{:S(2)}, u32[]{:S(2)}) collective-permute-start(bf16[96,1024]{1,0:T(8,128)(2,1)S(1)} %slice.401), channel_id=1, source_target_pairs={{0,2},{2,0},{4,6},{6,4},{8,10},{10,8},{12,14},{14,12},{16,18},{18,... | collective-permute-start | bytes 589832 | tf_op jit(solution)/shard_map/ppermute | solution.py:329
  170.9 23.4 %collective-permute-start.36 = (bf16[128,1024]{1,0:T(8,128)(2,1)S(1)}, bf16[128,1024]{1,0:T(8,128)(2,1)S(1)}, u32[]{:S(2)}, u32[]{:S(2)}) collective-permute-start(bf16[128,1024]{1,0:T(8,128)(2,1)S(1)} %fusion.37), channel_id=1, source_target_pairs={{0,8},{2,10},{4,12},{6,14},{8,0},{10,2},{12,4},{14,6},{16,24},{18,... | collective-permute-start | bytes 786440 | tf_op jit(solution)/shard_map/ppermute | solution.py:329
  208.8 29.1 %collective-permute-start.60 = (bf16[128,1536]{1,0:T(8,128)(2,1)S(1)}, bf16[128,1536]{1,0:T(8,128)(2,1)S(1)}, u32[]{:S(2)}, u32[]{:S(2)}) collective-permute-start(bf16[128,1536]{1,0:T(8,128)(2,1)S(1)} %pad_maximum_fusion.14), channel_id=1, source_target_pairs={{0,16},{2,18},{4,20},{6,22},{8,24},{10,26},{12,28},{14,30},{16,0},... | collective-permute-start | bytes 1179656 | tf_op jit(solution)/shard_map/ppermute | solution.py:329
  226.3 19.2 %collective-permute-start.50 = (bf16[128,1024]{1,0:T(8,128)(2,1)S(1)}, bf16[128,1024]{1,0:T(8,128)(2,1)S(1)}, u32[]{:S(2)}, u32[]{:S(2)}) collective-permute-start(bf16[128,1024]{1,0:T(8,128)(2,1)S(1)} %get-tuple-element.73), channel_id=1, source_target_pairs={{0,2},{2,0},{4,6},{6,4},{8,10},{10,8},{12,14},{14,12},{16,18},{18,... | collective-permute-start | bytes 786440 | tf_op jit(solution)/shard_map/ppermute | solution.py:329
  226.5 19.2 %collective-permute-start.52 = (bf16[128,1024]{1,0:T(8,128)(2,1)S(1)}, bf16[128,1024]{1,0:T(8,128)(2,1)S(1)}, u32[]{:S(2)}, u32[]{:S(2)}) collective-permute-start(bf16[128,1024]{1,0:T(8,128)(2,1)S(1)} %get-tuple-element.75), channel_id=1, source_target_pairs={{0,4},{2,6},{4,0},{6,2},{8,12},{10,14},{12,8},{14,10},{16,20},{18,... | collective-permute-start | bytes 786440 | tf_op jit(solution)/shard_map/ppermute | solution.py:329
  227.5 29.2 %collective-permute-start.43 = (bf16[256,1024]{1,0:T(8,128)(2,1)S(1)}, bf16[256,1024]{1,0:T(8,128)(2,1)S(1)}, u32[]{:S(2)}, u32[]{:S(2)}) collective-permute-start(bf16[256,1024]{1,0:T(8,128)(2,1)S(1)} %get-tuple-element.69), channel_id=1, source_target_pairs={{0,2},{2,0},{4,6},{6,4},{8,10},{10,8},{12,14},{14,12},{16,18},{18,... | collective-permute-start | bytes 1572872 | tf_op jit(solution)/shard_map/ppermute | solution.py:329
  228.1 32.9 %collective-permute-start.45 = (bf16[256,1024]{1,0:T(8,128)(2,1)S(1)}, bf16[256,1024]{1,0:T(8,128)(2,1)S(1)}, u32[]{:S(2)}, u32[]{:S(2)}) collective-permute-start(bf16[256,1024]{1,0:T(8,128)(2,1)S(1)} %get-tuple-element.71), channel_id=1, source_target_pairs={{0,4},{2,6},{4,0},{6,2},{8,12},{10,14},{12,8},{14,10},{16,20},{18,... | collective-permute-start | bytes 1572872 | tf_op jit(solution)/shard_map/ppermute | solution.py:329
  243.3 19.4 %collective-permute-start.41 = (bf16[2,128,1024]{2,1,0:T(8,128)(2,1)S(1)}, bf16[2,128,1024]{2,1,0:T(8,128)(2,1)S(1)}, u32[]{:S(2)}, u32[]{:S(2)}) collective-permute-start(bf16[2,128,1024]{2,1,0:T(8,128)(2,1)S(1)} %get-tuple-element.68), channel_id=1, source_target_pairs={{0,1},{1,0},{2,3},{3,2},{4,5},{5,4},{6,7},{7,6},{8,9},{9,8},{10,11... | collective-permute-start | bytes 1572872 | tf_op jit(solution)/shard_map/ppermute | solution.py:333
  245.5 18.1 %collective-permute-start.39 = (bf16[2,128,1024]{2,1,0:T(8,128)(2,1)S(1)}, bf16[2,128,1024]{2,1,0:T(8,128)(2,1)S(1)}, u32[]{:S(2)}, u32[]{:S(2)}) collective-permute-start(bf16[2,128,1024]{2,1,0:T(8,128)(2,1)S(1)} %get-tuple-element.66), channel_id=1, source_target_pairs={{0,1},{1,0},{2,3},{3,2},{4,5},{5,4},{6,7},{7,6},{8,9},{9,8},{10,11... | collective-permute-start | bytes 1572872 | tf_op jit(solution)/shard_map/ppermute | solution.py:333
  264.8 31.9 %collective-permute-start.40 = (bf16[128,1024]{1,0:T(8,128)(2,1)}, bf16[128,1024]{1,0:T(8,128)(2,1)}, u32[]{:S(2)}, u32[]{:S(2)}) collective-permute-start(bf16[128,1024]{1,0:T(8,128)(2,1)} %fusion.39), channel_id=1, source_target_pairs={{0,8},{2,10},{4,12},{6,14},{8,0},{10,2},{12,4},{14,6},{16,24},{18,... | collective-permute-start | bytes 786440 | tf_op jit(solution)/shard_map/ppermute | solution.py:329
  271.4 34.7 %collective-permute-start.55 = (bf16[128,1024]{1,0:T(8,128)(2,1)}, bf16[128,1024]{1,0:T(8,128)(2,1)}, u32[]{:S(2)}, u32[]{:S(2)}) collective-permute-start(bf16[128,1024]{1,0:T(8,128)(2,1)} %add_convert_fusion.10), channel_id=1, source_target_pairs={{0,1},{2,3},{4,5},{6,7},{8,9},{10,11},{12,13},{14,15},{17,16},{19,... | collective-permute-start | bytes 786440 | tf_op jit(solution)/shard_map/ppermute | solution.py:397
  277.8 20.8 %collective-permute-start.47 = (bf16[128,1024]{1,0:T(8,128)(2,1)S(1)}, bf16[128,1024]{1,0:T(8,128)(2,1)S(1)}, u32[]{:S(2)}, u32[]{:S(2)}) collective-permute-start(bf16[128,1024]{1,0:T(8,128)(2,1)S(1)} %pad_maximum_fusion.25), channel_id=1, source_target_pairs={{0,16},{2,18},{4,20},{6,22},{8,24},{10,26},{12,28},{14,30},{16,0},... | collective-permute-start | bytes 786440 | tf_op jit(solution)/shard_map/ppermute | solution.py:329
  (127 other events, 1146.9 us)

commit v6 on v5

--- a/solution.py
+++ b/solution.py
@@ -603,8 +603,8 @@
     for at in range(0, 768, 256):
         gate = matmul(tokens, whole[:, at : at + 256])
         upward = matmul(tokens, whole[:, 768 + at : 1024 + at])
-        gate_up[:, at : at + 256] = gate
-        gate_up[:, 768 + at : 1024 + at] = upward
+        gate_up[:, at : at + 256] = gate.astype(LOW)
+        gate_up[:, 768 + at : 1024 + at] = upward.astype(LOW)
         active[:, at : at + 256] = (gate * jax.nn.sigmoid(gate) * upward).astype(LOW)
 
 
@@ -612,7 +612,7 @@
     return call(
         gate_kernel,
         [SM, VM, VM, HB, HB, HB, HB],
-        [((512, 1536), WIDE), ((512, 768), LOW)],
+        [((512, 1536), LOW), ((512, 768), LOW)],
         [VM] * 2,
         [pltpu.VMEM((1024, 1536), LOW), pltpu.SemaphoreType.DMA((16,))],
         2 * 512 * 1024 * 1536,
@@ -633,8 +633,8 @@
     wait_all(down_copies)
     for at in range(0, 768, 256):
         grad_active = contract_cols(grad_out, down[at : at + 256])
-        gate = gate_up[:, at : at + 256]
-        upward = gate_up[:, 768 + at : 1024 + at]
+        gate = gate_up[:, at : at + 256].astype(WIDE)
+        upward = gate_up[:, 768 + at : 1024 + at].astype(WIDE)
         sigmoid = jax.nn.sigmoid(gate)
         grad_gate_up[:, at : at + 256] = (
             grad_active * upward * (sigmoid * (1.0 + gate * (1.0 - sigmoid)))

time: 313 us -> 313 us (level)
  no operation moved by 1% of the time
where the time goes in v6:
time: 313 us; the launch traced here: 312 us
  waiting for transfers between devices  115 us (37%)
  starting transfers between devices  89.2 us (28%)
  Pallas kernels  61.8 us (20%)
  other arithmetic  27.7 us (9%)
  local copies, waits for them, and re-layouts  16.3 us (5%)
    ppermute x57, waiting for transfers between devices, swap(): return lax.ppermute(values, 'dp', [(i, i ^ bit) for i in range(16)])  108 us
    pallas_call x11, Pallas kernels, call(): return lambda *operands: made(*operands, *after)  61.8 us
    ppermute x57, starting transfers between devices, swap(): return lax.ppermute(values, 'dp', [(i, i ^ bit) for i in range(16)])  48.1 us
    ppermute x11, starting transfers between devices, swap_core(): return lax.ppermute(values, 'ctx', [(0, 1), (1, 0)])  28.9 us
    add x8, other arithmetic, lion_step(): new_moments.append(BETA_TWO * moment_arr + (1.0 - BETA_TWO) * scaled)  10.1 us
    ppermute x4, starting transfers between devices, row_cross(): return lax.ppermute(values, ('dp', 'ctx'), pairs)  9.44 us
    unnamed x170, local copies, waits for them, and re-layouts  8.46 us
  transfers between devices with their start and end apart: 74, of which 22 were waited for; matrix products, arithmetic and copies ran while one was open for 10% of the time, Pallas kernels for 15%

profile of v6, /device:TPU:1, one launch (start us, length us, event | category | flops | bytes accessed | tf_op | source)
XLA Modules:
  0.0 312.4 jit_solution(14243128604137916915)
XLA Ops:
  15.3 3.8 %collective-permute-start.2 = (bf16[2,144]{1,0:T(2,128)(2,1)S(1)}, bf16[2,144]{1,0:T(2,128)(2,1)S(1)}, u32[]{:S(2)}, u32[]{:S(2)}) collective-permute-start(bf16[2,144]{1,0:T(2,128)(2,1)S(1)} %pad_maximum_fusion.37), channel_id=1, source_target_pairs={{0,16},{2,18},{4,20},{6,22},{8,24},{10,26},{12,28},{14,30},{16,0},... | collective-permute-start | bytes 1736 | tf_op jit(solution)/shard_map/ppermute | solution.py:329
  19.2 8.8 %collective-permute-done.2 = bf16[2,144]{1,0:T(2,128)(2,1)S(1)} collective-permute-done((bf16[2,144]{1,0:T(2,128)(2,1)S(1)}, bf16[2,144]{1,0:T(2,128)(2,1)S(1)}, u32[]{:S(2)}, u32[]{:S(2)}) %collective-permute-start.2) | collective-permute-done | bytes 608 | tf_op jit(solution)/shard_map/ppermute | solution.py:329
  37.3 3.6 %collective-permute-done.5 = bf16[128,1024]{1,0:T(8,128)(2,1)S(1)} collective-permute-done((bf16[128,1024]{1,0:T(8,128)(2,1)S(1)}, bf16[128,1024]{1,0:T(8,128)(2,1)S(1)}, u32[]{:S(2)}, u32[]{:S(2)}) %collective-permute-start.5) | collective-permute-done | bytes 262176 | tf_op jit(solution)/shard_map/ppermute | solution.py:329
  41.0 7.5 %collective-permute-start.6 = (bf16[2,128,1024]{2,1,0:T(8,128)(2,1)S(1)}, bf16[2,128,1024]{2,1,0:T(8,128)(2,1)S(1)}, u32[]{:S(2)}, u32[]{:S(2)}) collective-permute-start(bf16[2,128,1024]{2,1,0:T(8,128)(2,1)S(1)} %pad_maximum_fusion.2.refs_1_), channel_id=1, source_target_pairs={{0,1},{1,0},{2,3},{3,2},{4,5},{5,4},{6,7},{7,6},{8,9},{9,8},{10,11... | collective-permute-start | bytes 1572872 | tf_op jit(solution)/shard_map/ppermute | solution.py:333
  52.3 3.2 %collective-permute-done.11 = bf16[128,1024]{1,0:T(8,128)(2,1)S(1)} collective-permute-done((bf16[128,1024]{1,0:T(8,128)(2,1)S(1)}, bf16[128,1024]{1,0:T(8,128)(2,1)S(1)}, u32[]{:S(2)}, u32[]{:S(2)}) %collective-permute-start.11) | collective-permute-done | bytes 262176 | tf_op jit(solution)/shard_map/ppermute | solution.py:329
  59.1 10.6 %collective-permute-done.19.refs_6_ = bf16[96,1024]{1,0:T(8,128)(2,1)S(1)} collective-permute-done((bf16[96,1024]{1,0:T(8,128)(2,1)S(1)}, bf16[96,1024]{1,0:T(8,128)(2,1)S(1)}, u32[]{:S(2)}, u32[]{:S(2)}) %collective-permute-start.19) | collective-permute-done | bytes 196640 | tf_op jit(solution)/shard_map/ppermute | solution.py:329
  71.5 8.0 %shard_map.331 = (bf16[512,512]{1,0:T(8,128)(2,1)S(1)}, f32[512,768]{1,0:T(8,128)S(1)}, bf16[512,768]{1,0:T(8,128)(2,1)S(1)}, bf16[512,256]{1,0:T(8,128)(2,1)S(1)}, f32[512,128]{1,0:T(8,128)S(1)}) custom-call(s32[9]{0:T(128)S(1)} %pad_add_fusion.1.refs_0_, bf16[2,128,1024]{2,1,0:T(8,128)(2,1)S(1)} %pad_maximum_fusion.2.refs_1_, ...), custom_call_target="tpu_custom_call" | custom-call | flops 2000000000 | bytes 8000000 | tf_op jit(solution)/shard_map/pallas_call | solution.py:440
  81.6 2.7 shard_map.332
  84.3 6.9 %collective-permute-start.21 = (bf16[2,128,1024]{2,1,0:T(8,128)(2,1)S(1)}, bf16[2,128,1024]{2,1,0:T(8,128)(2,1)S(1)}, u32[]{:S(2)}, u32[]{:S(2)}) collective-permute-start(bf16[2,128,1024]{2,1,0:T(8,128)(2,1)S(1)} %get-tuple-element.54), channel_id=1, source_target_pairs={{0,1},{1,0},{2,3},{3,2},{4,5},{5,4},{6,7},{7,6},{8,9},{9,8},{10,11... | collective-permute-start | bytes 1572872 | tf_op jit(solution)/shard_map/ppermute | solution.py:333
  96.0 6.1 %collective-permute-done.29 = bf16[128,1536]{1,0:T(8,128)(2,1)S(1)} collective-permute-done((bf16[128,1536]{1,0:T(8,128)(2,1)S(1)}, bf16[128,1536]{1,0:T(8,128)(2,1)S(1)}, u32[]{:S(2)}, u32[]{:S(2)}) %collective-permute-start.29) | collective-permute-done | bytes 393248 | tf_op jit(solution)/shard_map/ppermute | solution.py:329
  106.3 4.7 %collective-permute-done.23 = bf16[128,1024]{1,0:T(8,128)(2,1)S(1)} collective-permute-done((bf16[128,1024]{1,0:T(8,128)(2,1)S(1)}, bf16[128,1024]{1,0:T(8,128)(2,1)S(1)}, u32[]{:S(2)}, u32[]{:S(2)}) %collective-permute-start.23) | collective-permute-done | bytes 262176 | tf_op jit(solution)/shard_map/ppermute | solution.py:329
  113.8 16.8 %collective-permute-done.32.refs_10_.refs_7_.refs_5_ = bf16[192,1024]{1,0:T(8,128)(2,1)S(1)} collective-permute-done((bf16[192,1024]{1,0:T(8,128)(2,1)S(1)}, bf16[192,1024]{1,0:T(8,128)(2,1)S(1)}, u32[]{:S(2)}, u32[]{:S(2)}) %collective-permute-start.32) | collective-permute-done | bytes 393248 | tf_op jit(solution)/shard_map/ppermute | solution.py:329
  130.6 6.9 %shard_map.333 = (bf16[512,1536]{1,0:T(8,128)(2,1)S(1)}, bf16[512,768]{1,0:T(8,128)(2,1)S(1)}) custom-call(s32[9]{0:T(128)S(1)} %pad_add_fusion.1.refs_0_, bf16[2,128,1024]{2,1,0:T(8,128)(2,1)S(1)} %pad_maximum_fusion.5.refs_1_, bf16[2,128,1024]{2,1,0:T(8,128)(2,1)S(1)} %collective-permute-done.24.refs_2_, ...), custom_call_target="tpu_custom_call" | custom-call | flops 1610612736 | bytes 10000000 | tf_op jit(solution)/shard_map/pallas_call | solution.py:440
  137.5 10.8 %shard_map.334 = (bf16[512,1536]{1,0:T(8,128)(2,1)S(1)}, bf16[2,128,1024]{2,1,0:T(8,128)(2,1)S(1)}, bf16[2,128,1024]{2,1,0:T(8,128)(2,1)S(1)}) custom-call(s32[9]{0:T(128)S(1)} %pad_add_fusion.1.refs_0_, bf16[2,128,1024]{2,1,0:T(8,128)(2,1)S(1)} %pad_maximum_fusion.6.refs_1_.refs_2_, bf16[2,128,1024]{2,1,0:T(8,128)(2,1)S(1)} %collective-permute-done.34.refs_2_.refs_3_, ...), custom_call_target="tpu_custom_call" | custom-call | flops 2415919104 | bytes 12000000 | tf_op jit(solution)/shard_map/pallas_call | solution.py:440
  148.3 3.4 %shard_map.341 = (bf16[192,1024]{1,0:T(8,128)(2,1)S(1)}, bf16[192,1024]{1,0:T(8,128)(2,1)}, bf16[192,1024]{1,0:T(8,128)(2,1)S(1)}, bf16[192,1024]{1,0:T(8,128)(2,1)S(1)}) custom-call(s32[9]{0:T(128)S(1)} %pad_add_fusion.1.refs_0_, bf16[512,768]{1,0:T(8,128)(2,1)S(1)} %get-tuple-element.55.refs_1_, ...), custom_call_target="tpu_custom_call" | custom-call | flops 805306368 | bytes 4000000 | tf_op jit(solution)/shard_map/pallas_call | solution.py:440
  159.4 6.8 %shard_map.340 = (bf16[256,1536]{1,0:T(8,128)(2,1)S(1)}, bf16[256,1536]{1,0:T(8,128)(2,1)S(1)}, bf16[256,1536]{1,0:T(8,128)(2,1)S(1)}, bf16[256,1536]{1,0:T(8,128)(2,1)S(1)}) custom-call(s32[9]{0:T(128)S(1)} %pad_add_fusion.1.refs_0_, bf16[2,128,1024]{2,1,0:T(8,128)(2,1)S(1)} %pad_maximum_fusion.5.refs_1_, bf16[2,128,1024]{2,1,0:T(8,128)(2,1)S(1)} %copy-done.21, ...), custom_call_target="tpu_custom_call" | custom-call | flops 1610612736 | bytes 6000000 | tf_op jit(solution)/shard_map/pallas_call | solution.py:440
  172.1 18.6 %collective-permute-done.64 = bf16[96,1024]{1,0:T(8,128)(2,1)S(1)} collective-permute-done((bf16[96,1024]{1,0:T(8,128)(2,1)S(1)}, bf16[96,1024]{1,0:T(8,128)(2,1)S(1)}, u32[]{:S(2)}, u32[]{:S(2)}) %collective-permute-start.64) | collective-permute-done | bytes 196640 | tf_op jit(solution)/shard_map/ppermute | solution.py:329
  190.9 3.5 %collective-permute-start.67 = (bf16[192,1024]{1,0:T(8,128)(2,1)S(1)}, bf16[192,1024]{1,0:T(8,128)(2,1)S(1)}, u32[]{:S(2)}, u32[]{:S(2)}) collective-permute-start(bf16[192,1024]{1,0:T(8,128)(2,1)S(1)} %pad_maximum_fusion.18), channel_id=1, source_target_pairs={{1,17},{3,19},{5,21},{7,23},{9,25},{11,27},{13,29},{15,31},{16,0},... | collective-permute-start | bytes 1179656 | tf_op jit(solution)/shard_map/ppermute | solution.py:346
  197.5 4.5 %collective-permute-done.67 = bf16[192,1024]{1,0:T(8,128)(2,1)S(1)} collective-permute-done((bf16[192,1024]{1,0:T(8,128)(2,1)S(1)}, bf16[192,1024]{1,0:T(8,128)(2,1)S(1)}, u32[]{:S(2)}, u32[]{:S(2)}) %collective-permute-start.67) | collective-permute-done | bytes 393248 | tf_op jit(solution)/shard_map/ppermute | solution.py:346
  203.5 4.1 %collective-permute-done.37 = bf16[128,1024]{1,0:T(8,128)(2,1)S(1)} collective-permute-done((bf16[128,1024]{1,0:T(8,128)(2,1)S(1)}, bf16[128,1024]{1,0:T(8,128)(2,1)S(1)}, u32[]{:S(2)}, u32[]{:S(2)}) %collective-permute-start.37) | collective-permute-done | bytes 262176 | tf_op jit(solution)/shard_map/ppermute | solution.py:329
  211.6 7.1 %shard_map.335 = (bf16[512,1024]{1,0:T(8,128)(2,1)S(1)}, f32[8,128]{1,0:T(8,128)S(1)}) custom-call(s32[9]{0:T(128)S(1)} %pad_add_fusion.1.refs_0_, bf16[2,128,1024]{2,1,0:T(8,128)(2,1)S(1)} %pad_maximum_fusion.7.refs_1_.refs_2_, bf16[2,128,1024]{2,1,0:T(8,128)(2,1)S(1)} %collective-permute-done.38.refs_2_.refs_3_, bf16[128,1024]{1,0:T(8,128)(2,1)S(1)} %copy-done.9, ...), custom_call_target="tpu_custom_call" | custom-call | flops 2000000000 | bytes 8000000 | tf_op jit(solution)/shard_map/pallas_call | solution.py:440
  218.7 4.9 %shard_map.336 = (bf16[256,1024]{1,0:T(8,128)(2,1)S(1)}, bf16[256,1024]{1,0:T(8,128)(2,1)S(1)}, bf16[256,1024]{1,0:T(8,128)(2,1)S(1)}, bf16[256,1024]{1,0:T(8,128)(2,1)S(1)}) custom-call(s32[9]{0:T(128)S(1)} %pad_add_fusion.1.refs_0_, bf16[2,128,1024]{2,1,0:T(8,128)(2,1)S(1)} %pad_maximum_fusion.2.refs_1_, bf16[2,128,1024]{2,1,0:T(8,128)(2,1)S(1)} %copy-done.17, ...), custom_call_target="tpu_custom_call" | custom-call | flops 1073741824 | bytes 6000000 | tf_op jit(solution)/shard_map/pallas_call | solution.py:440
  223.6 2.7 shard_map.339
  229.4 3.7 %shard_map.337 = (bf16[2,128,1024]{2,1,0:T(8,128)(2,1)S(1)}, bf16[2,128,1024]{2,1,0:T(8,128)(2,1)S(1)}) custom-call(s32[9]{0:T(128)S(1)} %pad_add_fusion.1.refs_0_, bf16[512,768]{1,0:T(8,128)(2,1)S(1)} %copy-done.33, bf16[192,1024]{1,0:T(8,128)(2,1)S(1)} %pad_maximum_fusion.12.refs_7_.refs_4_.refs_2_, bf16[192,1024]{1,0:T(8,128)(2,1)S(1)} %copy-done.24, ...), custom_call_target="tpu_custom_call" | custom-call | flops 805306368 | bytes 4000000 | tf_op jit(solution)/shard_map/pallas_call | solution.py:440
  233.1 4.9 %shard_map.338 = (bf16[2,128,1024]{2,1,0:T(8,128)(2,1)S(1)}, bf16[2,128,1024]{2,1,0:T(8,128)(2,1)S(1)}) custom-call(s32[9]{0:T(128)S(1)} %pad_add_fusion.1.refs_0_, bf16[512,1024]{1,0:T(8,128)(2,1)S(1)} %get-tuple-element.63.refs_3_.refs_1_, bf16[256,1024]{1,0:T(8,128)(2,1)S(1)} %pad_maximum_fusion.3.refs_3_.refs_2_, bf16[256,1024]{1,0:T(8,128)(2,1)S(1)} %copy-done.19, ...), custom_call_target="tpu_custom_call" | custom-call | flops 1073741824 | bytes 5000000 | tf_op jit(solution)/shard_map/pallas_call | solution.py:440
  238.2 5.2 %collective-permute-done.61 = bf16[64,1536]{1,0:T(8,128)(2,1)S(1)} collective-permute-done((bf16[64,1536]{1,0:T(8,128)(2,1)S(1)}, bf16[64,1536]{1,0:T(8,128)(2,1)S(1)}, u32[]{:S(2)}, u32[]{:S(2)}) %collective-permute-start.61) | collective-permute-done | bytes 196640 | tf_op jit(solution)/shard_map/ppermute | solution.py:329
  246.4 4.0 %collective-permute-done.51 = bf16[64,1024]{1,0:T(8,128)(2,1)S(1)} collective-permute-done((bf16[64,1024]{1,0:T(8,128)(2,1)S(1)}, bf16[64,1024]{1,0:T(8,128)(2,1)S(1)}, u32[]{:S(2)}, u32[]{:S(2)}) %collective-permute-start.51) | collective-permute-done | bytes 131104 | tf_op jit(solution)/shard_map/ppermute | solution.py:329
  250.6 3.6 %collective-permute-done.53 = bf16[64,1024]{1,0:T(8,128)(2,1)S(1)} collective-permute-done((bf16[64,1024]{1,0:T(8,128)(2,1)S(1)}, bf16[64,1024]{1,0:T(8,128)(2,1)S(1)}, u32[]{:S(2)}, u32[]{:S(2)}) %collective-permute-start.53) | collective-permute-done | bytes 131104 | tf_op jit(solution)/shard_map/ppermute | solution.py:329
  256.8 3.3 %collective-permute-start.54 = (bf16[128,1024]{1,0:T(8,128)(2,1)S(1)}, bf16[128,1024]{1,0:T(8,128)(2,1)S(1)}, u32[]{:S(2)}, u32[]{:S(2)}) collective-permute-start(bf16[128,1024]{1,0:T(8,128)(2,1)S(1)} %pad_maximum_fusion.28), channel_id=1, source_target_pairs={{1,17},{3,19},{5,21},{7,23},{9,25},{11,27},{13,29},{15,31},{16,0},... | collective-permute-start | bytes 786440 | tf_op jit(solution)/shard_map/ppermute | solution.py:346
  281.9 10.5 %collective-permute-done.71 = bf16[16,144]{1,0:T(8,128)(2,1)S(1)} collective-permute-done((bf16[16,144]{1,0:T(8,128)(2,1)S(1)}, bf16[16,144]{1,0:T(8,128)(2,1)S(1)}, u32[]{:S(2)}, u32[]{:S(2)}) %collective-permute-start.71) | collective-permute-done | bytes 4640 | tf_op jit(solution)/shard_map/ppermute | solution.py:329
  299.4 3.2 %collective-permute-done.48 = bf16[64,1024]{1,0:T(8,128)(2,1)S(1)} collective-permute-done((bf16[64,1024]{1,0:T(8,128)(2,1)S(1)}, bf16[64,1024]{1,0:T(8,128)(2,1)S(1)}, u32[]{:S(2)}, u32[]{:S(2)}) %collective-permute-start.48) | collective-permute-done | bytes 131104 | tf_op jit(solution)/shard_map/ppermute | solution.py:329
  302.7 3.6 %collective-permute-start.49 = (bf16[2,64,1024]{2,1,0:T(8,128)(2,1)S(1)}, bf16[2,64,1024]{2,1,0:T(8,128)(2,1)S(1)}, u32[]{:S(2)}, u32[]{:S(2)}) collective-permute-start(bf16[2,64,1024]{2,1,0:T(8,128)(2,1)S(1)} %pad_maximum_fusion.26), channel_id=1, source_target_pairs={{0,1},{1,0},{2,3},{3,2},{4,5},{5,4},{6,7},{7,6},{8,9},{9,8},{10,11... | collective-permute-start | bytes 786440 | tf_op jit(solution)/shard_map/ppermute | solution.py:333
  (457 shorter events, 111.4 us)
Async XLA Ops:
  6.2 28.3 %collective-permute-start.7 = (bf16[64,1024]{1,0:T(8,128)(2,1)}, bf16[64,1024]{1,0:T(8,128)(2,1)S(1)}, u32[]{:S(2)}, u32[]{:S(2)}) collective-permute-start(bf16[64,1024]{1,0:T(8,128)(2,1)} %pad_maximum_fusion.30), channel_id=1, source_target_pairs={{0,8},{2,10},{4,12},{6,14},{8,0},{10,2},{12,4},{14,6},{16,24},{18,... | collective-permute-start | bytes 393224 | tf_op jit(solution)/shard_map/ppermute | solution.py:329
  8.8 25.9 %collective-permute-start.13 = (bf16[128,1024]{1,0:T(8,128)(2,1)S(1)}, bf16[128,1024]{1,0:T(8,128)(2,1)S(1)}, u32[]{:S(2)}, u32[]{:S(2)}) collective-permute-start(bf16[128,1024]{1,0:T(8,128)(2,1)S(1)} %convert_element_type.387), channel_id=1, source_target_pairs={{0,16},{2,18},{4,20},{6,22},{8,24},{10,26},{12,28},{14,30},{17,1},... | collective-permute-start | bytes 786440 | tf_op jit(solution)/shard_map/ppermute | solution.py:346
  11.4 23.2 %collective-permute-start.25 = (bf16[64,1536]{1,0:T(8,128)(2,1)S(1)}, bf16[64,1536]{1,0:T(8,128)(2,1)S(1)}, u32[]{:S(2)}, u32[]{:S(2)}) collective-permute-start(bf16[64,1536]{1,0:T(8,128)(2,1)S(1)} %pad_maximum_fusion.29), channel_id=1, source_target_pairs={{0,8},{2,10},{4,12},{6,14},{8,0},{10,2},{12,4},{14,6},{16,24},{18,... | collective-permute-start | bytes 589832 | tf_op jit(solution)/shard_map/ppermute | solution.py:329
  14.0 35.9 %collective-permute-start.18 = (bf16[192,1024]{1,0:T(8,128)(2,1)}, bf16[192,1024]{1,0:T(8,128)(2,1)}, u32[]{:S(2)}, u32[]{:S(2)}) collective-permute-start(bf16[192,1024]{1,0:T(8,128)(2,1)} %convert_element_type.388), channel_id=1, source_target_pairs={{0,16},{2,18},{4,20},{6,22},{8,24},{10,26},{12,28},{14,30},{17,1},... | collective-permute-start | bytes 1179656 | tf_op jit(solution)/shard_map/ppermute | solution.py:346
  34.8 22.4 %collective-permute-start.16 = (bf16[64,1024]{1,0:T(8,128)(2,1)S(1)}, bf16[64,1024]{1,0:T(8,128)(2,1)S(1)}, u32[]{:S(2)}, u32[]{:S(2)}) collective-permute-start(bf16[64,1024]{1,0:T(8,128)(2,1)S(1)} %get-tuple-element.146), channel_id=1, source_target_pairs={{0,2},{2,0},{4,6},{6,4},{8,10},{10,8},{12,14},{14,12},{16,18},{18,... | collective-permute-start | bytes 393224 | tf_op jit(solution)/shard_map/ppermute | solution.py:329
  36.1 22.5 %collective-permute-start.14 = (bf16[64,1024]{1,0:T(8,128)(2,1)S(1)}, bf16[64,1024]{1,0:T(8,128)(2,1)S(1)}, u32[]{:S(2)}, u32[]{:S(2)}) collective-permute-start(bf16[64,1024]{1,0:T(8,128)(2,1)S(1)} %get-tuple-element.147), channel_id=1, source_target_pairs={{0,4},{2,6},{4,0},{6,2},{8,12},{10,14},{12,8},{14,10},{16,20},{18,... | collective-permute-start | bytes 393224 | tf_op jit(solution)/shard_map/ppermute | solution.py:329
  41.0 29.9 %collective-permute-start.6 = (bf16[2,128,1024]{2,1,0:T(8,128)(2,1)S(1)}, bf16[2,128,1024]{2,1,0:T(8,128)(2,1)S(1)}, u32[]{:S(2)}, u32[]{:S(2)}) collective-permute-start(bf16[2,128,1024]{2,1,0:T(8,128)(2,1)S(1)} %pad_maximum_fusion.2.refs_1_), channel_id=1, source_target_pairs={{0,1},{1,0},{2,3},{3,2},{4,5},{5,4},{6,7},{7,6},{8,9},{9,8},{10,11... | collective-permute-start | bytes 1572872 | tf_op jit(solution)/shard_map/ppermute | solution.py:333
  58.6 32.6 %collective-permute-start.26 = (bf16[128,1536]{1,0:T(8,128)(2,1)S(1)}, bf16[128,1536]{1,0:T(8,128)(2,1)S(1)}, u32[]{:S(2)}, u32[]{:S(2)}) collective-permute-start(bf16[128,1536]{1,0:T(8,128)(2,1)S(1)} %pad_maximum_fusion.8), channel_id=1, source_target_pairs={{0,16},{2,18},{4,20},{6,22},{8,24},{10,26},{12,28},{14,30},{16,0},... | collective-permute-start | bytes 1179656 | tf_op jit(solution)/shard_map/ppermute | solution.py:329
  71.4 41.8 %collective-permute-start.33 = (bf16[128,1024]{1,0:T(8,128)(2,1)S(1)}, bf16[128,1024]{1,0:T(8,128)(2,1)S(1)}, u32[]{:S(2)}, u32[]{:S(2)}) collective-permute-start(bf16[128,1024]{1,0:T(8,128)(2,1)S(1)} %bitcast.128), channel_id=1, source_target_pairs={{0,8},{2,10},{4,12},{6,14},{8,0},{10,2},{12,4},{14,6},{16,24},{18,... | collective-permute-start | bytes 786440 | tf_op jit(solution)/shard_map/ppermute | solution.py:329
  80.3 33.1 %collective-permute-start.31 = (bf16[192,1024]{1,0:T(8,128)(2,1)S(1)}, bf16[192,1024]{1,0:T(8,128)(2,1)S(1)}, u32[]{:S(2)}, u32[]{:S(2)}) collective-permute-start(bf16[192,1024]{1,0:T(8,128)(2,1)S(1)} %pad_maximum_fusion.12.refs_7_.refs_4_.refs_2_), channel_id=1, source_target_pairs={{0,2},{2,0},{4,6},{6,4},{8,10},{10,8},{12,14},{14,12},{16,18},{18,... | collective-permute-start | bytes 1179656 | tf_op jit(solution)/shard_map/ppermute | solution.py:329
  102.2 28.3 %collective-permute-start.30 = (bf16[256,1536]{1,0:T(8,128)(2,1)S(1)}, bf16[256,1536]{1,0:T(8,128)(2,1)S(1)}, u32[]{:S(2)}, u32[]{:S(2)}) collective-permute-start(bf16[256,1536]{1,0:T(8,128)(2,1)S(1)} %pad_maximum_fusion.1.refs_5_.refs_10_), channel_id=1, source_target_pairs={{0,4},{2,6},{4,0},{6,2},{8,12},{10,14},{12,8},{14,10},{16,20},{18,... | collective-permute-start | bytes 2359304 | tf_op jit(solution)/shard_map/ppermute | solution.py:329
  105.6 24.9 %collective-permute-start.28 = (bf16[256,1536]{1,0:T(8,128)(2,1)S(1)}, bf16[256,1536]{1,0:T(8,128)(2,1)S(1)}, u32[]{:S(2)}, u32[]{:S(2)}) collective-permute-start(bf16[256,1536]{1,0:T(8,128)(2,1)S(1)} %pad_maximum_fusion.refs_3_.refs_8_), channel_id=1, source_target_pairs={{0,2},{2,0},{4,6},{6,4},{8,10},{10,8},{12,14},{14,12},{16,18},{18,... | collective-permute-start | bytes 2359304 | tf_op jit(solution)/shard_map/ppermute | solution.py:329
  111.1 19.4 %collective-permute-start.24 = (bf16[2,128,1024]{2,1,0:T(8,128)(2,1)S(1)}, bf16[2,128,1024]{2,1,0:T(8,128)(2,1)S(1)}, u32[]{:S(2)}, u32[]{:S(2)}) collective-permute-start(bf16[2,128,1024]{2,1,0:T(8,128)(2,1)S(1)} %pad_maximum_fusion.5.refs_1_), channel_id=1, source_target_pairs={{0,1},{1,0},{2,3},{3,2},{4,5},{5,4},{6,7},{7,6},{8,9},{9,8},{10,11... | collective-permute-start | bytes 1572872 | tf_op jit(solution)/shard_map/ppermute | solution.py:333
  113.2 17.3 %collective-permute-start.32 = (bf16[192,1024]{1,0:T(8,128)(2,1)S(1)}, bf16[192,1024]{1,0:T(8,128)(2,1)S(1)}, u32[]{:S(2)}, u32[]{:S(2)}) collective-permute-start(bf16[192,1024]{1,0:T(8,128)(2,1)S(1)} %pad_maximum_fusion.13.refs_9_.refs_6_.refs_4_), channel_id=1, source_target_pairs={{0,4},{2,6},{4,0},{6,2},{8,12},{10,14},{12,8},{14,10},{16,20},{18,... | collective-permute-start | bytes 1179656 | tf_op jit(solution)/shard_map/ppermute | solution.py:329
  113.4 24.1 %collective-permute-start.34 = (bf16[2,128,1024]{2,1,0:T(8,128)(2,1)S(1)}, bf16[2,128,1024]{2,1,0:T(8,128)(2,1)S(1)}, u32[]{:S(2)}, u32[]{:S(2)}) collective-permute-start(bf16[2,128,1024]{2,1,0:T(8,128)(2,1)S(1)} %pad_maximum_fusion.6.refs_1_.refs_2_), channel_id=1, source_target_pairs={{0,1},{1,0},{2,3},{3,2},{4,5},{5,4},{6,7},{7,6},{8,9},{9,8},{10,11... | collective-permute-start | bytes 1572872 | tf_op jit(solution)/shard_map/ppermute | solution.py:333
  154.0 16.4 %collective-permute-start.65 = (bf16[192,1024]{1,0:T(8,128)(2,1)}, bf16[192,1024]{1,0:T(8,128)(2,1)S(1)}, u32[]{:S(2)}, u32[]{:S(2)}) collective-permute-start(bf16[192,1024]{1,0:T(8,128)(2,1)} %copy-done.27), channel_id=1, source_target_pairs={{0,4},{2,6},{4,0},{6,2},{8,12},{10,14},{12,8},{14,10},{16,20},{18,... | collective-permute-start | bytes 1179656 | tf_op jit(solution)/shard_map/ppermute | solution.py:329
  155.1 15.6 %collective-permute-start.35 = (bf16[2,128,1024]{2,1,0:T(8,128)(2,1)}, bf16[2,128,1024]{2,1,0:T(8,128)(2,1)S(1)}, u32[]{:S(2)}, u32[]{:S(2)}) collective-permute-start(bf16[2,128,1024]{2,1,0:T(8,128)(2,1)} %copy-done.22), channel_id=1, source_target_pairs={{0,1},{1,0},{2,3},{3,2},{4,5},{5,4},{6,7},{7,6},{8,9},{9,8},{10,11... | collective-permute-start | bytes 1572872 | tf_op jit(solution)/shard_map/ppermute | solution.py:333
  166.3 30.2 %collective-permute-start.56 = (bf16[256,1536]{1,0:T(8,128)(2,1)S(1)}, bf16[256,1536]{1,0:T(8,128)(2,1)S(1)}, u32[]{:S(2)}, u32[]{:S(2)}) collective-permute-start(bf16[256,1536]{1,0:T(8,128)(2,1)S(1)} %get-tuple-element.78), channel_id=1, source_target_pairs={{0,2},{2,0},{4,6},{6,4},{8,10},{10,8},{12,14},{14,12},{16,18},{18,... | collective-permute-start | bytes 2359304 | tf_op jit(solution)/shard_map/ppermute | solution.py:329
  167.7 29.3 %collective-permute-start.58 = (bf16[256,1536]{1,0:T(8,128)(2,1)S(1)}, bf16[256,1536]{1,0:T(8,128)(2,1)S(1)}, u32[]{:S(2)}, u32[]{:S(2)}) collective-permute-start(bf16[256,1536]{1,0:T(8,128)(2,1)S(1)} %get-tuple-element.80), channel_id=1, source_target_pairs={{0,4},{2,6},{4,0},{6,2},{8,12},{10,14},{12,8},{14,10},{16,20},{18,... | collective-permute-start | bytes 2359304 | tf_op jit(solution)/shard_map/ppermute | solution.py:329
  169.0 21.7 %collective-permute-start.64 = (bf16[96,1024]{1,0:T(8,128)(2,1)S(1)}, bf16[96,1024]{1,0:T(8,128)(2,1)S(1)}, u32[]{:S(2)}, u32[]{:S(2)}) collective-permute-start(bf16[96,1024]{1,0:T(8,128)(2,1)S(1)} %slice.399), channel_id=1, source_target_pairs={{0,4},{2,6},{4,0},{6,2},{8,12},{10,14},{12,8},{14,10},{16,20},{18,... | collective-permute-start | bytes 589832 | tf_op jit(solution)/shard_map/ppermute | solution.py:329
  170.5 20.3 %collective-permute-start.66 = (bf16[96,1024]{1,0:T(8,128)(2,1)S(1)}, bf16[96,1024]{1,0:T(8,128)(2,1)S(1)}, u32[]{:S(2)}, u32[]{:S(2)}) collective-permute-start(bf16[96,1024]{1,0:T(8,128)(2,1)S(1)} %slice.401), channel_id=1, source_target_pairs={{0,2},{2,0},{4,6},{6,4},{8,10},{10,8},{12,14},{14,12},{16,18},{18,... | collective-permute-start | bytes 589832 | tf_op jit(solution)/shard_map/ppermute | solution.py:329
  171.0 23.4 %collective-permute-start.36 = (bf16[128,1024]{1,0:T(8,128)(2,1)S(1)}, bf16[128,1024]{1,0:T(8,128)(2,1)S(1)}, u32[]{:S(2)}, u32[]{:S(2)}) collective-permute-start(bf16[128,1024]{1,0:T(8,128)(2,1)S(1)} %fusion.37), channel_id=1, source_target_pairs={{0,8},{2,10},{4,12},{6,14},{8,0},{10,2},{12,4},{14,6},{16,24},{18,... | collective-permute-start | bytes 786440 | tf_op jit(solution)/shard_map/ppermute | solution.py:329
  208.9 29.1 %collective-permute-start.60 = (bf16[128,1536]{1,0:T(8,128)(2,1)S(1)}, bf16[128,1536]{1,0:T(8,128)(2,1)S(1)}, u32[]{:S(2)}, u32[]{:S(2)}) collective-permute-start(bf16[128,1536]{1,0:T(8,128)(2,1)S(1)} %pad_maximum_fusion.14), channel_id=1, source_target_pairs={{0,16},{2,18},{4,20},{6,22},{8,24},{10,26},{12,28},{14,30},{16,0},... | collective-permute-start | bytes 1179656 | tf_op jit(solution)/shard_map/ppermute | solution.py:329
  226.4 19.2 %collective-permute-start.50 = (bf16[128,1024]{1,0:T(8,128)(2,1)S(1)}, bf16[128,1024]{1,0:T(8,128)(2,1)S(1)}, u32[]{:S(2)}, u32[]{:S(2)}) collective-permute-start(bf16[128,1024]{1,0:T(8,128)(2,1)S(1)} %get-tuple-element.73), channel_id=1, source_target_pairs={{0,2},{2,0},{4,6},{6,4},{8,10},{10,8},{12,14},{14,12},{16,18},{18,... | collective-permute-start | bytes 786440 | tf_op jit(solution)/shard_map/ppermute | solution.py:329
  226.6 19.2 %collective-permute-start.52 = (bf16[128,1024]{1,0:T(8,128)(2,1)S(1)}, bf16[128,1024]{1,0:T(8,128)(2,1)S(1)}, u32[]{:S(2)}, u32[]{:S(2)}) collective-permute-start(bf16[128,1024]{1,0:T(8,128)(2,1)S(1)} %get-tuple-element.75), channel_id=1, source_target_pairs={{0,4},{2,6},{4,0},{6,2},{8,12},{10,14},{12,8},{14,10},{16,20},{18,... | collective-permute-start | bytes 786440 | tf_op jit(solution)/shard_map/ppermute | solution.py:329
  227.6 29.2 %collective-permute-start.43 = (bf16[256,1024]{1,0:T(8,128)(2,1)S(1)}, bf16[256,1024]{1,0:T(8,128)(2,1)S(1)}, u32[]{:S(2)}, u32[]{:S(2)}) collective-permute-start(bf16[256,1024]{1,0:T(8,128)(2,1)S(1)} %get-tuple-element.69), channel_id=1, source_target_pairs={{0,2},{2,0},{4,6},{6,4},{8,10},{10,8},{12,14},{14,12},{16,18},{18,... | collective-permute-start | bytes 1572872 | tf_op jit(solution)/shard_map/ppermute | solution.py:329
  228.1 32.9 %collective-permute-start.45 = (bf16[256,1024]{1,0:T(8,128)(2,1)S(1)}, bf16[256,1024]{1,0:T(8,128)(2,1)S(1)}, u32[]{:S(2)}, u32[]{:S(2)}) collective-permute-start(bf16[256,1024]{1,0:T(8,128)(2,1)S(1)} %get-tuple-element.71), channel_id=1, source_target_pairs={{0,4},{2,6},{4,0},{6,2},{8,12},{10,14},{12,8},{14,10},{16,20},{18,... | collective-permute-start | bytes 1572872 | tf_op jit(solution)/shard_map/ppermute | solution.py:329
  243.4 19.4 %collective-permute-start.41 = (bf16[2,128,1024]{2,1,0:T(8,128)(2,1)S(1)}, bf16[2,128,1024]{2,1,0:T(8,128)(2,1)S(1)}, u32[]{:S(2)}, u32[]{:S(2)}) collective-permute-start(bf16[2,128,1024]{2,1,0:T(8,128)(2,1)S(1)} %get-tuple-element.68), channel_id=1, source_target_pairs={{0,1},{1,0},{2,3},{3,2},{4,5},{5,4},{6,7},{7,6},{8,9},{9,8},{10,11... | collective-permute-start | bytes 1572872 | tf_op jit(solution)/shard_map/ppermute | solution.py:333
  245.6 18.1 %collective-permute-start.39 = (bf16[2,128,1024]{2,1,0:T(8,128)(2,1)S(1)}, bf16[2,128,1024]{2,1,0:T(8,128)(2,1)S(1)}, u32[]{:S(2)}, u32[]{:S(2)}) collective-permute-start(bf16[2,128,1024]{2,1,0:T(8,128)(2,1)S(1)} %get-tuple-element.66), channel_id=1, source_target_pairs={{0,1},{1,0},{2,3},{3,2},{4,5},{5,4},{6,7},{7,6},{8,9},{9,8},{10,11... | collective-permute-start | bytes 1572872 | tf_op jit(solution)/shard_map/ppermute | solution.py:333
  264.9 32.0 %collective-permute-start.40 = (bf16[128,1024]{1,0:T(8,128)(2,1)}, bf16[128,1024]{1,0:T(8,128)(2,1)}, u32[]{:S(2)}, u32[]{:S(2)}) collective-permute-start(bf16[128,1024]{1,0:T(8,128)(2,1)} %fusion.39), channel_id=1, source_target_pairs={{0,8},{2,10},{4,12},{6,14},{8,0},{10,2},{12,4},{14,6},{16,24},{18,... | collective-permute-start | bytes 786440 | tf_op jit(solution)/shard_map/ppermute | solution.py:329
  271.5 34.7 %collective-permute-start.55 = (bf16[128,1024]{1,0:T(8,128)(2,1)}, bf16[128,1024]{1,0:T(8,128)(2,1)}, u32[]{:S(2)}, u32[]{:S(2)}) collective-permute-start(bf16[128,1024]{1,0:T(8,128)(2,1)} %add_convert_fusion.10), channel_id=1, source_target_pairs={{0,1},{2,3},{4,5},{6,7},{8,9},{10,11},{12,13},{14,15},{17,16},{19,... | collective-permute-start | bytes 786440 | tf_op jit(solution)/shard_map/ppermute | solution.py:397
  277.9 20.8 %collective-permute-start.47 = (bf16[128,1024]{1,0:T(8,128)(2,1)S(1)}, bf16[128,1024]{1,0:T(8,128)(2,1)S(1)}, u32[]{:S(2)}, u32[]{:S(2)}) collective-permute-start(bf16[128,1024]{1,0:T(8,128)(2,1)S(1)} %pad_maximum_fusion.25), channel_id=1, source_target_pairs={{0,16},{2,18},{4,20},{6,22},{8,24},{10,26},{12,28},{14,30},{16,0},... | collective-permute-start | bytes 786440 | tf_op jit(solution)/shard_map/ppermute | solution.py:329
  (127 other events, 1147.2 us)
